TPU v7x, 256 devices: a whole 4x4x8 slice. The times are simulated.
256 devices in a mesh: region: 2 (over core), column: 4 (over x), layer: 32 (over z, y).
Axes of the slice: x: 4, y: 4, z: 8, core: 2. Of those that a mesh axis runs over, the one named last changes fastest.
Arguments:
- rhs: float32 [3, 256, 32, 512], P(None, 'layer', 'region', 'column'), may hold values from -0.8 to 0.8
- guess: float32 [3, 256, 32, 512], P(None, 'layer', 'region', 'column'), may hold values from -0.8 to 0.8
- diag_block: float32 [9, 256, 32, 512], P(None, 'layer', 'region', 'column'), may hold values from -4 to 4
- couple: float32 [3, 256, 32, 512], P(None, 'layer', 'region', 'column'), may hold values from 0.05 to 0.2
- pivot_inv: float32 [9, 256, 32, 512], P(None, 'layer', 'region', 'column')
- lower: float32 [9, 256, 32, 512], P(None, 'layer', 'region', 'column')
- upper: float32 [9, 256, 32, 512], P(None, 'layer', 'region', 'column')
- well_couple: float32 [9, 256, 32, 512], P(None, 'layer', 'region', 'column'), may hold values from -2 to 2
- well_inv: float32 [9, 16], replicated, may hold values from -0.0234375 to 0.0234375
- comp_tiles: int32 [32], replicated, may hold values from 0 to 127, as said below
- counts: int32 [16], replicated, may hold values from 0 to 16, as said below
Outputs:
- preconditioned: float32 [3, 256, 32, 512], P(None, 'layer', 'region', 'column')
Inputs may be any that keep to these rules, and one draw needn't show every extreme that they name: `comp_tiles`: well w is owned by the device with index w % 8 over region and column. Each device over region and column has exactly 4 perforated tiles, on distinct rows; they go in groups of exactly 2 to 2 distinct owners; no tile is listed twice; lists are sorted by well and within a well by tile id. The counts sum to 32; a well has at most 2 tiles of any one device.
All inputs are finite; a program needn't handle non-finite values.
Results may differ from a plain program's by a relative error of at most 0.00016.
Values sent between devices are 32-bit elements; how exact they have to be, the bound alone decides.
No kernel may reach another device: no remote copies, remote signals or barrier semaphores. Data moves between devices by JAX's collectives and lax.ppermute only.
A program may use at most 64 MiB of HBM per device.

v0:
```python
import jax
import jax.numpy as jnp
from jax import lax
from jax.sharding import PartitionSpec as P

CAP = 2


HIGH = lax.Precision.HIGHEST


def extended(block, sides, width):
    for axis, dim in sides:
        count = lax.axis_size(axis)
        forward = [(i, i + 1) for i in range(count - 1)]
        backward = [(target, source) for source, target in forward]
        low = lax.ppermute(
            lax.slice_in_dim(block, block.shape[dim] - width, None, axis=dim), axis, forward
        )
        high = lax.ppermute(lax.slice_in_dim(block, 0, width, axis=dim), axis, backward)
        block = jnp.concatenate([low, block, high], axis=dim)
    return block


def shifted(shard, axis, by):
    peers = lax.axis_size(axis)
    pairs = [(i, i + by) for i in range(peers) if 0 <= i + by < peers]
    return lax.ppermute(shard, axis, pairs)


def block_mix(blk, vec):
    return jnp.stack(
        [blk[3 * i] * vec[0] + blk[3 * i + 1] * vec[1] + blk[3 * i + 2] * vec[2] for i in range(3)]
    )


def block_mix_t(blk, vec):
    return jnp.stack(
        [blk[j] * vec[0] + blk[3 + j] * vec[1] + blk[6 + j] * vec[2] for j in range(3)]
    )


def compose(first, second):
    return jnp.stack(
        [
            first[3 * i] * second[j]
            + first[3 * i + 1] * second[3 + j]
            + first[3 * i + 2] * second[6 + j]
            for i in range(3)
            for j in range(3)
        ]
    )


def identity_blocks(shape):
    ones = jnp.ones(shape, jnp.float32)
    zeros = jnp.zeros(shape, jnp.float32)
    return jnp.stack([ones if entry % 4 == 0 else zeros for entry in range(9)])


def well_rates(well_inv, totals):
    return jnp.stack(
        [
            well_inv[3 * i] * totals[:, 0]
            + well_inv[3 * i + 1] * totals[:, 1]
            + well_inv[3 * i + 2] * totals[:, 2]
            for i in range(3)
        ]
    )


def local(
    rhs,
    guess,
    diag_block,
    couple,
    pivot_inv,
    lower,
    upper,
    well_couple,
    well_inv,
    comp_tiles,
    counts,
):
    depth = rhs.shape[1]
    rows = rhs.shape[2]
    span = rhs.shape[3]
    padded = extended(guess, (("region", 2), ("column", 3), ("layer", 1)), 1)
    beside = padded[:, 2:, 1:-1, 1:-1] + padded[:, :-2, 1:-1, 1:-1]
    beside = beside + padded[:, 1:-1, 2:, 1:-1] + padded[:, 1:-1, :-2, 1:-1]
    beside = beside + padded[:, 1:-1, 1:-1, 2:] + padded[:, 1:-1, 1:-1, :-2]
    resid = rhs - (block_mix(diag_block, guess) - couple * beside)
    empty_state = jnp.zeros((3, rows, span), jnp.float32)
    identity = identity_blocks((rows, span))

    def sweep_down(entry):
        result = []
        state = entry
        for k in range(depth):
            state = block_mix(pivot_inv[:, k], resid[:, k] - block_mix(lower[:, k], state))
            result.append(state)
        return result

    trial_down = sweep_down(empty_state)
    down_map = identity
    for k in range(depth):
        down_map = compose(-compose(pivot_inv[:, k], lower[:, k]), down_map)

    def pass_down(step, carry):
        return shifted(block_mix(down_map, carry) + trial_down[-1], "layer", 1)

    entry_down = lax.fori_loop(0, lax.axis_size("layer") - 1, pass_down, empty_state)
    forward = sweep_down(entry_down)

    def sweep_up(entry):
        result = [empty_state] * depth
        state = entry
        for k in reversed(range(depth)):
            state = forward[k] - block_mix(pivot_inv[:, k], block_mix(upper[:, k], state))
            result[k] = state
        return result

    trial_up = sweep_up(empty_state)
    up_map = identity
    for k in reversed(range(depth)):
        up_map = compose(-compose(pivot_inv[:, k], upper[:, k]), up_map)

    def pass_up(step, carry):
        return shifted(block_mix(up_map, carry) + trial_up[0], "layer", -1)

    entry_up = lax.fori_loop(0, lax.axis_size("layer") - 1, pass_up, empty_state)
    solved = jnp.stack(sweep_up(entry_up), axis=1)
    myself = lax.axis_index(("region", "column"))
    areas = lax.axis_size(("region", "column"))
    nperf = comp_tiles.shape[0]
    nwell = counts.shape[0]
    ends = jnp.cumsum(counts)
    place = jnp.arange(nperf, dtype=jnp.int32)
    well_of = jnp.sum((place[:, None] >= ends[None, :]).astype(jnp.int32), axis=1)
    well_hot = well_of[:, None] == jnp.arange(nwell, dtype=jnp.int32)[None, :]
    owner_of = well_of % areas
    sender = comp_tiles // rows
    row_of = comp_tiles % rows
    before = (
        (sender[:, None] == sender[None, :])
        & (owner_of[:, None] == owner_of[None, :])
        & (row_of[None, :] < row_of[:, None])
    )
    slot_of = jnp.sum(before.astype(jnp.int32), axis=1)
    mine = (sender == myself).astype(jnp.float32)
    owned = (owner_of == myself).astype(jnp.float32)
    peer_hot = (owner_of[:, None] == jnp.arange(areas, dtype=jnp.int32)[None, :]).astype(
        jnp.float32
    )
    sender_hot = (sender[:, None] == jnp.arange(areas, dtype=jnp.int32)[None, :]).astype(
        jnp.float32
    )
    slot_hot = (slot_of[:, None] == jnp.arange(CAP, dtype=jnp.int32)[None, :]).astype(jnp.float32)
    row_hot = (row_of[:, None] == jnp.arange(rows, dtype=jnp.int32)[None, :]).astype(jnp.float32)
    well_float = well_hot.astype(jnp.float32)
    row_sums = jnp.sum(block_mix(well_couple, solved), axis=(1, 3))
    pick = jnp.einsum("po,pk,pr->okr", peer_hot * mine[:, None], slot_hot, row_hot, precision=HIGH)
    inbox = jnp.einsum(
        "ps,pk,pw->skw", sender_hot * owned[:, None], slot_hot, well_float, precision=HIGH
    )
    slot_out = jnp.einsum("okr,ir->iok", pick, row_sums, precision=HIGH)
    slot_sums = lax.all_to_all(
        slot_out, ("region", "column"), split_axis=1, concat_axis=1, tiled=True
    )
    partial_sums = jnp.einsum("skw,isk->wi", inbox, slot_sums, precision=HIGH)
    totals = lax.psum(partial_sums, "layer")
    slot_rate = jnp.einsum("skw,iw->isk", inbox, well_rates(well_inv, totals), precision=HIGH)
    answers = lax.all_to_all(
        slot_rate, ("region", "column"), split_axis=1, concat_axis=1, tiled=True
    )
    row_rate = jnp.einsum("okr,iok->ir", pick, answers, precision=HIGH)
    delta = block_mix_t(well_couple, row_rate[:, None, :, None])
    return solved - delta


def solution(mesh):
    return jax.shard_map(
        local,
        mesh=mesh,
        in_specs=(
            P(None, "layer", "region", "column"),
            P(None, "layer", "region", "column"),
            P(None, "layer", "region", "column"),
            P(None, "layer", "region", "column"),
            P(None, "layer", "region", "column"),
            P(None, "layer", "region", "column"),
            P(None, "layer", "region", "column"),
            P(None, "layer", "region", "column"),
            P(),
            P(),
            P(),
        ),
        out_specs=P(None, "layer", "region", "column"),
        check_vma=False,
    )
```

profile of v0, /device:TPU:129, one launch (start us, length us, event | category | flops | bytes accessed | tf_op | source)
XLA Modules:
  0.0 778.1 jit_solution(4318197425017904540)
XLA Ops:
  62.5 6.2 collective-permute-done.7
  90.6 246.9 %while.20 = (s32[]{:T(128)}, f32[3,16,128]{2,1,0:T(8,128)S(1)}, f32[16,128]{1,0:T(8,128)S(1)}, f32[16,128]{1,0:T(8,128)S(1)}, f32[16,128]{1,0:T(8,128)S(1)}, /*i...) while((s32[]{:T(128)}, f32[3,16,128]{2,1,0:T(8,128)S(1)}, ...), condition=%wide.region_1.0_spmd, body=%wide.region_0.0_spmd.sunk | while | flops 49154 | bytes 295077 | solution.py:112
  100.5 6.0 collective-permute-done
  124.3 6.0 collective-permute-done
  140.1 6.3 collective-permute-done
  156.3 6.0 collective-permute-done
  180.0 6.0 collective-permute-done
  195.9 6.0 collective-permute-done
  203.8 6.4 collective-permute-done
  212.2 6.0 collective-permute-done
  228.0 6.0 collective-permute-done
  251.8 6.0 collective-permute-done
  267.6 6.3 collective-permute-done
  275.9 6.0 collective-permute-done
  331.3 6.2 collective-permute-done
  357.9 240.6 %while.21 = (s32[]{:T(128)}, f32[3,16,128]{2,1,0:T(8,128)S(1)}, f32[16,128]{1,0:T(8,128)S(1)}, f32[16,128]{1,0:T(8,128)S(1)}, f32[16,128]{1,0:T(8,128)S(1)}, /*i...) while((s32[]{:T(128)}, f32[3,16,128]{2,1,0:T(8,128)S(1)}, ...), condition=%wide.region_3.0_spmd, body=%wide.region_2.0_spmd.sunk | while | flops 49154 | bytes 295077 | solution.py:131
  368.8 7.0 collective-permute-start.1
  376.7 7.0 collective-permute-start.1
  384.6 7.0 collective-permute-start.1
  392.5 7.0 collective-permute-start.1
  400.5 7.0 collective-permute-start.1
  408.4 7.0 collective-permute-start.1
  416.3 7.0 collective-permute-start.1
  424.2 7.0 collective-permute-start.1
  432.1 7.0 collective-permute-start.1
  440.0 7.0 collective-permute-start.1
  448.0 7.0 collective-permute-start.1
  455.9 7.0 collective-permute-start.1
  463.8 7.0 collective-permute-start.1
  471.7 7.0 collective-permute-start.1
  479.6 7.0 collective-permute-start.1
  487.6 7.0 collective-permute-start.1
  495.5 7.0 collective-permute-start.1
  503.4 7.0 collective-permute-start.1
  511.3 7.0 collective-permute-start.1
  519.2 7.0 collective-permute-start.1
  527.2 7.0 collective-permute-start.1
  535.1 7.0 collective-permute-start.1
  543.0 7.1 collective-permute-start.1
  551.1 7.0 collective-permute-start.1
  559.0 7.0 collective-permute-start.1
  566.9 7.0 collective-permute-start.1
  574.8 7.0 collective-permute-start.1
  582.8 7.0 collective-permute-start.1
  590.7 7.0 collective-permute-start.1
  611.7 77.1 %all-to-all-start = ((f32[3,8,2]{0,2,1:T(2,128)}), f32[3,8,2]{0,2,1:T(2,128)S(1)}, u32[]{:S(2)}, u32[]{:S(2)}) async-start(f32[3,8,2]{0,2,1:T(2,128)} %copy.96), calls=%async_computation | async-start | bytes 16384 | tf_op jit(solution)/shard_map/all_to_all | solution.py:167
  693.9 61.5 %psum.7 = f32[16,3]{0,1:T(4,128)S(1)} all-reduce(f32[16,3]{0,1:T(4,128)S(1)} %convolution_bitcast_fusion.3), channel_id=1, replica_groups=mesh['region'=2,'column'=4,'layer'=32] {'layer'}, use_global_device_ids=true, to_apply=%region_8.9 | all-reduce | flops 48 | bytes 384 | tf_op jit(solution)/shard_map/psum | solution.py:171
  755.7 21.4 %all_to_all.10 = f32[3,8,2]{0,2,1:T(2,128)S(1)} all-to-all(f32[3,8,2]{0,2,1:T(2,128)S(1)} %copy.98), channel_id=1, replica_groups=mesh['region'=2,'column'=4,'layer'=32] {'region','column'}, dimensions={1} | all-to-all | bytes 384 | tf_op jit(solution)/shard_map/all_to_all | solution.py:173
  (605 shorter events, 328.3 us)
Async XLA Ops:
  1.6 41.1 %collective-permute-start.2 = (f32[3,8,1,128]{3,2,0,1:T(1,128)}, f32[3,8,1,128]{3,2,0,1:T(1,128)S(1)}, u32[]{:S(2)}, u32[]{:S(2)}) collective-permute-start(f32[3,8,1,128]{3,2,0,1:T(1,128)} %get-tuple-element.625), channel_id=1, source_target_pairs={{0,128},{1,129},{2,130},{3,131},{4,132},{5,133},{6,134},{7,135},{8... | collective-permute-start | bytes 36872 | tf_op jit(solution)/shard_map/ppermute | solution.py:17
  3.1 39.7 %collective-permute-start.3 = (f32[3,8,1,128]{3,2,0,1:T(1,128)}, f32[3,8,1,128]{3,2,0,1:T(1,128)S(1)}, u32[]{:S(2)}, u32[]{:S(2)}) collective-permute-start(f32[3,8,1,128]{3,2,0,1:T(1,128)} %get-tuple-element.626), channel_id=1, source_target_pairs={{128,0},{129,1},{130,2},{131,3},{132,4},{133,5},{134,6},{135,7},{1... | collective-permute-start | bytes 36872 | tf_op jit(solution)/shard_map/ppermute | solution.py:20
  43.0 10.6 %collective-permute-start.5 = (f32[3,8,18,1]{3,2,0,1:T(8,128)S(1)}, f32[3,8,18,1]{3,2,0,1:T(8,128)S(1)}, u32[]{:S(2)}, u32[]{:S(2)}) collective-permute-start(f32[3,8,18,1]{3,2,0,1:T(8,128)S(1)} %get-tuple-element.623), channel_id=1, source_target_pairs={{32,0},{64,32},{96,64},{33,1},{65,33},{97,65},{34,2},{66,34},{98,6... | collective-permute-start | bytes 5192 | tf_op jit(solution)/shard_map/ppermute | solution.py:20
  44.3 10.7 %collective-permute-start.4 = (f32[3,8,18,1]{3,2,0,1:T(8,128)S(1)}, f32[3,8,18,1]{3,2,0,1:T(8,128)S(1)}, u32[]{:S(2)}, u32[]{:S(2)}) collective-permute-start(f32[3,8,18,1]{3,2,0,1:T(8,128)S(1)} %get-tuple-element.624), channel_id=1, source_target_pairs={{0,32},{32,64},{64,96},{1,33},{33,65},{65,97},{2,34},{34,66},{66,9... | collective-permute-start | bytes 5192 | tf_op jit(solution)/shard_map/ppermute | solution.py:17
  59.9 8.7 %collective-permute-start.7 = (f32[3,1,18,130]{3,2,0,1:T(8,128)}, f32[3,1,18,130]{3,2,0,1:T(8,128)}, u32[]{:S(2)}, u32[]{:S(2)}) collective-permute-start(f32[3,1,18,130]{3,2,0,1:T(8,128)} %get-tuple-element.535), channel_id=1, source_target_pairs={{0,1},{1,2},{2,3},{3,4},{4,5},{5,6},{6,7},{7,8},{8,9},{9,10},{10,1... | collective-permute-start | bytes 84248 | tf_op jit(solution)/shard_map/ppermute | solution.py:17
  98.6 7.9 %collective-permute-start = (f32[3,16,128]{2,1,0:T(8,128)S(1)}, f32[3,16,128]{2,1,0:T(8,128)S(1)}, u32[]{:S(2)}, u32[]{:S(2)}) collective-permute-start(f32[3,16,128]{2,1,0:T(8,128)S(1)} %maximum_add_fusion.4), channel_id=1, source_target_pairs={{0,1},{1,2},{2,3},{3,4},{4,5},{5,6},{6,7},{7,8},{8,9},{9,10},{10,1... | collective-permute-start | bytes 73736 | tf_op jit(solution)/shard_map/while/body/eval_jaxpr/ppermute | solution.py:28
  106.5 7.9 %collective-permute-start = (f32[3,16,128]{2,1,0:T(8,128)S(1)}, f32[3,16,128]{2,1,0:T(8,128)S(1)}, u32[]{:S(2)}, u32[]{:S(2)}) collective-permute-start(f32[3,16,128]{2,1,0:T(8,128)S(1)} %maximum_add_fusion.4), channel_id=1, source_target_pairs={{0,1},{1,2},{2,3},{3,4},{4,5},{5,6},{6,7},{7,8},{8,9},{9,10},{10,1... | collective-permute-start | bytes 73736 | tf_op jit(solution)/shard_map/while/body/eval_jaxpr/ppermute | solution.py:28
  122.4 7.9 %collective-permute-start = (f32[3,16,128]{2,1,0:T(8,128)S(1)}, f32[3,16,128]{2,1,0:T(8,128)S(1)}, u32[]{:S(2)}, u32[]{:S(2)}) collective-permute-start(f32[3,16,128]{2,1,0:T(8,128)S(1)} %maximum_add_fusion.4), channel_id=1, source_target_pairs={{0,1},{1,2},{2,3},{3,4},{4,5},{5,6},{6,7},{7,8},{8,9},{9,10},{10,1... | collective-permute-start | bytes 73736 | tf_op jit(solution)/shard_map/while/body/eval_jaxpr/ppermute | solution.py:28
  130.3 7.9 %collective-permute-start = (f32[3,16,128]{2,1,0:T(8,128)S(1)}, f32[3,16,128]{2,1,0:T(8,128)S(1)}, u32[]{:S(2)}, u32[]{:S(2)}) collective-permute-start(f32[3,16,128]{2,1,0:T(8,128)S(1)} %maximum_add_fusion.4), channel_id=1, source_target_pairs={{0,1},{1,2},{2,3},{3,4},{4,5},{5,6},{6,7},{7,8},{8,9},{9,10},{10,1... | collective-permute-start | bytes 73736 | tf_op jit(solution)/shard_map/while/body/eval_jaxpr/ppermute | solution.py:28
  138.2 8.2 %collective-permute-start = (f32[3,16,128]{2,1,0:T(8,128)S(1)}, f32[3,16,128]{2,1,0:T(8,128)S(1)}, u32[]{:S(2)}, u32[]{:S(2)}) collective-permute-start(f32[3,16,128]{2,1,0:T(8,128)S(1)} %maximum_add_fusion.4), channel_id=1, source_target_pairs={{0,1},{1,2},{2,3},{3,4},{4,5},{5,6},{6,7},{7,8},{8,9},{9,10},{10,1... | collective-permute-start | bytes 73736 | tf_op jit(solution)/shard_map/while/body/eval_jaxpr/ppermute | solution.py:28
  154.3 7.9 %collective-permute-start = (f32[3,16,128]{2,1,0:T(8,128)S(1)}, f32[3,16,128]{2,1,0:T(8,128)S(1)}, u32[]{:S(2)}, u32[]{:S(2)}) collective-permute-start(f32[3,16,128]{2,1,0:T(8,128)S(1)} %maximum_add_fusion.4), channel_id=1, source_target_pairs={{0,1},{1,2},{2,3},{3,4},{4,5},{5,6},{6,7},{7,8},{8,9},{9,10},{10,1... | collective-permute-start | bytes 73736 | tf_op jit(solution)/shard_map/while/body/eval_jaxpr/ppermute | solution.py:28
  162.3 7.9 %collective-permute-start = (f32[3,16,128]{2,1,0:T(8,128)S(1)}, f32[3,16,128]{2,1,0:T(8,128)S(1)}, u32[]{:S(2)}, u32[]{:S(2)}) collective-permute-start(f32[3,16,128]{2,1,0:T(8,128)S(1)} %maximum_add_fusion.4), channel_id=1, source_target_pairs={{0,1},{1,2},{2,3},{3,4},{4,5},{5,6},{6,7},{7,8},{8,9},{9,10},{10,1... | collective-permute-start | bytes 73736 | tf_op jit(solution)/shard_map/while/body/eval_jaxpr/ppermute | solution.py:28
  178.1 7.9 %collective-permute-start = (f32[3,16,128]{2,1,0:T(8,128)S(1)}, f32[3,16,128]{2,1,0:T(8,128)S(1)}, u32[]{:S(2)}, u32[]{:S(2)}) collective-permute-start(f32[3,16,128]{2,1,0:T(8,128)S(1)} %maximum_add_fusion.4), channel_id=1, source_target_pairs={{0,1},{1,2},{2,3},{3,4},{4,5},{5,6},{6,7},{7,8},{8,9},{9,10},{10,1... | collective-permute-start | bytes 73736 | tf_op jit(solution)/shard_map/while/body/eval_jaxpr/ppermute | solution.py:28
  193.9 7.9 %collective-permute-start = (f32[3,16,128]{2,1,0:T(8,128)S(1)}, f32[3,16,128]{2,1,0:T(8,128)S(1)}, u32[]{:S(2)}, u32[]{:S(2)}) collective-permute-start(f32[3,16,128]{2,1,0:T(8,128)S(1)} %maximum_add_fusion.4), channel_id=1, source_target_pairs={{0,1},{1,2},{2,3},{3,4},{4,5},{5,6},{6,7},{7,8},{8,9},{9,10},{10,1... | collective-permute-start | bytes 73736 | tf_op jit(solution)/shard_map/while/body/eval_jaxpr/ppermute | solution.py:28
  201.9 8.4 %collective-permute-start = (f32[3,16,128]{2,1,0:T(8,128)S(1)}, f32[3,16,128]{2,1,0:T(8,128)S(1)}, u32[]{:S(2)}, u32[]{:S(2)}) collective-permute-start(f32[3,16,128]{2,1,0:T(8,128)S(1)} %maximum_add_fusion.4), channel_id=1, source_target_pairs={{0,1},{1,2},{2,3},{3,4},{4,5},{5,6},{6,7},{7,8},{8,9},{9,10},{10,1... | collective-permute-start | bytes 73736 | tf_op jit(solution)/shard_map/while/body/eval_jaxpr/ppermute | solution.py:28
  210.2 7.9 %collective-permute-start = (f32[3,16,128]{2,1,0:T(8,128)S(1)}, f32[3,16,128]{2,1,0:T(8,128)S(1)}, u32[]{:S(2)}, u32[]{:S(2)}) collective-permute-start(f32[3,16,128]{2,1,0:T(8,128)S(1)} %maximum_add_fusion.4), channel_id=1, source_target_pairs={{0,1},{1,2},{2,3},{3,4},{4,5},{5,6},{6,7},{7,8},{8,9},{9,10},{10,1... | collective-permute-start | bytes 73736 | tf_op jit(solution)/shard_map/while/body/eval_jaxpr/ppermute | solution.py:28
  265.7 8.3 %collective-permute-start = (f32[3,16,128]{2,1,0:T(8,128)S(1)}, f32[3,16,128]{2,1,0:T(8,128)S(1)}, u32[]{:S(2)}, u32[]{:S(2)}) collective-permute-start(f32[3,16,128]{2,1,0:T(8,128)S(1)} %maximum_add_fusion.4), channel_id=1, source_target_pairs={{0,1},{1,2},{2,3},{3,4},{4,5},{5,6},{6,7},{7,8},{8,9},{9,10},{10,1... | collective-permute-start | bytes 73736 | tf_op jit(solution)/shard_map/while/body/eval_jaxpr/ppermute | solution.py:28
  329.4 8.1 %collective-permute-start = (f32[3,16,128]{2,1,0:T(8,128)S(1)}, f32[3,16,128]{2,1,0:T(8,128)S(1)}, u32[]{:S(2)}, u32[]{:S(2)}) collective-permute-start(f32[3,16,128]{2,1,0:T(8,128)S(1)} %maximum_add_fusion.4), channel_id=1, source_target_pairs={{0,1},{1,2},{2,3},{3,4},{4,5},{5,6},{6,7},{7,8},{8,9},{9,10},{10,1... | collective-permute-start | bytes 73736 | tf_op jit(solution)/shard_map/while/body/eval_jaxpr/ppermute | solution.py:28
  368.8 7.9 %collective-permute-start.1 = (f32[3,16,128]{2,1,0:T(8,128)S(1)}, f32[3,16,128]{2,1,0:T(8,128)S(1)}, u32[]{:S(2)}, u32[]{:S(2)}) collective-permute-start(f32[3,16,128]{2,1,0:T(8,128)S(1)} %maximum_add_fusion.5), channel_id=1, source_target_pairs={{1,0},{2,1},{3,2},{4,3},{5,4},{6,5},{7,6},{8,7},{9,8},{10,9},{11,1... | collective-permute-start | bytes 73736 | tf_op jit(solution)/shard_map/while/body/eval_jaxpr/ppermute | solution.py:28
  376.7 7.9 %collective-permute-start.1 = (f32[3,16,128]{2,1,0:T(8,128)S(1)}, f32[3,16,128]{2,1,0:T(8,128)S(1)}, u32[]{:S(2)}, u32[]{:S(2)}) collective-permute-start(f32[3,16,128]{2,1,0:T(8,128)S(1)} %maximum_add_fusion.5), channel_id=1, source_target_pairs={{1,0},{2,1},{3,2},{4,3},{5,4},{6,5},{7,6},{8,7},{9,8},{10,9},{11,1... | collective-permute-start | bytes 73736 | tf_op jit(solution)/shard_map/while/body/eval_jaxpr/ppermute | solution.py:28
  384.6 7.9 %collective-permute-start.1 = (f32[3,16,128]{2,1,0:T(8,128)S(1)}, f32[3,16,128]{2,1,0:T(8,128)S(1)}, u32[]{:S(2)}, u32[]{:S(2)}) collective-permute-start(f32[3,16,128]{2,1,0:T(8,128)S(1)} %maximum_add_fusion.5), channel_id=1, source_target_pairs={{1,0},{2,1},{3,2},{4,3},{5,4},{6,5},{7,6},{8,7},{9,8},{10,9},{11,1... | collective-permute-start | bytes 73736 | tf_op jit(solution)/shard_map/while/body/eval_jaxpr/ppermute | solution.py:28
  392.5 7.9 %collective-permute-start.1 = (f32[3,16,128]{2,1,0:T(8,128)S(1)}, f32[3,16,128]{2,1,0:T(8,128)S(1)}, u32[]{:S(2)}, u32[]{:S(2)}) collective-permute-start(f32[3,16,128]{2,1,0:T(8,128)S(1)} %maximum_add_fusion.5), channel_id=1, source_target_pairs={{1,0},{2,1},{3,2},{4,3},{5,4},{6,5},{7,6},{8,7},{9,8},{10,9},{11,1... | collective-permute-start | bytes 73736 | tf_op jit(solution)/shard_map/while/body/eval_jaxpr/ppermute | solution.py:28
  400.5 7.9 %collective-permute-start.1 = (f32[3,16,128]{2,1,0:T(8,128)S(1)}, f32[3,16,128]{2,1,0:T(8,128)S(1)}, u32[]{:S(2)}, u32[]{:S(2)}) collective-permute-start(f32[3,16,128]{2,1,0:T(8,128)S(1)} %maximum_add_fusion.5), channel_id=1, source_target_pairs={{1,0},{2,1},{3,2},{4,3},{5,4},{6,5},{7,6},{8,7},{9,8},{10,9},{11,1... | collective-permute-start | bytes 73736 | tf_op jit(solution)/shard_map/while/body/eval_jaxpr/ppermute | solution.py:28
  408.4 7.9 %collective-permute-start.1 = (f32[3,16,128]{2,1,0:T(8,128)S(1)}, f32[3,16,128]{2,1,0:T(8,128)S(1)}, u32[]{:S(2)}, u32[]{:S(2)}) collective-permute-start(f32[3,16,128]{2,1,0:T(8,128)S(1)} %maximum_add_fusion.5), channel_id=1, source_target_pairs={{1,0},{2,1},{3,2},{4,3},{5,4},{6,5},{7,6},{8,7},{9,8},{10,9},{11,1... | collective-permute-start | bytes 73736 | tf_op jit(solution)/shard_map/while/body/eval_jaxpr/ppermute | solution.py:28
  416.3 7.9 %collective-permute-start.1 = (f32[3,16,128]{2,1,0:T(8,128)S(1)}, f32[3,16,128]{2,1,0:T(8,128)S(1)}, u32[]{:S(2)}, u32[]{:S(2)}) collective-permute-start(f32[3,16,128]{2,1,0:T(8,128)S(1)} %maximum_add_fusion.5), channel_id=1, source_target_pairs={{1,0},{2,1},{3,2},{4,3},{5,4},{6,5},{7,6},{8,7},{9,8},{10,9},{11,1... | collective-permute-start | bytes 73736 | tf_op jit(solution)/shard_map/while/body/eval_jaxpr/ppermute | solution.py:28
  424.2 7.9 %collective-permute-start.1 = (f32[3,16,128]{2,1,0:T(8,128)S(1)}, f32[3,16,128]{2,1,0:T(8,128)S(1)}, u32[]{:S(2)}, u32[]{:S(2)}) collective-permute-start(f32[3,16,128]{2,1,0:T(8,128)S(1)} %maximum_add_fusion.5), channel_id=1, source_target_pairs={{1,0},{2,1},{3,2},{4,3},{5,4},{6,5},{7,6},{8,7},{9,8},{10,9},{11,1... | collective-permute-start | bytes 73736 | tf_op jit(solution)/shard_map/while/body/eval_jaxpr/ppermute | solution.py:28
  432.1 7.9 %collective-permute-start.1 = (f32[3,16,128]{2,1,0:T(8,128)S(1)}, f32[3,16,128]{2,1,0:T(8,128)S(1)}, u32[]{:S(2)}, u32[]{:S(2)}) collective-permute-start(f32[3,16,128]{2,1,0:T(8,128)S(1)} %maximum_add_fusion.5), channel_id=1, source_target_pairs={{1,0},{2,1},{3,2},{4,3},{5,4},{6,5},{7,6},{8,7},{9,8},{10,9},{11,1... | collective-permute-start | bytes 73736 | tf_op jit(solution)/shard_map/while/body/eval_jaxpr/ppermute | solution.py:28
  440.0 7.9 %collective-permute-start.1 = (f32[3,16,128]{2,1,0:T(8,128)S(1)}, f32[3,16,128]{2,1,0:T(8,128)S(1)}, u32[]{:S(2)}, u32[]{:S(2)}) collective-permute-start(f32[3,16,128]{2,1,0:T(8,128)S(1)} %maximum_add_fusion.5), channel_id=1, source_target_pairs={{1,0},{2,1},{3,2},{4,3},{5,4},{6,5},{7,6},{8,7},{9,8},{10,9},{11,1... | collective-permute-start | bytes 73736 | tf_op jit(solution)/shard_map/while/body/eval_jaxpr/ppermute | solution.py:28
  448.0 7.9 %collective-permute-start.1 = (f32[3,16,128]{2,1,0:T(8,128)S(1)}, f32[3,16,128]{2,1,0:T(8,128)S(1)}, u32[]{:S(2)}, u32[]{:S(2)}) collective-permute-start(f32[3,16,128]{2,1,0:T(8,128)S(1)} %maximum_add_fusion.5), channel_id=1, source_target_pairs={{1,0},{2,1},{3,2},{4,3},{5,4},{6,5},{7,6},{8,7},{9,8},{10,9},{11,1... | collective-permute-start | bytes 73736 | tf_op jit(solution)/shard_map/while/body/eval_jaxpr/ppermute | solution.py:28
  455.9 7.9 %collective-permute-start.1 = (f32[3,16,128]{2,1,0:T(8,128)S(1)}, f32[3,16,128]{2,1,0:T(8,128)S(1)}, u32[]{:S(2)}, u32[]{:S(2)}) collective-permute-start(f32[3,16,128]{2,1,0:T(8,128)S(1)} %maximum_add_fusion.5), channel_id=1, source_target_pairs={{1,0},{2,1},{3,2},{4,3},{5,4},{6,5},{7,6},{8,7},{9,8},{10,9},{11,1... | collective-permute-start | bytes 73736 | tf_op jit(solution)/shard_map/while/body/eval_jaxpr/ppermute | solution.py:28
  463.8 7.9 %collective-permute-start.1 = (f32[3,16,128]{2,1,0:T(8,128)S(1)}, f32[3,16,128]{2,1,0:T(8,128)S(1)}, u32[]{:S(2)}, u32[]{:S(2)}) collective-permute-start(f32[3,16,128]{2,1,0:T(8,128)S(1)} %maximum_add_fusion.5), channel_id=1, source_target_pairs={{1,0},{2,1},{3,2},{4,3},{5,4},{6,5},{7,6},{8,7},{9,8},{10,9},{11,1... | collective-permute-start | bytes 73736 | tf_op jit(solution)/shard_map/while/body/eval_jaxpr/ppermute | solution.py:28
  471.7 7.9 %collective-permute-start.1 = (f32[3,16,128]{2,1,0:T(8,128)S(1)}, f32[3,16,128]{2,1,0:T(8,128)S(1)}, u32[]{:S(2)}, u32[]{:S(2)}) collective-permute-start(f32[3,16,128]{2,1,0:T(8,128)S(1)} %maximum_add_fusion.5), channel_id=1, source_target_pairs={{1,0},{2,1},{3,2},{4,3},{5,4},{6,5},{7,6},{8,7},{9,8},{10,9},{11,1... | collective-permute-start | bytes 73736 | tf_op jit(solution)/shard_map/while/body/eval_jaxpr/ppermute | solution.py:28
  479.6 7.9 %collective-permute-start.1 = (f32[3,16,128]{2,1,0:T(8,128)S(1)}, f32[3,16,128]{2,1,0:T(8,128)S(1)}, u32[]{:S(2)}, u32[]{:S(2)}) collective-permute-start(f32[3,16,128]{2,1,0:T(8,128)S(1)} %maximum_add_fusion.5), channel_id=1, source_target_pairs={{1,0},{2,1},{3,2},{4,3},{5,4},{6,5},{7,6},{8,7},{9,8},{10,9},{11,1... | collective-permute-start | bytes 73736 | tf_op jit(solution)/shard_map/while/body/eval_jaxpr/ppermute | solution.py:28
  487.6 7.9 %collective-permute-start.1 = (f32[3,16,128]{2,1,0:T(8,128)S(1)}, f32[3,16,128]{2,1,0:T(8,128)S(1)}, u32[]{:S(2)}, u32[]{:S(2)}) collective-permute-start(f32[3,16,128]{2,1,0:T(8,128)S(1)} %maximum_add_fusion.5), channel_id=1, source_target_pairs={{1,0},{2,1},{3,2},{4,3},{5,4},{6,5},{7,6},{8,7},{9,8},{10,9},{11,1... | collective-permute-start | bytes 73736 | tf_op jit(solution)/shard_map/while/body/eval_jaxpr/ppermute | solution.py:28
  495.5 7.9 %collective-permute-start.1 = (f32[3,16,128]{2,1,0:T(8,128)S(1)}, f32[3,16,128]{2,1,0:T(8,128)S(1)}, u32[]{:S(2)}, u32[]{:S(2)}) collective-permute-start(f32[3,16,128]{2,1,0:T(8,128)S(1)} %maximum_add_fusion.5), channel_id=1, source_target_pairs={{1,0},{2,1},{3,2},{4,3},{5,4},{6,5},{7,6},{8,7},{9,8},{10,9},{11,1... | collective-permute-start | bytes 73736 | tf_op jit(solution)/shard_map/while/body/eval_jaxpr/ppermute | solution.py:28
  503.4 7.9 %collective-permute-start.1 = (f32[3,16,128]{2,1,0:T(8,128)S(1)}, f32[3,16,128]{2,1,0:T(8,128)S(1)}, u32[]{:S(2)}, u32[]{:S(2)}) collective-permute-start(f32[3,16,128]{2,1,0:T(8,128)S(1)} %maximum_add_fusion.5), channel_id=1, source_target_pairs={{1,0},{2,1},{3,2},{4,3},{5,4},{6,5},{7,6},{8,7},{9,8},{10,9},{11,1... | collective-permute-start | bytes 73736 | tf_op jit(solution)/shard_map/while/body/eval_jaxpr/ppermute | solution.py:28
  511.3 7.9 %collective-permute-start.1 = (f32[3,16,128]{2,1,0:T(8,128)S(1)}, f32[3,16,128]{2,1,0:T(8,128)S(1)}, u32[]{:S(2)}, u32[]{:S(2)}) collective-permute-start(f32[3,16,128]{2,1,0:T(8,128)S(1)} %maximum_add_fusion.5), channel_id=1, source_target_pairs={{1,0},{2,1},{3,2},{4,3},{5,4},{6,5},{7,6},{8,7},{9,8},{10,9},{11,1... | collective-permute-start | bytes 73736 | tf_op jit(solution)/shard_map/while/body/eval_jaxpr/ppermute | solution.py:28
  519.2 7.9 %collective-permute-start.1 = (f32[3,16,128]{2,1,0:T(8,128)S(1)}, f32[3,16,128]{2,1,0:T(8,128)S(1)}, u32[]{:S(2)}, u32[]{:S(2)}) collective-permute-start(f32[3,16,128]{2,1,0:T(8,128)S(1)} %maximum_add_fusion.5), channel_id=1, source_target_pairs={{1,0},{2,1},{3,2},{4,3},{5,4},{6,5},{7,6},{8,7},{9,8},{10,9},{11,1... | collective-permute-start | bytes 73736 | tf_op jit(solution)/shard_map/while/body/eval_jaxpr/ppermute | solution.py:28
  527.2 7.9 %collective-permute-start.1 = (f32[3,16,128]{2,1,0:T(8,128)S(1)}, f32[3,16,128]{2,1,0:T(8,128)S(1)}, u32[]{:S(2)}, u32[]{:S(2)}) collective-permute-start(f32[3,16,128]{2,1,0:T(8,128)S(1)} %maximum_add_fusion.5), channel_id=1, source_target_pairs={{1,0},{2,1},{3,2},{4,3},{5,4},{6,5},{7,6},{8,7},{9,8},{10,9},{11,1... | collective-permute-start | bytes 73736 | tf_op jit(solution)/shard_map/while/body/eval_jaxpr/ppermute | solution.py:28
  535.1 7.9 %collective-permute-start.1 = (f32[3,16,128]{2,1,0:T(8,128)S(1)}, f32[3,16,128]{2,1,0:T(8,128)S(1)}, u32[]{:S(2)}, u32[]{:S(2)}) collective-permute-start(f32[3,16,128]{2,1,0:T(8,128)S(1)} %maximum_add_fusion.5), channel_id=1, source_target_pairs={{1,0},{2,1},{3,2},{4,3},{5,4},{6,5},{7,6},{8,7},{9,8},{10,9},{11,1... | collective-permute-start | bytes 73736 | tf_op jit(solution)/shard_map/while/body/eval_jaxpr/ppermute | solution.py:28
  543.0 8.1 %collective-permute-start.1 = (f32[3,16,128]{2,1,0:T(8,128)S(1)}, f32[3,16,128]{2,1,0:T(8,128)S(1)}, u32[]{:S(2)}, u32[]{:S(2)}) collective-permute-start(f32[3,16,128]{2,1,0:T(8,128)S(1)} %maximum_add_fusion.5), channel_id=1, source_target_pairs={{1,0},{2,1},{3,2},{4,3},{5,4},{6,5},{7,6},{8,7},{9,8},{10,9},{11,1... | collective-permute-start | bytes 73736 | tf_op jit(solution)/shard_map/while/body/eval_jaxpr/ppermute | solution.py:28
  551.1 7.9 %collective-permute-start.1 = (f32[3,16,128]{2,1,0:T(8,128)S(1)}, f32[3,16,128]{2,1,0:T(8,128)S(1)}, u32[]{:S(2)}, u32[]{:S(2)}) collective-permute-start(f32[3,16,128]{2,1,0:T(8,128)S(1)} %maximum_add_fusion.5), channel_id=1, source_target_pairs={{1,0},{2,1},{3,2},{4,3},{5,4},{6,5},{7,6},{8,7},{9,8},{10,9},{11,1... | collective-permute-start | bytes 73736 | tf_op jit(solution)/shard_map/while/body/eval_jaxpr/ppermute | solution.py:28
  559.0 7.9 %collective-permute-start.1 = (f32[3,16,128]{2,1,0:T(8,128)S(1)}, f32[3,16,128]{2,1,0:T(8,128)S(1)}, u32[]{:S(2)}, u32[]{:S(2)}) collective-permute-start(f32[3,16,128]{2,1,0:T(8,128)S(1)} %maximum_add_fusion.5), channel_id=1, source_target_pairs={{1,0},{2,1},{3,2},{4,3},{5,4},{6,5},{7,6},{8,7},{9,8},{10,9},{11,1... | collective-permute-start | bytes 73736 | tf_op jit(solution)/shard_map/while/body/eval_jaxpr/ppermute | solution.py:28
  566.9 7.9 %collective-permute-start.1 = (f32[3,16,128]{2,1,0:T(8,128)S(1)}, f32[3,16,128]{2,1,0:T(8,128)S(1)}, u32[]{:S(2)}, u32[]{:S(2)}) collective-permute-start(f32[3,16,128]{2,1,0:T(8,128)S(1)} %maximum_add_fusion.5), channel_id=1, source_target_pairs={{1,0},{2,1},{3,2},{4,3},{5,4},{6,5},{7,6},{8,7},{9,8},{10,9},{11,1... | collective-permute-start | bytes 73736 | tf_op jit(solution)/shard_map/while/body/eval_jaxpr/ppermute | solution.py:28
  574.8 7.9 %collective-permute-start.1 = (f32[3,16,128]{2,1,0:T(8,128)S(1)}, f32[3,16,128]{2,1,0:T(8,128)S(1)}, u32[]{:S(2)}, u32[]{:S(2)}) collective-permute-start(f32[3,16,128]{2,1,0:T(8,128)S(1)} %maximum_add_fusion.5), channel_id=1, source_target_pairs={{1,0},{2,1},{3,2},{4,3},{5,4},{6,5},{7,6},{8,7},{9,8},{10,9},{11,1... | collective-permute-start | bytes 73736 | tf_op jit(solution)/shard_map/while/body/eval_jaxpr/ppermute | solution.py:28
  582.8 7.9 %collective-permute-start.1 = (f32[3,16,128]{2,1,0:T(8,128)S(1)}, f32[3,16,128]{2,1,0:T(8,128)S(1)}, u32[]{:S(2)}, u32[]{:S(2)}) collective-permute-start(f32[3,16,128]{2,1,0:T(8,128)S(1)} %maximum_add_fusion.5), channel_id=1, source_target_pairs={{1,0},{2,1},{3,2},{4,3},{5,4},{6,5},{7,6},{8,7},{9,8},{10,9},{11,1... | collective-permute-start | bytes 73736 | tf_op jit(solution)/shard_map/while/body/eval_jaxpr/ppermute | solution.py:28
  590.7 7.9 %collective-permute-start.1 = (f32[3,16,128]{2,1,0:T(8,128)S(1)}, f32[3,16,128]{2,1,0:T(8,128)S(1)}, u32[]{:S(2)}, u32[]{:S(2)}) collective-permute-start(f32[3,16,128]{2,1,0:T(8,128)S(1)} %maximum_add_fusion.5), channel_id=1, source_target_pairs={{1,0},{2,1},{3,2},{4,3},{5,4},{6,5},{7,6},{8,7},{9,8},{10,9},{11,1... | collective-permute-start | bytes 73736 | tf_op jit(solution)/shard_map/while/body/eval_jaxpr/ppermute | solution.py:28
  611.7 82.0 %all-to-all-start = ((f32[3,8,2]{0,2,1:T(2,128)}), f32[3,8,2]{0,2,1:T(2,128)S(1)}, u32[]{:S(2)}, u32[]{:S(2)}) async-start(f32[3,8,2]{0,2,1:T(2,128)} %copy.96), calls=%async_computation | async-start | bytes 16384 | tf_op jit(solution)/shard_map/all_to_all | solution.py:167
  (84 other events, 579.2 us)
where the time goes:
time: 786 us; the launch traced here: 778 us
  starting transfers between devices  362 us (46%)
  waiting for transfers between devices  234 us (30%)
  blocking collectives  82.9 us (11%)
  other arithmetic  75.6 us (10%)
  local copies, waits for them, and re-layouts  20.4 us (3%)
    ppermute x62, starting transfers between devices, shifted(): return lax.ppermute(shard, axis, pairs)  269 us
    ppermute x62, waiting for transfers between devices, shifted(): return lax.ppermute(shard, axis, pairs)  216 us
    all_to_all x1, starting transfers between devices, local(): lax.all_to_all(slot_out, ('region', 'column'), split_axis=1, concat_axis=...  77.1 us
    psum x1, blocking collectives, local(): totals = lax.psum(partial_sums, 'layer')  61.5 us
    add x125, other arithmetic, block_mix(): blk[3 * i] * vec[0] + blk[3 * i + 1] * vec[1] + blk[3 * i + 2] * vec[2]  35.5 us
    all_to_all x1, blocking collectives, local(): lax.all_to_all(slot_rate, ('region', 'column'), split_axis=1, concat_axis...  21.4 us
    unnamed x126, local copies, waits for them, and re-layouts  17.6 us
  transfers between devices with their start and end apart: 69, of which 66 were waited for; matrix products, arithmetic and copies ran while one was open for 3% of the time, Pallas kernels for 0%

commit v1 on v0

v1 whole, which is shorter than its diff:
```python
import jax
import jax.numpy as jnp
from jax import lax
from jax.experimental import pallas as pl
from jax.experimental.pallas import tpu as pltpu
from jax.sharding import PartitionSpec as P

AREA = ("region", "column")
DEPTH, ROWS, LANES = 8, 16, 128
HALF = LANES // 2
PACK = 48
BACK = 8

LEFT = {"lower": 0, "state": 9, "pivot": 18, "well": 27, "source": 36, "couple": 39, "guess": 42}
RIGHT = {"upper": 0, "cross": 9, "state": 18, "well": 27, "source": 36, "couple": 39, "guess": 42}


def mat(a, b):
    return [
        a[3 * i] * b[m] + a[3 * i + 1] * b[3 + m] + a[3 * i + 2] * b[6 + m]
        for i in range(3)
        for m in range(3)
    ]


def vec(a, x):
    return [a[3 * i] * x[0] + a[3 * i + 1] * x[1] + a[3 * i + 2] * x[2] for i in range(3)]


def neg(a):
    return [-entry for entry in a]


def add(a, b):
    return [x + y for x, y in zip(a, b)]


def sub(a, b):
    return [x - y for x, y in zip(a, b)]


def iota(shape, axis):
    return lax.broadcasted_iota(jnp.int32, shape, axis)


def edges_kernel(guess, x_out, right_out, left_out):
    region = lax.axis_index("region")
    lane = iota((ROWS, LANES), 1)
    right = jnp.zeros((ROWS, LANES), jnp.float32)
    left = jnp.zeros((ROWS, LANES), jnp.float32)
    for c in range(3):
        for k in range(DEPTH):
            place = c * DEPTH + k
            block = guess[c, k]
            right = jnp.where(lane == place, pltpu.roll(block, (place + 1) % LANES, 1), right)
            left = jnp.where(lane == place, pltpu.roll(block, place, 1) if place else block, left)
            x_out[place : place + 1, :] = jnp.where(
                region == 0, guess[c, k, ROWS - 1 :, :], guess[c, k, :1, :]
            )
    right_out[...] = right
    left_out[...] = left


def maps_kernel(
    x_in, right_in, left_in, rhs, guess, diag, couple, pivot, lower, upper, well,
    send, cross_out, state_out, trial_out, well_out, forward, states,
):
    region = lax.axis_index("region")
    column = lax.axis_index("column")
    n_column = lax.axis_size("column")
    lane = iota((8, LANES), 1)
    row = iota((8, LANES), 0)
    is_left = lane < HALF
    well_sums = jnp.zeros((8, LANES), jnp.float32)
    for h in range(2):
        at = slice(8 * h, 8 * h + 8)

        def load(ref, k, count):
            return [ref[c, k, at, :] for c in range(count)]

        edge_right = jnp.where(column > 0, right_in[at, :], 0.0)
        edge_left = jnp.where(column < n_column - 1, left_in[at, :], 0.0)

        def residual(k):
            mid = load(guess, k, 3)
            out = vec(load(diag, k, 9), mid)
            for c in range(3):
                g = mid[c]
                place = c * DEPTH + k
                x_row = x_in[place : place + 1, :]
                if h == 0:
                    outer = jnp.where(region > 0, x_row, 0.0)
                    below = jnp.where(row == 0, outer, pltpu.roll(g, 1, 0))
                    above = guess[c, k, 1:9, :]
                else:
                    outer = jnp.where(region == 0, x_row, 0.0)
                    below = guess[c, k, 7:15, :]
                    above = jnp.where(row == 7, outer, pltpu.roll(g, 7, 0))
                first = pltpu.roll(edge_right, LANES - place, 1) if place else edge_right
                before = jnp.where(lane == 0, first, pltpu.roll(g, 1, 1))
                last = pltpu.roll(edge_left, LANES - 1 - place, 1)
                after = jnp.where(lane == LANES - 1, last, pltpu.roll(g, LANES - 1, 1))
                beside = below + above + before + after
                if k > 0:
                    beside = beside + guess[c, k - 1, at, :]
                if k < DEPTH - 1:
                    beside = beside + guess[c, k + 1, at, :]
                out[c] = rhs[c, k, at, :] - (out[c] - couple[c, k, at, :] * beside)
            return out

        f = None
        big_f = None
        for k in range(DEPTH):
            res = residual(k)
            pinv = load(pivot, k, 9)
            if k == 0:
                f = vec(pinv, res)
                big_f = pinv
            else:
                low = load(lower, k, 9)
                f = vec(pinv, sub(res, vec(low, f)))
                big_f = neg(mat(pinv, mat(low, big_f)))
            for c in range(3):
                forward[c, k] = f[c]
            for c in range(9):
                states[c, k] = big_f[c]

        def put(place, left, right):
            low_cols = jnp.where(is_left, left, pltpu.roll(right, HALF, 1))
            high_cols = jnp.where(is_left, pltpu.roll(left, HALF, 1), right)
            send[pl.ds(16 * h * PACK + place, 8, 2 * PACK), :] = low_cols
            send[pl.ds((16 * h + 1) * PACK + place, 8, 2 * PACK), :] = high_cols

        top = DEPTH - 1
        s, cross, state = f, big_f, load(pivot, top, 9)
        coef = load(well, top, 9)
        well_state, well_cross, well_const = mat(coef, state), mat(coef, cross), vec(coef, s)
        for k in reversed(range(DEPTH)):
            if k < top:
                both = mat(load(pivot, k, 9), load(upper, k, 9))
                s = sub([forward[c, k] for c in range(3)], vec(both, s))
                cross = sub([states[c, k] for c in range(9)], mat(both, cross))
                state = neg(mat(both, state))
                coef = load(well, k, 9)
                well_state = add(well_state, mat(coef, state))
                well_cross = add(well_cross, mat(coef, cross))
                well_const = add(well_const, vec(coef, s))
            for c in range(3):
                trial_out[c, k, at, :] = s[c]
            for c in range(9):
                cross_out[c, k, at, :] = cross[c]
                state_out[c, k, at, :] = state[c]

        for e in range(9):
            put(e, lower[e, 0, at, :], upper[e, top, at, :])
            put(9 + e, states[e, top], cross[e])
            put(18 + e, pivot[e, top, at, :], state[e])
            put(27 + e, well_cross[e], well_state[e])
        for c in range(3):
            put(36 + c, forward[c, top], s[c])
            put(39 + c, couple[c, 0, at, :], couple[c, top, at, :])
            put(42 + c, guess[c, top, at, :], guess[c, 0, at, :])
            total = jnp.sum(well_const[c], axis=1, keepdims=True)
            well_sums = well_sums + jnp.where(lane == c * ROWS + 8 * h + row, total, 0.0)
        for place in range(45, PACK):
            put(place, jnp.zeros((8, LANES), jnp.float32), jnp.zeros((8, LANES), jnp.float32))
    well_out[...] = jnp.broadcast_to(jnp.sum(well_sums, axis=0, keepdims=True), (8, LANES))


def chain_kernel(peers, got, well_sums, send, step_ref, base_ref, inflow_ref):
    layer = lax.axis_index("layer")
    lane = iota((peers, LANES), 1)
    row = iota((peers, LANES), 0)
    is_left = lane < HALF

    def take(place, count):
        return [got[pl.ds(place + e, peers, PACK), :] for e in range(count)]

    def swap(a):
        return [pltpu.roll(entry, HALF, 1) for entry in a]

    def chain(step, base, order):
        for e in range(9):
            step_ref[e] = step[e]
        for c in range(3):
            base_ref[c] = base[c]
        x = [jnp.zeros((1, LANES), jnp.float32)] * 3
        for d in order:
            at = slice(d, d + 1)
            for c in range(3):
                inflow_ref[c, at, :] = x[c]
            x = sub([base_ref[c, at, :] for c in range(3)], vec([step_ref[e, at, :] for e in range(9)], x))
        return [inflow_ref[c] for c in range(3)]

    edge = take(0, 9)
    states = take(9, 9)
    pivots = take(18, 9)
    source = take(36, 3)
    couple = take(39, 3)
    guess = take(42, 3)
    from_below = [jnp.where(row == 0, 0.0, pltpu.roll(g, 1, 0)) for g in guess]
    from_above = [jnp.where(row == peers - 1, 0.0, pltpu.roll(g, peers - 1, 0)) for g in guess]
    near = [c * jnp.where(is_left, b, a) for c, b, a in zip(couple, from_below, from_above)]
    above = swap(near)
    base = add(add(source, vec(pivots, above)), vec(states, near))
    step = mat(states, edge)
    f_in = chain(step, base, range(peers))
    u = sub(near, vec(edge, f_in))
    up_base = add(add(source, vec(states, swap(u))), vec(pivots, near))
    s_in = chain(mat(pivots, edge), up_base, reversed(range(peers)))
    w = sub(near, vec(edge, s_in))
    both = [jnp.where(is_left, a, b) for a, b in zip(u, w)]
    parts = vec(take(27, 9), both)
    mine = well_sums[0:1, :]
    one = iota((1, LANES), 1)
    for c in range(3):
        total = jnp.sum(jnp.sum(parts[c], axis=0, keepdims=True), axis=1, keepdims=True)
        mine = mine + jnp.where(one == c * ROWS + layer // 2, total, 0.0)
        send[pl.ds(c, peers, BACK), :] = both[c]
    send[pl.ds(3, peers, BACK), :] = jnp.broadcast_to(mine, (peers, LANES))
    for place in range(4, BACK):
        send[pl.ds(place, peers, BACK), :] = jnp.zeros((peers, LANES), jnp.float32)


def solved_kernel(areas, peers, got, cross, state, trial, solved, sums):
    is_left = iota((ROWS, LANES), 1) < HALF
    u, w = [], []
    for c in range(3):
        low_cols = got[pl.ds(c, ROWS, 2 * BACK), :]
        high_cols = got[pl.ds(BACK + c, ROWS, 2 * BACK), :]
        u.append(jnp.where(is_left, low_cols, pltpu.roll(high_cols, HALF, 1)))
        w.append(jnp.where(is_left, pltpu.roll(low_cols, HALF, 1), high_cols))
    total = jnp.sum(got[pl.ds(3, peers, BACK), :], axis=0, keepdims=True)
    sums[...] = jnp.broadcast_to(total, (8 * areas, LANES))
    for k in range(DEPTH):
        part = add(vec([cross[e, k] for e in range(9)], u), vec([state[e, k] for e in range(9)], w))
        for c in range(3):
            solved[c, k] = trial[c, k] + part[c]


def wells_kernel(areas, nperf, nwell, tiles, counts, inverse, sums, solved, well, out):
    me = lax.axis_index("region") * lax.axis_size("column") + lax.axis_index("column")
    lane = iota((areas, LANES), 1)
    tile_all = iota((areas, LANES), 0) * ROWS + lane % ROWS
    tile_own = me * ROWS + iota((ROWS, LANES), 0)
    place_all = jnp.full((areas, LANES), -1, jnp.int32)
    place_own = jnp.full((ROWS, LANES), -1, jnp.int32)
    for p in range(nperf):
        place_all = jnp.where(tile_all == tiles[p], p, place_all)
        place_own = jnp.where(tile_own == tiles[p], p, place_own)
    well_all = jnp.where(place_all < 0, -1, 0)
    well_own = jnp.where(place_own < 0, -2, 0)
    end = 0
    for w in range(nwell):
        end = end + counts[w]
        well_all = well_all + (place_all >= end).astype(jnp.int32)
        well_own = well_own + (place_own >= end).astype(jnp.int32)
    gathered = jnp.zeros((ROWS, LANES), jnp.float32)
    for a in range(areas):
        same = well_own == well_all[a : a + 1, :]
        gathered = gathered + jnp.where(same, sums[8 * a : 8 * a + 1, :], 0.0)
    wide = iota((ROWS, LANES), 1)
    totals = [
        jnp.sum(
            jnp.where((wide >= c * ROWS) & (wide < (c + 1) * ROWS), gathered, 0.0),
            axis=1,
            keepdims=True,
        )
        for c in range(3)
    ]
    block = []
    for e in range(9):
        entry = jnp.zeros((ROWS, LANES), jnp.float32)
        for w in range(nwell):
            entry = jnp.where(well_own == w, inverse[e, w], entry)
        block.append(entry)
    rate = vec(block, totals)
    for k in range(DEPTH):
        for c in range(3):
            out[c, k] = solved[c, k] - (
                well[c, k] * rate[0] + well[3 + c, k] * rate[1] + well[6 + c, k] * rate[2]
            )


def f32(*shape):
    return jax.ShapeDtypeStruct(shape, jnp.float32)


def call(kernel, out_shape, scratch=(), in_specs=None):
    extra = {} if in_specs is None else {"in_specs": in_specs}
    return pl.pallas_call(
        kernel,
        out_shape=out_shape,
        scratch_shapes=scratch,
        compiler_params=pltpu.CompilerParams(vmem_limit_bytes=40 * 1024 * 1024),
        **extra,
    )


def moved(value, axis, by):
    count = lax.axis_size(axis)
    return lax.ppermute(value, axis, [(i, (i + by) % count) for i in range(count)])


def exchanged(value, axes):
    return lax.all_to_all(value, axes, split_axis=0, concat_axis=0, tiled=True)


def local(rhs, guess, diag, couple, pivot, lower, upper, well, inverse, tiles, counts):
    peers = lax.axis_size("layer")
    areas = lax.axis_size(AREA)
    cells = (DEPTH, ROWS, LANES)
    x_face, right_face, left_face = call(
        edges_kernel, (f32(3 * DEPTH, LANES), f32(ROWS, LANES), f32(ROWS, LANES))
    )(guess)
    right_in = moved(right_face, "column", 1)
    left_in = moved(left_face, "column", -1)
    x_in = moved(x_face, "region", 1)
    send, cross, state, trial, well_sums = call(
        maps_kernel,
        (f32(peers * PACK, LANES), f32(9, *cells), f32(9, *cells), f32(3, *cells), f32(8, LANES)),
        [pltpu.VMEM((3, DEPTH, 8, LANES), jnp.float32), pltpu.VMEM((9, DEPTH, 8, LANES), jnp.float32)],
    )(x_in, right_in, left_in, rhs, guess, diag, couple, pivot, lower, upper, well)
    got = exchanged(send.reshape(peers, PACK, LANES), "layer").reshape(peers * PACK, LANES)
    back = call(
        lambda *refs: chain_kernel(peers, *refs),
        f32(peers * BACK, LANES),
        [
            pltpu.VMEM((9, peers, LANES), jnp.float32),
            pltpu.VMEM((3, peers, LANES), jnp.float32),
            pltpu.VMEM((3, peers, LANES), jnp.float32),
        ],
    )(got, well_sums)
    got = exchanged(back.reshape(peers, BACK, LANES), "layer").reshape(peers * BACK, LANES)
    solved, sums = call(
        lambda *refs: solved_kernel(areas, peers, *refs), (f32(3, *cells), f32(8 * areas, LANES))
    )(got, cross, state, trial)
    sums = exchanged(sums.reshape(areas, 8, LANES), AREA).reshape(8 * areas, LANES)
    vmem = pl.BlockSpec(memory_space=pltpu.VMEM)
    smem = pl.BlockSpec(memory_space=pltpu.SMEM)
    return call(
        lambda *refs: wells_kernel(areas, tiles.shape[0], counts.shape[0], *refs),
        f32(3, *cells),
        in_specs=[smem, smem, smem, vmem, vmem, vmem],
    )(tiles, counts, inverse, sums, solved, well)


def solution(mesh):
    cells = P(None, "layer", "region", "column")
    return jax.shard_map(
        local,
        mesh=mesh,
        in_specs=(cells,) * 8 + (P(),) * 3,
        out_specs=cells,
        check_vma=False,
    )
```

time: 786 us -> 77.3 us (0.10)
  the two profiles are of different devices: /device:TPU:129 before, /device:TPU:1 now
where the time goes in v1:
time: 77.3 us; the launch traced here: 76.8 us
  blocking collectives  57.5 us (74%)
  local copies, waits for them, and re-layouts  7.84 us (10%)
  starting transfers between devices  6.02 us (8%)
  Pallas kernels  4.37 us (6%)
  waiting for transfers between devices  1.04 us (1%)
    all_to_all x3, blocking collectives, exchanged(): return lax.all_to_all(value, axes, split_axis=0, concat_axis=0, tiled=True)  57.5 us
    unnamed x22, local copies, waits for them, and re-layouts  7.84 us
    ppermute x3, starting transfers between devices, moved(): lax.ppermute(value, axis, [(i, (i + by) % count) for i in range(count)])  6.02 us
    pallas_call x1, Pallas kernels, local(): call(maps_kernel, (f32(peers * PACK, LANES), f32(9, *cells), f32(9, *cell...  1.69 us
    pallas_call x1, Pallas kernels, local(): call(lambda *refs: wells_kernel(areas, tiles.shape[0], counts.shape[0], *...  1.57 us
  transfers between devices with their start and end apart: 3, of which 1 were waited for; matrix products, arithmetic and copies ran while one was open for 0% of the time, Pallas kernels for 0%

profile of v1, /device:TPU:1, one launch (start us, length us, event | category | flops | bytes accessed | tf_op | source)
XLA Modules:
  0.0 76.8 jit_solution(14782360361172561317)
XLA Ops:
  0.0 0.0 copy-start.1
  0.0 0.9 %copy-done.1 = f32[3,8,16,128]{3,2,1,0:T(8,128)S(1)} copy-done((f32[3,8,16,128]{3,2,1,0:T(8,128)S(1)}, f32[3,8,16,128]{3,2,1,0:T(8,128)}, u32[]{:S(2)}) %copy-start.1) | copy-done | bytes 196632
  0.9 0.0 copy-start.6
  0.9 0.2 shard_map.109
  1.1 3.3 %collective-permute-start = (f32[24,128]{1,0:T(8,128)S(1)}, f32[24,128]{1,0:T(8,128)S(1)}, u32[]{:S(2)}, u32[]{:S(2)}) collective-permute-start(f32[24,128]{1,0:T(8,128)S(1)} %get-tuple-element.15), channel_id=1, source_target_pairs={{0,128},{128,0},{1,129},{129,1},{2,130},{130,2},{3,131},{131,3},{4... | collective-permute-start | bytes 36872 | tf_op jit(solution)/shard_map/ppermute | solution.py:302
  4.4 0.0 collective-permute-start.1
  4.4 2.7 %collective-permute-start.2 = (f32[16,128]{1,0:T(8,128)S(1)}, f32[16,128]{1,0:T(8,128)S(1)}, u32[]{:S(2)}, u32[]{:S(2)}) collective-permute-start(f32[16,128]{1,0:T(8,128)S(1)} %get-tuple-element.17), channel_id=1, source_target_pairs={{0,96},{32,0},{64,32},{96,64},{1,97},{33,1},{65,33},{97,65},{2,98}... | collective-permute-start | bytes 24584 | tf_op jit(solution)/shard_map/ppermute | solution.py:302
  7.1 1.0 %collective-permute-done.1.right_in = f32[16,128]{1,0:T(8,128)S(1)} collective-permute-done((f32[16,128]{1,0:T(8,128)S(1)}, f32[16,128]{1,0:T(8,128)S(1)}, u32[]{:S(2)}, u32[]{:S(2)}) %collective-permute-start.1) | collective-permute-done | bytes 8224 | tf_op jit(solution)/shard_map/ppermute | solution.py:302
  8.1 0.0 collective-permute-done.2.left_in
  8.2 0.0 collective-permute-done.x_in
  8.2 0.0 copy-done.6
  8.2 0.0 copy-start
  8.2 1.1 %copy-done = f32[9,8,16,128]{3,2,1,0:T(8,128)S(1)} copy-done((f32[9,8,16,128]{3,2,1,0:T(8,128)S(1)}, f32[9,8,16,128]{3,2,1,0:T(8,128)}, u32[]{:S(2)}) %copy-start) | copy-done | bytes 589848
  9.2 0.0 copy-start.2
  9.2 1.1 %copy-done.2 = f32[9,8,16,128]{3,2,1,0:T(8,128)S(1)} copy-done((f32[9,8,16,128]{3,2,1,0:T(8,128)S(1)}, f32[9,8,16,128]{3,2,1,0:T(8,128)}, u32[]{:S(2)}) %copy-start.2) | copy-done | bytes 589848
  10.3 0.0 copy-start.3
  10.3 1.1 %copy-done.3 = f32[9,8,16,128]{3,2,1,0:T(8,128)S(1)} copy-done((f32[9,8,16,128]{3,2,1,0:T(8,128)S(1)}, f32[9,8,16,128]{3,2,1,0:T(8,128)}, u32[]{:S(2)}) %copy-start.3) | copy-done | bytes 589848
  11.4 0.0 copy-start.4
  11.4 1.1 %copy-done.4 = f32[9,8,16,128]{3,2,1,0:T(8,128)S(1)} copy-done((f32[9,8,16,128]{3,2,1,0:T(8,128)S(1)}, f32[9,8,16,128]{3,2,1,0:T(8,128)}, u32[]{:S(2)}) %copy-start.4) | copy-done | bytes 589848
  12.4 0.0 copy-start.5
  12.4 1.1 %copy-done.5 = f32[9,8,16,128]{3,2,1,0:T(8,128)S(1)} copy-done((f32[9,8,16,128]{3,2,1,0:T(8,128)S(1)}, f32[9,8,16,128]{3,2,1,0:T(8,128)}, u32[]{:S(2)}) %copy-start.5) | copy-done | bytes 589848
  13.5 0.0 copy-start.7
  13.5 0.9 %copy-done.7 = f32[3,8,16,128]{3,2,1,0:T(8,128)S(1)} copy-done((f32[3,8,16,128]{3,2,1,0:T(8,128)S(1)}, f32[3,8,16,128]{3,2,1,0:T(8,128)}, u32[]{:S(2)}) %copy-start.7) | copy-done | bytes 196632
  14.4 1.7 %shard_map.110 = (f32[1536,128]{1,0:T(8,128)S(1)}, f32[9,8,16,128]{3,2,1,0:T(8,128)S(1)}, f32[9,8,16,128]{3,2,1,0:T(8,128)S(1)}, f32[3,8,16,128]{3,2,1,0:T(8,128)S(1)}, f32[8,128]{1,0:T(8,128)S(1)}) custom-call(f32[24,128]{1,0:T(8,128)S(1)} %collective-permute-done.x_in, f32[16,128]{1,0:T(8,128)S(1)} %collective-permute-done.1.right_in, ...), custom_call_target="tpu_custom_call" | custom-call | tf_op jit(solution)/shard_map/pallas_call | solution.py:319
  16.1 30.4 %all_to_all.15 = f32[32,48,128]{2,1,0:T(8,128)S(1)} all-to-all(f32[32,48,128]{2,1,0:T(8,128)S(1)} %bitcast.7), channel_id=1, replica_groups=mesh['region'=2,'column'=4,'layer'=32] {'layer'}, dimensions={0} | all-to-all | bytes 1572864 | tf_op jit(solution)/shard_map/all_to_all | solution.py:306
  46.5 0.7 shard_map.111
  47.2 15.2 %all_to_all.16 = f32[32,8,128]{2,1,0:T(8,128)S(1)} all-to-all(f32[32,8,128]{2,1,0:T(8,128)S(1)} %bitcast.9), channel_id=1, replica_groups=mesh['region'=2,'column'=4,'layer'=32] {'layer'}, dimensions={0} | all-to-all | bytes 262144 | tf_op jit(solution)/shard_map/all_to_all | solution.py:306
  62.4 0.0 copy-start.8
  62.4 0.2 shard_map.112
  62.6 11.9 %all_to_all.17 = f32[8,8,128]{2,1,0:T(8,128)S(1)} all-to-all(f32[8,8,128]{2,1,0:T(8,128)S(1)} %bitcast.11), channel_id=1, replica_groups=mesh['region'=2,'column'=4,'layer'=32] {'region','column'}, dimensions={0} | all-to-all | bytes 65536 | tf_op jit(solution)/shard_map/all_to_all | solution.py:306
  74.6 0.0 copy-start.9
  74.6 0.0 copy-start.10
  74.6 0.0 copy-done.8
  74.6 0.6 copy-done.9
  75.2 0.0 copy-done.10
  75.2 1.6 %shard_map.113 = f32[3,8,16,128]{3,2,1,0:T(8,128)} custom-call(s32[32]{0:T(128)S(1)} %copy-done.9, s32[16]{0:T(128)S(1)} %copy-done.10, f32[9,16]{1,0:T(8,128)S(1)} %copy-done.8, f32[64,128]{1,0:T(8,128)S(1)} %bitcast.10, f32[3,8,16,128]{3,2,1,0:T(8,128)S(1)} %get-tuple-element.24.refs_4_, f32[9,8,16,128]{3,2,1,0:T(8,128)S(1)} %copy-done), custom_call_target="tpu_custom_call" | custom-call | tf_op jit(solution)/shard_map/pallas_call | solution.py:341
Async XLA Ops:
  0.0 0.9 %copy-start.1 = (f32[3,8,16,128]{3,2,1,0:T(8,128)S(1)}, f32[3,8,16,128]{3,2,1,0:T(8,128)}, u32[]{:S(2)}) copy-start(f32[3,8,16,128]{3,2,1,0:T(8,128)} %guess.3) | copy-start | bytes 589828
  0.9 7.2 %copy-start.6 = (f32[3,8,16,128]{3,2,1,0:T(8,128)S(1)}, f32[3,8,16,128]{3,2,1,0:T(8,128)}, u32[]{:S(2)}) copy-start(f32[3,8,16,128]{3,2,1,0:T(8,128)} %rhs.1) | copy-start | bytes 589828
  1.1 7.1 %collective-permute-start = (f32[24,128]{1,0:T(8,128)S(1)}, f32[24,128]{1,0:T(8,128)S(1)}, u32[]{:S(2)}, u32[]{:S(2)}) collective-permute-start(f32[24,128]{1,0:T(8,128)S(1)} %get-tuple-element.15), channel_id=1, source_target_pairs={{0,128},{128,0},{1,129},{129,1},{2,130},{130,2},{3,131},{131,3},{4... | collective-permute-start | bytes 36872 | tf_op jit(solution)/shard_map/ppermute | solution.py:302
  4.4 3.7 %collective-permute-start.1 = (f32[16,128]{1,0:T(8,128)S(1)}, f32[16,128]{1,0:T(8,128)S(1)}, u32[]{:S(2)}, u32[]{:S(2)}) collective-permute-start(f32[16,128]{1,0:T(8,128)S(1)} %get-tuple-element.16), channel_id=1, source_target_pairs={{0,32},{32,64},{64,96},{96,0},{1,33},{33,65},{65,97},{97,1},{2,34}... | collective-permute-start | bytes 24584 | tf_op jit(solution)/shard_map/ppermute | solution.py:302
  4.4 3.7 %collective-permute-start.2 = (f32[16,128]{1,0:T(8,128)S(1)}, f32[16,128]{1,0:T(8,128)S(1)}, u32[]{:S(2)}, u32[]{:S(2)}) collective-permute-start(f32[16,128]{1,0:T(8,128)S(1)} %get-tuple-element.17), channel_id=1, source_target_pairs={{0,96},{32,0},{64,32},{96,64},{1,97},{33,1},{65,33},{97,65},{2,98}... | collective-permute-start | bytes 24584 | tf_op jit(solution)/shard_map/ppermute | solution.py:302
  8.2 1.1 %copy-start = (f32[9,8,16,128]{3,2,1,0:T(8,128)S(1)}, f32[9,8,16,128]{3,2,1,0:T(8,128)}, u32[]{:S(2)}) copy-start(f32[9,8,16,128]{3,2,1,0:T(8,128)} %refs_5_.1) | copy-start | bytes 1769476
  9.2 1.1 %copy-start.2 = (f32[9,8,16,128]{3,2,1,0:T(8,128)S(1)}, f32[9,8,16,128]{3,2,1,0:T(8,128)}, u32[]{:S(2)}) copy-start(f32[9,8,16,128]{3,2,1,0:T(8,128)} %diag.1) | copy-start | bytes 1769476
  10.3 1.1 %copy-start.3 = (f32[9,8,16,128]{3,2,1,0:T(8,128)S(1)}, f32[9,8,16,128]{3,2,1,0:T(8,128)}, u32[]{:S(2)}) copy-start(f32[9,8,16,128]{3,2,1,0:T(8,128)} %pivot.1) | copy-start | bytes 1769476
  11.4 1.1 %copy-start.4 = (f32[9,8,16,128]{3,2,1,0:T(8,128)S(1)}, f32[9,8,16,128]{3,2,1,0:T(8,128)}, u32[]{:S(2)}) copy-start(f32[9,8,16,128]{3,2,1,0:T(8,128)} %lower.1) | copy-start | bytes 1769476
  12.4 1.1 %copy-start.5 = (f32[9,8,16,128]{3,2,1,0:T(8,128)S(1)}, f32[9,8,16,128]{3,2,1,0:T(8,128)}, u32[]{:S(2)}) copy-start(f32[9,8,16,128]{3,2,1,0:T(8,128)} %upper.1) | copy-start | bytes 1769476
  13.5 0.9 %copy-start.7 = (f32[3,8,16,128]{3,2,1,0:T(8,128)S(1)}, f32[3,8,16,128]{3,2,1,0:T(8,128)}, u32[]{:S(2)}) copy-start(f32[3,8,16,128]{3,2,1,0:T(8,128)} %couple.1) | copy-start | bytes 589828
  62.4 12.1 %copy-start.8 = (f32[9,16]{1,0:T(8,128)S(1)}, f32[9,16]{1,0:T(8,128)}, u32[]{:S(2)}) copy-start(f32[9,16]{1,0:T(8,128)} %refs_2_.1) | copy-start | bytes 1732
  74.6 0.7 copy-start.9
  74.6 0.7 copy-start.10

commit v2 on v1

v2 whole, which is shorter than its diff:
```python
import jax
import jax.numpy as jnp
from jax import lax
from jax.experimental import pallas as pl
from jax.experimental.pallas import tpu as pltpu
from jax.sharding import PartitionSpec as P

AREA = ("region", "column")
DEPTH, ROWS, LANES = 8, 16, 128
HALF = LANES // 2
PACK = 32
BACK = 8

STEP, MIXED, WELL, SOURCE = 0, 9, 18, 27


def mat(a, b):
    return [
        a[3 * i] * b[m] + a[3 * i + 1] * b[3 + m] + a[3 * i + 2] * b[6 + m]
        for i in range(3)
        for m in range(3)
    ]


def vec(a, x):
    return [a[3 * i] * x[0] + a[3 * i + 1] * x[1] + a[3 * i + 2] * x[2] for i in range(3)]


def neg(a):
    return [-entry for entry in a]


def add(a, b):
    return [x + y for x, y in zip(a, b)]


def sub(a, b):
    return [x - y for x, y in zip(a, b)]


def iota(shape, axis):
    return lax.broadcasted_iota(jnp.int32, shape, axis)


def edges_kernel(guess, x_out, right_out, left_out, top_out, bottom_out):
    region = lax.axis_index("region")
    lane = iota((ROWS, LANES), 1)
    right = jnp.zeros((ROWS, LANES), jnp.float32)
    left = jnp.zeros((ROWS, LANES), jnp.float32)
    for c in range(3):
        for k in range(DEPTH):
            place = c * DEPTH + k
            block = guess[c, k]
            right = jnp.where(lane == place, pltpu.roll(block, (place + 1) % LANES, 1), right)
            left = jnp.where(lane == place, pltpu.roll(block, place, 1) if place else block, left)
            x_out[place : place + 1, :] = jnp.where(
                region == 0, guess[c, k, ROWS - 1 :, :], guess[c, k, :1, :]
            )
        top_out[c] = guess[c, DEPTH - 1]
        bottom_out[c] = guess[c, 0]
    right_out[...] = right
    left_out[...] = left


def put(send, h, place, left, right):
    is_left = iota((8, LANES), 1) < HALF
    low_cols = jnp.where(is_left, left, pltpu.roll(right, HALF, 1))
    high_cols = jnp.where(is_left, pltpu.roll(left, HALF, 1), right)
    send[pl.ds(16 * h * PACK + place, 8, 2 * PACK), :] = low_cols
    send[pl.ds((16 * h + 1) * PACK + place, 8, 2 * PACK), :] = high_cols


def well_masks(areas, nperf, nwell, tiles, counts, inverse, same_out, block_out):
    me = lax.axis_index("region") * lax.axis_size("column") + lax.axis_index("column")
    tile_all = iota((areas, LANES), 0) * ROWS + iota((areas, LANES), 1) % ROWS
    tile_own = me * ROWS + iota((ROWS, LANES), 0)
    place_all = jnp.full((areas, LANES), -1, jnp.int32)
    place_own = jnp.full((ROWS, LANES), -1, jnp.int32)
    for p in range(nperf):
        place_all = jnp.where(tile_all == tiles[p], p, place_all)
        place_own = jnp.where(tile_own == tiles[p], p, place_own)
    well_all = jnp.where(place_all < 0, -1, 0)
    well_own = jnp.where(place_own < 0, -2, 0)
    end = 0
    for w in range(nwell):
        end = end + counts[w]
        well_all = well_all + (place_all >= end).astype(jnp.int32)
        well_own = well_own + (place_own >= end).astype(jnp.int32)
    for a in range(areas):
        same_out[a] = (well_own == well_all[a : a + 1, :]).astype(jnp.float32)
    for e in range(9):
        entry = jnp.zeros((ROWS, LANES), jnp.float32)
        for w in range(nwell):
            entry = jnp.where(well_own == w, inverse[e, w], entry)
        block_out[e] = entry


def maps_kernel(
    areas, nperf, nwell,
    tiles, counts, inverse, pivot, lower, upper, well,
    send, cross_out, state_out, same_out, block_out, states,
):
    well_masks(areas, nperf, nwell, tiles, counts, inverse, same_out, block_out)
    top = DEPTH - 1
    for h in range(2):
        at = slice(8 * h, 8 * h + 8)

        def load(ref, k):
            return [ref[c, k, at, :] for c in range(9)]

        state = None
        for k in range(DEPTH):
            low = load(lower, k)
            state = neg(mat(load(pivot, k), low if k == 0 else mat(low, state)))
            for c in range(9):
                states[c, k] = state[c]
        down = state
        cross = state
        well_state, well_cross = None, None
        for k in reversed(range(DEPTH)):
            both = mat(load(pivot, k), load(upper, k))
            if k == top:
                state = neg(both)
            else:
                cross = sub([states[c, k] for c in range(9)], mat(both, cross))
                state = neg(mat(both, state))
            coef = load(well, k)
            more_state, more_cross = mat(coef, state), mat(coef, cross)
            well_state = more_state if k == top else add(well_state, more_state)
            well_cross = more_cross if k == top else add(well_cross, more_cross)
            for c in range(9):
                cross_out[c, k, at, :] = cross[c]
                state_out[c, k, at, :] = state[c]
        zero = jnp.zeros((8, LANES), jnp.float32)
        for e in range(9):
            put(send, h, STEP + e, down[e], state[e])
            put(send, h, MIXED + e, well_cross[e], cross[e])
            put(send, h, WELL + e, zero, well_state[e])
        for place in range(30, PACK):
            put(send, h, place, zero, zero)


def trial_kernel(
    x_in, right_in, left_in, below_in, above_in, rhs, guess, diag, couple, pivot, lower, upper, well, sent,
    send, trial_out, well_out, forward,
):
    region = lax.axis_index("region")
    column = lax.axis_index("column")
    layer = lax.axis_index("layer")
    n_column = lax.axis_size("column")
    n_layer = lax.axis_size("layer")
    lane = iota((8, LANES), 1)
    row = iota((8, LANES), 0)
    top = DEPTH - 1
    well_sums = jnp.zeros((8, LANES), jnp.float32)
    for h in range(2):
        at = slice(8 * h, 8 * h + 8)

        def load(ref, k, count=9):
            return [ref[c, k, at, :] for c in range(count)]

        edge_right = jnp.where(column > 0, right_in[at, :], 0.0)
        edge_left = jnp.where(column < n_column - 1, left_in[at, :], 0.0)

        def residual(k):
            mid = load(guess, k, 3)
            out = vec(load(diag, k), mid)
            for c in range(3):
                g = mid[c]
                place = c * DEPTH + k
                x_row = x_in[place : place + 1, :]
                if h == 0:
                    outer = jnp.where(region > 0, x_row, 0.0)
                    below = jnp.where(row == 0, outer, pltpu.roll(g, 1, 0))
                    above = guess[c, k, 1:9, :]
                else:
                    outer = jnp.where(region == 0, x_row, 0.0)
                    below = guess[c, k, 7:15, :]
                    above = jnp.where(row == 7, outer, pltpu.roll(g, 7, 0))
                first = pltpu.roll(edge_right, LANES - place, 1) if place else edge_right
                before = jnp.where(lane == 0, first, pltpu.roll(g, 1, 1))
                last = pltpu.roll(edge_left, LANES - 1 - place, 1)
                after = jnp.where(lane == LANES - 1, last, pltpu.roll(g, LANES - 1, 1))
                beside = below + above + before + after
                if k > 0:
                    beside = beside + guess[c, k - 1, at, :]
                else:
                    beside = beside + jnp.where(layer > 0, below_in[c, at, :], 0.0)
                if k < top:
                    beside = beside + guess[c, k + 1, at, :]
                else:
                    beside = beside + jnp.where(layer < n_layer - 1, above_in[c, at, :], 0.0)
                out[c] = rhs[c, k, at, :] - (out[c] - couple[c, k, at, :] * beside)
            return out

        f = None
        for k in range(DEPTH):
            res = residual(k)
            f = vec(load(pivot, k), res if k == 0 else sub(res, vec(load(lower, k), f)))
            for c in range(3):
                forward[c, k] = f[c]
        s, well_const = f, None
        for k in reversed(range(DEPTH)):
            if k < top:
                s = sub([forward[c, k] for c in range(3)], vec(load(pivot, k), vec(load(upper, k), s)))
            more = vec(load(well, k), s)
            well_const = more if k == top else add(well_const, more)
            for c in range(3):
                trial_out[c, k, at, :] = s[c]
        for c in range(3):
            put(send, h, SOURCE + c, f[c], s[c])
            total = jnp.sum(well_const[c], axis=1, keepdims=True)
            well_sums = well_sums + jnp.where(lane == c * ROWS + 8 * h + row, total, 0.0)
    well_out[...] = jnp.broadcast_to(jnp.sum(well_sums, axis=0, keepdims=True), (8, LANES))


def chain_kernel(peers, got, well_sums, send, step_ref, base_ref, inflow_ref):
    layer = lax.axis_index("layer")
    is_left = iota((peers, LANES), 1) < HALF

    def take(place, count):
        return [got[pl.ds(place + e, peers, PACK), :] for e in range(count)]

    def chain(base, order):
        for c in range(3):
            base_ref[c] = base[c]
        x = [jnp.zeros((1, LANES), jnp.float32)] * 3
        for d in order:
            at = slice(d, d + 1)
            for c in range(3):
                inflow_ref[c, at, :] = x[c]
            x = add([base_ref[c, at, :] for c in range(3)], vec([step_ref[e, at, :] for e in range(9)], x))
        return [inflow_ref[c] for c in range(3)]

    for e, step in enumerate(take(STEP, 9)):
        step_ref[e] = step
    source = take(SOURCE, 3)
    mixed = take(MIXED, 9)
    down = chain(source, range(peers))
    up_base = add(source, vec(mixed, [pltpu.roll(x, HALF, 1) for x in down]))
    up = chain(up_base, reversed(range(peers)))
    both = [jnp.where(is_left, a, b) for a, b in zip(down, up)]
    coef = [jnp.where(is_left, a, b) for a, b in zip(mixed, take(WELL, 9))]
    parts = vec(coef, both)
    mine = well_sums[0:1, :]
    one = iota((1, LANES), 1)
    for c in range(3):
        total = jnp.sum(jnp.sum(parts[c], axis=0, keepdims=True), axis=1, keepdims=True)
        mine = mine + jnp.where(one == c * ROWS + layer // 2, total, 0.0)
        send[pl.ds(c, peers, BACK), :] = both[c]
    send[pl.ds(3, peers, BACK), :] = jnp.broadcast_to(mine, (peers, LANES))
    for place in range(4, BACK):
        send[pl.ds(place, peers, BACK), :] = jnp.zeros((peers, LANES), jnp.float32)


def solved_kernel(areas, peers, got, cross, state, trial, solved, sums):
    is_left = iota((ROWS, LANES), 1) < HALF
    u, w = [], []
    for c in range(3):
        low_cols = got[pl.ds(c, ROWS, 2 * BACK), :]
        high_cols = got[pl.ds(BACK + c, ROWS, 2 * BACK), :]
        u.append(jnp.where(is_left, low_cols, pltpu.roll(high_cols, HALF, 1)))
        w.append(jnp.where(is_left, pltpu.roll(low_cols, HALF, 1), high_cols))
    total = jnp.sum(got[pl.ds(3, peers, BACK), :], axis=0, keepdims=True)
    sums[...] = jnp.broadcast_to(total, (8 * areas, LANES))
    for k in range(DEPTH):
        part = add(vec([cross[e, k] for e in range(9)], u), vec([state[e, k] for e in range(9)], w))
        for c in range(3):
            solved[c, k] = trial[c, k] + part[c]


def wells_kernel(areas, sums, same, block, solved, well, out):
    gathered = jnp.zeros((ROWS, LANES), jnp.float32)
    for a in range(areas):
        gathered = gathered + jnp.where(same[a] > 0.0, sums[8 * a : 8 * a + 1, :], 0.0)
    wide = iota((ROWS, LANES), 1)
    totals = [
        jnp.sum(
            jnp.where((wide >= c * ROWS) & (wide < (c + 1) * ROWS), gathered, 0.0),
            axis=1,
            keepdims=True,
        )
        for c in range(3)
    ]
    rate = vec([block[e] for e in range(9)], totals)
    for k in range(DEPTH):
        for c in range(3):
            out[c, k] = solved[c, k] - (
                well[c, k] * rate[0] + well[3 + c, k] * rate[1] + well[6 + c, k] * rate[2]
            )


def f32(*shape):
    return jax.ShapeDtypeStruct(shape, jnp.float32)


VMEM = pl.BlockSpec(memory_space=pltpu.VMEM)
SMEM = pl.BlockSpec(memory_space=pltpu.SMEM)
LONG = pl.CostEstimate(flops=20_000_000, bytes_accessed=8_000_000, transcendentals=0)
FIRST = pl.CostEstimate(flops=20_000_000_000, bytes_accessed=80_000_000, transcendentals=0)


def call(kernel, out_shape, in_specs, scratch=(), cost=None, aliases=None):
    return pl.pallas_call(
        kernel,
        out_shape=out_shape,
        in_specs=in_specs,
        out_specs=jax.tree.map(lambda _: VMEM, out_shape),
        scratch_shapes=scratch,
        cost_estimate=cost,
        input_output_aliases=aliases or {},
        compiler_params=pltpu.CompilerParams(vmem_limit_bytes=32 * 1024 * 1024),
    )


def moved(value, axis, by):
    count = lax.axis_size(axis)
    return lax.ppermute(value, axis, [(i, (i + by) % count) for i in range(count)])


def exchanged(value, axes):
    return lax.all_to_all(value, axes, split_axis=0, concat_axis=0, tiled=True)


def local(rhs, guess, diag, couple, pivot, lower, upper, well, inverse, tiles, counts):
    peers = lax.axis_size("layer")
    areas = lax.axis_size(AREA)
    cells = (DEPTH, ROWS, LANES)
    x_face, right_face, left_face, top_face, bottom_face = call(
        edges_kernel,
        (
            f32(3 * DEPTH, LANES), f32(ROWS, LANES), f32(ROWS, LANES),
            f32(3, ROWS, LANES), f32(3, ROWS, LANES),
        ),
        [VMEM],
        cost=FIRST,
    )(guess)
    below_in = moved(top_face, "layer", 1)
    above_in = moved(bottom_face, "layer", -1)
    right_in = moved(right_face, "column", 1)
    left_in = moved(left_face, "column", -1)
    x_in = moved(x_face, "region", 1)
    nine, three = f32(9, *cells), f32(3, *cells)
    send, cross, state, same, block = call(
        lambda *refs: maps_kernel(areas, tiles.shape[0], counts.shape[0], *refs),
        (f32(peers * PACK, LANES), nine, nine, f32(areas, ROWS, LANES), f32(9, ROWS, LANES)),
        [SMEM] * 3 + [VMEM] * 4,
        [pltpu.VMEM((9, DEPTH, 8, LANES), jnp.float32)],
        cost=LONG,
    )(tiles, counts, inverse, pivot, lower, upper, well)
    send, trial, well_sums = call(
        trial_kernel,
        (f32(peers * PACK, LANES), three, f32(8, LANES)),
        [VMEM] * 14,
        [pltpu.VMEM((3, DEPTH, 8, LANES), jnp.float32)],
        aliases={13: 0},
    )(x_in, right_in, left_in, below_in, above_in, rhs, guess, diag, couple, pivot, lower, upper, well, send)
    got = exchanged(send.reshape(peers, PACK, LANES), "layer").reshape(peers * PACK, LANES)
    back = call(
        lambda *refs: chain_kernel(peers, *refs),
        f32(peers * BACK, LANES),
        [VMEM] * 2,
        [
            pltpu.VMEM((9, peers, LANES), jnp.float32),
            pltpu.VMEM((3, peers, LANES), jnp.float32),
            pltpu.VMEM((3, peers, LANES), jnp.float32),
        ],
    )(got, well_sums)
    got = exchanged(back.reshape(peers, BACK, LANES), "layer").reshape(peers * BACK, LANES)
    solved, sums = call(
        lambda *refs: solved_kernel(areas, peers, *refs), (three, f32(8 * areas, LANES)), [VMEM] * 4
    )(got, cross, state, trial)
    sums = exchanged(sums.reshape(areas, 8, LANES), AREA).reshape(8 * areas, LANES)
    return call(lambda *refs: wells_kernel(areas, *refs), three, [VMEM] * 5)(
        sums, same, block, solved, well
    )


def solution(mesh):
    cells = P(None, "layer", "region", "column")
    return jax.shard_map(
        local,
        mesh=mesh,
        in_specs=(cells,) * 8 + (P(),) * 3,
        out_specs=cells,
        check_vma=False,
    )
```

time: 77.3 us -> 65.6 us (0.85)
  blocking collectives: 57.5 us -> 47 us
  local copies, waits for them, and re-layouts: 7.84 us -> 1.12 us
  starting transfers between devices: 6.02 us -> 12.7 us
  waiting for transfers between devices: 1.04 us -> 0.01 us
    all_to_all x3, blocking collectives: 57.5 us -> 47 us  [exchanged(): return lax.all_to_all(value, axes, split_axis=0, concat_axis=0, tiled=True)]
    unnamed x22 -> x24, local copies, waits for them, and re-layouts: 7.84 us -> 1.12 us
    ppermute x3 -> x5, starting transfers between devices: 6.02 us -> 12.7 us  [moved(): lax.ppermute(value, axis, [(i, (i + by) % count) for i in range(count)])]
    ppermute x3 -> x5, waiting for transfers between devices: 1.04 us -> 0.01 us  [moved(): lax.ppermute(value, axis, [(i, (i + by) % count) for i in range(count)])]
    pallas_call x3 -> x4, Pallas kernels: 3.48 us -> 3.54 us  [the longest x1 1.95 us: local(): call(lambda *refs: maps_kernel(areas, tiles.shape[0], counts.shape[0], *r...]
  transfers between devices with their start and end apart: 3 -> 5, of which waited for: 1 -> 0; matrix products, arithmetic and copies ran while one was open for 0% -> 0% of each run, Pallas kernels for 0% -> 3%
where the time goes in v2:
time: 65.6 us; the launch traced here: 65.4 us
  blocking collectives  47 us (72%)
  starting transfers between devices  12.7 us (19%)
  Pallas kernels  4.35 us (7%)
  local copies, waits for them, and re-layouts  1.12 us (2%)
    all_to_all x3, blocking collectives, exchanged(): return lax.all_to_all(value, axes, split_axis=0, concat_axis=0, tiled=True)  47 us
    ppermute x5, starting transfers between devices, moved(): lax.ppermute(value, axis, [(i, (i + by) % count) for i in range(count)])  12.7 us
    pallas_call x1, Pallas kernels, local(): call(lambda *refs: maps_kernel(areas, tiles.shape[0], counts.shape[0], *r...  1.95 us
  transfers between devices with their start and end apart: 5, of which 0 were waited for; matrix products, arithmetic and copies ran while one was open for 0% of the time, Pallas kernels for 3%

profile of v2, /device:TPU:1, one launch (start us, length us, event | category | flops | bytes accessed | tf_op | source)
XLA Modules:
  0.0 65.4 jit_solution(9632974188730112378)
XLA Ops:
  0.0 0.0 copy-start
  0.0 0.0 copy-start.3
  0.0 0.0 copy-start.2
  0.0 0.0 copy-start.1
  0.0 0.0 copy-start.5
  0.0 1.1 %copy-done.5 = f32[3,8,16,128]{3,2,1,0:T(8,128)S(1)} copy-done((f32[3,8,16,128]{3,2,1,0:T(8,128)S(1)}, f32[3,8,16,128]{3,2,1,0:T(8,128)}, u32[]{:S(2)}) %copy-start.5) | copy-done | bytes 196632
  1.1 0.2 shard_map.109
  1.3 0.0 copy-start.9
  1.3 2.2 %collective-permute-start.3 = (f32[3,16,128]{2,1,0:T(8,128)S(1)}, f32[3,16,128]{2,1,0:T(8,128)S(1)}, u32[]{:S(2)}, u32[]{:S(2)}) collective-permute-start(f32[3,16,128]{2,1,0:T(8,128)S(1)} %get-tuple-element.23), channel_id=1, source_target_pairs={{0,1},{1,2},{2,3},{3,4},{4,5},{5,6},{6,7},{7,8},{8,9},{9,10},{10,1... | collective-permute-start | bytes 73736 | tf_op jit(solution)/shard_map/ppermute | solution.py:318
  3.5 6.8 %collective-permute-start.4 = (f32[3,16,128]{2,1,0:T(8,128)S(1)}, f32[3,16,128]{2,1,0:T(8,128)S(1)}, u32[]{:S(2)}, u32[]{:S(2)}) collective-permute-start(f32[3,16,128]{2,1,0:T(8,128)S(1)} %get-tuple-element.24), channel_id=1, source_target_pairs={{0,31},{1,0},{2,1},{3,2},{4,3},{5,4},{6,5},{7,6},{8,7},{9,8},{10,9... | collective-permute-start | bytes 73736 | tf_op jit(solution)/shard_map/ppermute | solution.py:318
  10.3 1.0 %collective-permute-start = (f32[24,128]{1,0:T(8,128)S(1)}, f32[24,128]{1,0:T(8,128)S(1)}, u32[]{:S(2)}, u32[]{:S(2)}) collective-permute-start(f32[24,128]{1,0:T(8,128)S(1)} %get-tuple-element.20), channel_id=1, source_target_pairs={{0,128},{128,0},{1,129},{129,1},{2,130},{130,2},{3,131},{131,3},{4... | collective-permute-start | bytes 36872 | tf_op jit(solution)/shard_map/ppermute | solution.py:318
  11.3 0.0 copy-start.10
  11.3 0.0 copy-start.11
  11.3 1.2 %collective-permute-start.1 = (f32[16,128]{1,0:T(8,128)S(1)}, f32[16,128]{1,0:T(8,128)S(1)}, u32[]{:S(2)}, u32[]{:S(2)}) collective-permute-start(f32[16,128]{1,0:T(8,128)S(1)} %get-tuple-element.21), channel_id=1, source_target_pairs={{0,32},{32,64},{64,96},{96,0},{1,33},{33,65},{65,97},{97,1},{2,34}... | collective-permute-start | bytes 24584 | tf_op jit(solution)/shard_map/ppermute | solution.py:318
  12.5 0.0 copy-start.4
  12.5 0.0 copy-start.6
  12.5 0.0 copy-start.7
  12.5 0.0 copy-start.8
  12.5 1.5 %collective-permute-start.2 = (f32[16,128]{1,0:T(8,128)S(1)}, f32[16,128]{1,0:T(8,128)S(1)}, u32[]{:S(2)}, u32[]{:S(2)}) collective-permute-start(f32[16,128]{1,0:T(8,128)S(1)} %get-tuple-element.22), channel_id=1, source_target_pairs={{0,96},{32,0},{64,32},{96,64},{1,97},{33,1},{65,33},{97,65},{2,98}... | collective-permute-start | bytes 24584 | tf_op jit(solution)/shard_map/ppermute | solution.py:318
  14.0 0.0 copy-done
  14.0 0.0 copy-done.3
  14.0 0.0 copy-done.2
  14.0 0.0 copy-done.1
  14.0 0.0 copy-done.9
  14.0 0.0 copy-done.10
  14.1 0.0 copy-done.11
  14.1 1.9 %shard_map.110 = (f32[1024,128]{1,0:T(8,128)S(1)}, f32[9,8,16,128]{3,2,1,0:T(8,128)S(1)}, f32[9,8,16,128]{3,2,1,0:T(8,128)S(1)}, f32[8,16,128]{2,1,0:T(8,128)S(1)}, f32[9,16,128]{2,1,0:T(8,128)S(1)}) custom-call(s32[32]{0:T(128)S(1)} %copy-done.10, s32[16]{0:T(128)S(1)} %copy-done.11, f32[9,16]{1,0:T(8,128)S(1)} %copy-done.9, ...), custom_call_target="tpu_custom_call" | custom-call | flops 20000000 | bytes 8000000 | tf_op jit(solution)/shard_map/pallas_call | solution.py:344
  16.0 0.0 collective-permute-done.1.right_in
  16.0 0.0 collective-permute-done.2.left_in
  16.0 0.0 collective-permute-done.x_in
  16.1 0.0 collective-permute-done.3.below_in
  16.1 0.0 collective-permute-done.4.above_in
  16.1 0.0 copy-done.4
  16.1 0.0 copy-done.6
  16.1 0.0 copy-done.7
  16.1 0.0 copy-done.8
  16.1 0.5 shard_map.111
  16.7 21.7 %all_to_all.15 = f32[32,32,128]{2,1,0:T(8,128)S(1)} all-to-all(f32[32,32,128]{2,1,0:T(8,128)S(1)} %bitcast.6), channel_id=1, replica_groups=mesh['region'=2,'column'=4,'layer'=32] {'layer'}, dimensions={0} | all-to-all | bytes 1048576 | tf_op jit(solution)/shard_map/all_to_all | solution.py:322
  38.4 0.7 shard_map.112
  39.0 14.3 %all_to_all.16 = f32[32,8,128]{2,1,0:T(8,128)S(1)} all-to-all(f32[32,8,128]{2,1,0:T(8,128)S(1)} %bitcast.9), channel_id=1, replica_groups=mesh['region'=2,'column'=4,'layer'=32] {'layer'}, dimensions={0} | all-to-all | bytes 262144 | tf_op jit(solution)/shard_map/all_to_all | solution.py:322
  53.3 0.2 shard_map.113
  53.5 11.0 %all_to_all.17 = f32[8,8,128]{2,1,0:T(8,128)S(1)} all-to-all(f32[8,8,128]{2,1,0:T(8,128)S(1)} %bitcast.11), channel_id=1, replica_groups=mesh['region'=2,'column'=4,'layer'=32] {'region','column'}, dimensions={0} | all-to-all | bytes 65536 | tf_op jit(solution)/shard_map/all_to_all | solution.py:322
  64.5 0.8 %shard_map.114 = f32[3,8,16,128]{3,2,1,0:T(8,128)} custom-call(f32[64,128]{1,0:T(8,128)S(1)} %bitcast.10, f32[8,16,128]{2,1,0:T(8,128)S(1)} %get-tuple-element.32.refs_1_, f32[9,16,128]{2,1,0:T(8,128)S(1)} %get-tuple-element.33.refs_2_, f32[3,8,16,128]{3,2,1,0:T(8,128)S(1)} %get-tuple-element.34.refs_3_, f32[9,8,16,128]{3,2,1,0:T(8,128)S(1)} %copy-done), custom_call_target="tpu_custom_call" | custom-call | tf_op jit(solution)/shard_map/pallas_call | solution.py:374
Async XLA Ops:
  0.0 14.0 %copy-start = (f32[9,8,16,128]{3,2,1,0:T(8,128)S(1)}, f32[9,8,16,128]{3,2,1,0:T(8,128)}, u32[]{:S(2)}) copy-start(f32[9,8,16,128]{3,2,1,0:T(8,128)} %refs_4_.3) | copy-start | bytes 1769476
  0.0 14.0 %copy-start.3 = (f32[9,8,16,128]{3,2,1,0:T(8,128)S(1)}, f32[9,8,16,128]{3,2,1,0:T(8,128)}, u32[]{:S(2)}) copy-start(f32[9,8,16,128]{3,2,1,0:T(8,128)} %upper.1) | copy-start | bytes 1769476
  0.0 14.0 %copy-start.2 = (f32[9,8,16,128]{3,2,1,0:T(8,128)S(1)}, f32[9,8,16,128]{3,2,1,0:T(8,128)}, u32[]{:S(2)}) copy-start(f32[9,8,16,128]{3,2,1,0:T(8,128)} %lower.1) | copy-start | bytes 1769476
  0.0 14.0 %copy-start.1 = (f32[9,8,16,128]{3,2,1,0:T(8,128)S(1)}, f32[9,8,16,128]{3,2,1,0:T(8,128)}, u32[]{:S(2)}) copy-start(f32[9,8,16,128]{3,2,1,0:T(8,128)} %pivot.1) | copy-start | bytes 1769476
  0.0 1.1 %copy-start.5 = (f32[3,8,16,128]{3,2,1,0:T(8,128)S(1)}, f32[3,8,16,128]{3,2,1,0:T(8,128)}, u32[]{:S(2)}) copy-start(f32[3,8,16,128]{3,2,1,0:T(8,128)} %guess.3) | copy-start | bytes 589828
  1.3 12.8 %copy-start.9 = (f32[9,16]{1,0:T(8,128)S(1)}, f32[9,16]{1,0:T(8,128)}, u32[]{:S(2)}) copy-start(f32[9,16]{1,0:T(8,128)} %refs_2_.1) | copy-start | bytes 1732
  1.3 14.8 %collective-permute-start.3 = (f32[3,16,128]{2,1,0:T(8,128)S(1)}, f32[3,16,128]{2,1,0:T(8,128)S(1)}, u32[]{:S(2)}, u32[]{:S(2)}) collective-permute-start(f32[3,16,128]{2,1,0:T(8,128)S(1)} %get-tuple-element.23), channel_id=1, source_target_pairs={{0,1},{1,2},{2,3},{3,4},{4,5},{5,6},{6,7},{7,8},{8,9},{9,10},{10,1... | collective-permute-start | bytes 73736 | tf_op jit(solution)/shard_map/ppermute | solution.py:318
  3.5 12.6 %collective-permute-start.4 = (f32[3,16,128]{2,1,0:T(8,128)S(1)}, f32[3,16,128]{2,1,0:T(8,128)S(1)}, u32[]{:S(2)}, u32[]{:S(2)}) collective-permute-start(f32[3,16,128]{2,1,0:T(8,128)S(1)} %get-tuple-element.24), channel_id=1, source_target_pairs={{0,31},{1,0},{2,1},{3,2},{4,3},{5,4},{6,5},{7,6},{8,7},{9,8},{10,9... | collective-permute-start | bytes 73736 | tf_op jit(solution)/shard_map/ppermute | solution.py:318
  10.3 5.8 %collective-permute-start = (f32[24,128]{1,0:T(8,128)S(1)}, f32[24,128]{1,0:T(8,128)S(1)}, u32[]{:S(2)}, u32[]{:S(2)}) collective-permute-start(f32[24,128]{1,0:T(8,128)S(1)} %get-tuple-element.20), channel_id=1, source_target_pairs={{0,128},{128,0},{1,129},{129,1},{2,130},{130,2},{3,131},{131,3},{4... | collective-permute-start | bytes 36872 | tf_op jit(solution)/shard_map/ppermute | solution.py:318
  11.3 2.8 %copy-start.10 = (s32[32]{0:T(128)S(1)}, s32[32]{0:T(128)}, u32[]{:S(2)}) copy-start(s32[32]{0:T(128)} %refs_0_.1) | copy-start | bytes 388
  11.3 2.8 %copy-start.11 = (s32[16]{0:T(128)S(1)}, s32[16]{0:T(128)}, u32[]{:S(2)}) copy-start(s32[16]{0:T(128)} %refs_1_.1) | copy-start | bytes 196
  11.3 4.8 %collective-permute-start.1 = (f32[16,128]{1,0:T(8,128)S(1)}, f32[16,128]{1,0:T(8,128)S(1)}, u32[]{:S(2)}, u32[]{:S(2)}) collective-permute-start(f32[16,128]{1,0:T(8,128)S(1)} %get-tuple-element.21), channel_id=1, source_target_pairs={{0,32},{32,64},{64,96},{96,0},{1,33},{33,65},{65,97},{97,1},{2,34}... | collective-permute-start | bytes 24584 | tf_op jit(solution)/shard_map/ppermute | solution.py:318
  12.5 3.6 %copy-start.4 = (f32[9,8,16,128]{3,2,1,0:T(8,128)S(1)}, f32[9,8,16,128]{3,2,1,0:T(8,128)}, u32[]{:S(2)}) copy-start(f32[9,8,16,128]{3,2,1,0:T(8,128)} %diag.1) | copy-start | bytes 1769476
  12.5 3.6 %copy-start.6 = (f32[3,8,16,128]{3,2,1,0:T(8,128)S(1)}, f32[3,8,16,128]{3,2,1,0:T(8,128)}, u32[]{:S(2)}) copy-start(f32[3,8,16,128]{3,2,1,0:T(8,128)} %guess.3) | copy-start | bytes 589828
  12.5 3.6 %copy-start.7 = (f32[3,8,16,128]{3,2,1,0:T(8,128)S(1)}, f32[3,8,16,128]{3,2,1,0:T(8,128)}, u32[]{:S(2)}) copy-start(f32[3,8,16,128]{3,2,1,0:T(8,128)} %rhs.1) | copy-start | bytes 589828
  12.5 3.6 %copy-start.8 = (f32[3,8,16,128]{3,2,1,0:T(8,128)S(1)}, f32[3,8,16,128]{3,2,1,0:T(8,128)}, u32[]{:S(2)}) copy-start(f32[3,8,16,128]{3,2,1,0:T(8,128)} %couple.1) | copy-start | bytes 589828
  12.5 3.6 %collective-permute-start.2 = (f32[16,128]{1,0:T(8,128)S(1)}, f32[16,128]{1,0:T(8,128)S(1)}, u32[]{:S(2)}, u32[]{:S(2)}) collective-permute-start(f32[16,128]{1,0:T(8,128)S(1)} %get-tuple-element.22), channel_id=1, source_target_pairs={{0,96},{32,0},{64,32},{96,64},{1,97},{33,1},{65,33},{97,65},{2,98}... | collective-permute-start | bytes 24584 | tf_op jit(solution)/shard_map/ppermute | solution.py:318

commit v3 on v2

--- a/solution.py
+++ b/solution.py
@@ -8,10 +8,10 @@
 AREA = ("region", "column")
 DEPTH, ROWS, LANES = 8, 16, 128
 HALF = LANES // 2
-PACK = 32
-BACK = 8
-
-STEP, MIXED, WELL, SOURCE = 0, 9, 18, 27
+PACK = 26
+BACK = 4
+
+STEP, MIXED, WELL, SOURCE = 0, 9, 18, 23
 
 
 def mat(a, b):
@@ -135,9 +135,8 @@
         for e in range(9):
             put(send, h, STEP + e, down[e], state[e])
             put(send, h, MIXED + e, well_cross[e], cross[e])
-            put(send, h, WELL + e, zero, well_state[e])
-        for place in range(30, PACK):
-            put(send, h, place, zero, zero)
+        for e in range(5):
+            put(send, h, WELL + e, well_state[e], well_state[5 + e] if e < 4 else zero)
 
 
 def trial_kernel(
@@ -240,7 +239,9 @@
     up_base = add(source, vec(mixed, [pltpu.roll(x, HALF, 1) for x in down]))
     up = chain(up_base, reversed(range(peers)))
     both = [jnp.where(is_left, a, b) for a, b in zip(down, up)]
-    coef = [jnp.where(is_left, a, b) for a, b in zip(mixed, take(WELL, 9))]
+    packed = take(WELL, 5)
+    well_state = [pltpu.roll(x, HALF, 1) for x in packed] + packed[:4]
+    coef = [jnp.where(is_left, a, b) for a, b in zip(mixed, well_state)]
     parts = vec(coef, both)
     mine = well_sums[0:1, :]
     one = iota((1, LANES), 1)
@@ -355,7 +356,7 @@
         [pltpu.VMEM((3, DEPTH, 8, LANES), jnp.float32)],
         aliases={13: 0},
     )(x_in, right_in, left_in, below_in, above_in, rhs, guess, diag, couple, pivot, lower, upper, well, send)
-    got = exchanged(send.reshape(peers, PACK, LANES), "layer").reshape(peers * PACK, LANES)
+    got = exchanged(send.reshape(peers, PACK, 1, LANES), "layer").reshape(peers * PACK, LANES)
     back = call(
         lambda *refs: chain_kernel(peers, *refs),
         f32(peers * BACK, LANES),
@@ -366,7 +367,7 @@
             pltpu.VMEM((3, peers, LANES), jnp.float32),
         ],
     )(got, well_sums)
-    got = exchanged(back.reshape(peers, BACK, LANES), "layer").reshape(peers * BACK, LANES)
+    got = exchanged(back.reshape(peers, BACK, 1, LANES), "layer").reshape(peers * BACK, LANES)
     solved, sums = call(
         lambda *refs: solved_kernel(areas, peers, *refs), (three, f32(8 * areas, LANES)), [VMEM] * 4
     )(got, cross, state, trial)

time: 65.6 us -> 62.6 us (0.954)
  blocking collectives: 47 us -> 44.4 us
    all_to_all x3, blocking collectives: 47 us -> 44.4 us  [exchanged(): return lax.all_to_all(value, axes, split_axis=0, concat_axis=0, tiled=True)]
where the time goes in v3:
time: 62.6 us; the launch traced here: 62.4 us
  blocking collectives  44.4 us (71%)
  starting transfers between devices  12.7 us (20%)
  Pallas kernels  4.02 us (6%)
  local copies, waits for them, and re-layouts  1.12 us (2%)
    all_to_all x3, blocking collectives, exchanged(): return lax.all_to_all(value, axes, split_axis=0, concat_axis=0, tiled=True)  44.4 us
    ppermute x5, starting transfers between devices, moved(): lax.ppermute(value, axis, [(i, (i + by) % count) for i in range(count)])  12.7 us
    pallas_call x1, Pallas kernels, local(): call(lambda *refs: maps_kernel(areas, tiles.shape[0], counts.shape[0], *r...  1.83 us
  transfers between devices with their start and end apart: 5, of which 0 were waited for; matrix products, arithmetic and copies ran while one was open for 0% of the time, Pallas kernels for 3%

profile of v3, /device:TPU:1, one launch (start us, length us, event | category | flops | bytes accessed | tf_op | source)
XLA Modules:
  0.0 62.4 jit_solution(1632716760104550101)
XLA Ops:
  0.0 0.0 copy-start
  0.0 0.0 copy-start.3
  0.0 0.0 copy-start.2
  0.0 0.0 copy-start.1
  0.0 0.0 copy-start.5
  0.0 1.1 %copy-done.5 = f32[3,8,16,128]{3,2,1,0:T(8,128)S(1)} copy-done((f32[3,8,16,128]{3,2,1,0:T(8,128)S(1)}, f32[3,8,16,128]{3,2,1,0:T(8,128)}, u32[]{:S(2)}) %copy-start.5) | copy-done | bytes 196632
  1.1 0.2 shard_map.109
  1.3 0.0 copy-start.9
  1.3 2.2 %collective-permute-start.3 = (f32[3,16,128]{2,1,0:T(8,128)S(1)}, f32[3,16,128]{2,1,0:T(8,128)S(1)}, u32[]{:S(2)}, u32[]{:S(2)}) collective-permute-start(f32[3,16,128]{2,1,0:T(8,128)S(1)} %get-tuple-element.23), channel_id=1, source_target_pairs={{0,1},{1,2},{2,3},{3,4},{4,5},{5,6},{6,7},{7,8},{8,9},{9,10},{10,1... | collective-permute-start | bytes 73736 | tf_op jit(solution)/shard_map/ppermute | solution.py:319
  3.5 6.8 %collective-permute-start.4 = (f32[3,16,128]{2,1,0:T(8,128)S(1)}, f32[3,16,128]{2,1,0:T(8,128)S(1)}, u32[]{:S(2)}, u32[]{:S(2)}) collective-permute-start(f32[3,16,128]{2,1,0:T(8,128)S(1)} %get-tuple-element.24), channel_id=1, source_target_pairs={{0,31},{1,0},{2,1},{3,2},{4,3},{5,4},{6,5},{7,6},{8,7},{9,8},{10,9... | collective-permute-start | bytes 73736 | tf_op jit(solution)/shard_map/ppermute | solution.py:319
  10.3 1.0 %collective-permute-start = (f32[24,128]{1,0:T(8,128)S(1)}, f32[24,128]{1,0:T(8,128)S(1)}, u32[]{:S(2)}, u32[]{:S(2)}) collective-permute-start(f32[24,128]{1,0:T(8,128)S(1)} %get-tuple-element.20), channel_id=1, source_target_pairs={{0,128},{128,0},{1,129},{129,1},{2,130},{130,2},{3,131},{131,3},{4... | collective-permute-start | bytes 36872 | tf_op jit(solution)/shard_map/ppermute | solution.py:319
  11.3 0.0 copy-start.10
  11.3 0.0 copy-start.11
  11.3 1.2 %collective-permute-start.1 = (f32[16,128]{1,0:T(8,128)S(1)}, f32[16,128]{1,0:T(8,128)S(1)}, u32[]{:S(2)}, u32[]{:S(2)}) collective-permute-start(f32[16,128]{1,0:T(8,128)S(1)} %get-tuple-element.21), channel_id=1, source_target_pairs={{0,32},{32,64},{64,96},{96,0},{1,33},{33,65},{65,97},{97,1},{2,34}... | collective-permute-start | bytes 24584 | tf_op jit(solution)/shard_map/ppermute | solution.py:319
  12.5 0.0 copy-start.4
  12.5 0.0 copy-start.6
  12.5 0.0 copy-start.7
  12.5 0.0 copy-start.8
  12.5 1.5 %collective-permute-start.2 = (f32[16,128]{1,0:T(8,128)S(1)}, f32[16,128]{1,0:T(8,128)S(1)}, u32[]{:S(2)}, u32[]{:S(2)}) collective-permute-start(f32[16,128]{1,0:T(8,128)S(1)} %get-tuple-element.22), channel_id=1, source_target_pairs={{0,96},{32,0},{64,32},{96,64},{1,97},{33,1},{65,33},{97,65},{2,98}... | collective-permute-start | bytes 24584 | tf_op jit(solution)/shard_map/ppermute | solution.py:319
  14.0 0.0 copy-done
  14.0 0.0 copy-done.3
  14.0 0.0 copy-done.2
  14.0 0.0 copy-done.1
  14.0 0.0 copy-done.9
  14.0 0.0 copy-done.10
  14.1 0.0 copy-done.11
  14.1 1.8 %shard_map.110 = (f32[832,128]{1,0:T(8,128)S(1)}, f32[9,8,16,128]{3,2,1,0:T(8,128)S(1)}, f32[9,8,16,128]{3,2,1,0:T(8,128)S(1)}, f32[8,16,128]{2,1,0:T(8,128)S(1)}, f32[9,16,128]{2,1,0:T(8,128)S(1)}) custom-call(s32[32]{0:T(128)S(1)} %copy-done.10, s32[16]{0:T(128)S(1)} %copy-done.11, f32[9,16]{1,0:T(8,128)S(1)} %copy-done.9, ...), custom_call_target="tpu_custom_call" | custom-call | flops 20000000 | bytes 8000000 | tf_op jit(solution)/shard_map/pallas_call | solution.py:345
  15.9 0.0 collective-permute-done.1.right_in
  15.9 0.0 collective-permute-done.2.left_in
  15.9 0.0 collective-permute-done.x_in
  15.9 0.0 collective-permute-done.3.below_in
  15.9 0.0 collective-permute-done.4.above_in
  15.9 0.0 copy-done.4
  15.9 0.0 copy-done.6
  16.0 0.0 copy-done.7
  16.0 0.0 copy-done.8
  16.0 0.5 shard_map.111
  16.5 19.6 %all_to_all.15 = f32[32,26,1,128]{3,2,1,0:T(1,128)S(1)} all-to-all(f32[32,26,1,128]{3,2,1,0:T(1,128)S(1)} %bitcast.8), channel_id=1, replica_groups=mesh['region'=2,'column'=4,'layer'=32] {'layer'}, dimensions={0} | all-to-all | bytes 851968 | tf_op jit(solution)/shard_map/all_to_all | solution.py:323
  36.1 0.5 shard_map.112
  36.6 13.9 %all_to_all.16 = f32[32,4,1,128]{3,1,2,0:T(4,128)S(1)} all-to-all(f32[32,4,1,128]{3,1,2,0:T(4,128)S(1)} %bitcast.11), channel_id=1, replica_groups=mesh['region'=2,'column'=4,'layer'=32] {'layer'}, dimensions={0} | all-to-all | bytes 131072 | tf_op jit(solution)/shard_map/all_to_all | solution.py:323
  50.5 0.2 shard_map.113
  50.7 10.9 %all_to_all.17 = f32[8,8,128]{2,1,0:T(8,128)S(1)} all-to-all(f32[8,8,128]{2,1,0:T(8,128)S(1)} %bitcast.13), channel_id=1, replica_groups=mesh['region'=2,'column'=4,'layer'=32] {'region','column'}, dimensions={0} | all-to-all | bytes 65536 | tf_op jit(solution)/shard_map/all_to_all | solution.py:323
  61.6 0.8 %shard_map.114 = f32[3,8,16,128]{3,2,1,0:T(8,128)} custom-call(f32[64,128]{1,0:T(8,128)S(1)} %bitcast.12, f32[8,16,128]{2,1,0:T(8,128)S(1)} %get-tuple-element.32.refs_1_, f32[9,16,128]{2,1,0:T(8,128)S(1)} %get-tuple-element.33.refs_2_, f32[3,8,16,128]{3,2,1,0:T(8,128)S(1)} %get-tuple-element.34.refs_3_, f32[9,8,16,128]{3,2,1,0:T(8,128)S(1)} %copy-done), custom_call_target="tpu_custom_call" | custom-call | tf_op jit(solution)/shard_map/pallas_call | solution.py:375
Async XLA Ops:
  0.0 14.0 %copy-start = (f32[9,8,16,128]{3,2,1,0:T(8,128)S(1)}, f32[9,8,16,128]{3,2,1,0:T(8,128)}, u32[]{:S(2)}) copy-start(f32[9,8,16,128]{3,2,1,0:T(8,128)} %refs_4_.3) | copy-start | bytes 1769476
  0.0 14.0 %copy-start.3 = (f32[9,8,16,128]{3,2,1,0:T(8,128)S(1)}, f32[9,8,16,128]{3,2,1,0:T(8,128)}, u32[]{:S(2)}) copy-start(f32[9,8,16,128]{3,2,1,0:T(8,128)} %upper.1) | copy-start | bytes 1769476
  0.0 14.0 %copy-start.2 = (f32[9,8,16,128]{3,2,1,0:T(8,128)S(1)}, f32[9,8,16,128]{3,2,1,0:T(8,128)}, u32[]{:S(2)}) copy-start(f32[9,8,16,128]{3,2,1,0:T(8,128)} %lower.1) | copy-start | bytes 1769476
  0.0 14.0 %copy-start.1 = (f32[9,8,16,128]{3,2,1,0:T(8,128)S(1)}, f32[9,8,16,128]{3,2,1,0:T(8,128)}, u32[]{:S(2)}) copy-start(f32[9,8,16,128]{3,2,1,0:T(8,128)} %pivot.1) | copy-start | bytes 1769476
  0.0 1.1 %copy-start.5 = (f32[3,8,16,128]{3,2,1,0:T(8,128)S(1)}, f32[3,8,16,128]{3,2,1,0:T(8,128)}, u32[]{:S(2)}) copy-start(f32[3,8,16,128]{3,2,1,0:T(8,128)} %guess.3) | copy-start | bytes 589828
  1.3 12.8 %copy-start.9 = (f32[9,16]{1,0:T(8,128)S(1)}, f32[9,16]{1,0:T(8,128)}, u32[]{:S(2)}) copy-start(f32[9,16]{1,0:T(8,128)} %refs_2_.1) | copy-start | bytes 1732
  1.3 14.6 %collective-permute-start.3 = (f32[3,16,128]{2,1,0:T(8,128)S(1)}, f32[3,16,128]{2,1,0:T(8,128)S(1)}, u32[]{:S(2)}, u32[]{:S(2)}) collective-permute-start(f32[3,16,128]{2,1,0:T(8,128)S(1)} %get-tuple-element.23), channel_id=1, source_target_pairs={{0,1},{1,2},{2,3},{3,4},{4,5},{5,6},{6,7},{7,8},{8,9},{9,10},{10,1... | collective-permute-start | bytes 73736 | tf_op jit(solution)/shard_map/ppermute | solution.py:319
  3.5 12.5 %collective-permute-start.4 = (f32[3,16,128]{2,1,0:T(8,128)S(1)}, f32[3,16,128]{2,1,0:T(8,128)S(1)}, u32[]{:S(2)}, u32[]{:S(2)}) collective-permute-start(f32[3,16,128]{2,1,0:T(8,128)S(1)} %get-tuple-element.24), channel_id=1, source_target_pairs={{0,31},{1,0},{2,1},{3,2},{4,3},{5,4},{6,5},{7,6},{8,7},{9,8},{10,9... | collective-permute-start | bytes 73736 | tf_op jit(solution)/shard_map/ppermute | solution.py:319
  10.3 5.6 %collective-permute-start = (f32[24,128]{1,0:T(8,128)S(1)}, f32[24,128]{1,0:T(8,128)S(1)}, u32[]{:S(2)}, u32[]{:S(2)}) collective-permute-start(f32[24,128]{1,0:T(8,128)S(1)} %get-tuple-element.20), channel_id=1, source_target_pairs={{0,128},{128,0},{1,129},{129,1},{2,130},{130,2},{3,131},{131,3},{4... | collective-permute-start | bytes 36872 | tf_op jit(solution)/shard_map/ppermute | solution.py:319
  11.3 2.8 %copy-start.10 = (s32[32]{0:T(128)S(1)}, s32[32]{0:T(128)}, u32[]{:S(2)}) copy-start(s32[32]{0:T(128)} %refs_0_.1) | copy-start | bytes 388
  11.3 2.8 %copy-start.11 = (s32[16]{0:T(128)S(1)}, s32[16]{0:T(128)}, u32[]{:S(2)}) copy-start(s32[16]{0:T(128)} %refs_1_.1) | copy-start | bytes 196
  11.3 4.6 %collective-permute-start.1 = (f32[16,128]{1,0:T(8,128)S(1)}, f32[16,128]{1,0:T(8,128)S(1)}, u32[]{:S(2)}, u32[]{:S(2)}) collective-permute-start(f32[16,128]{1,0:T(8,128)S(1)} %get-tuple-element.21), channel_id=1, source_target_pairs={{0,32},{32,64},{64,96},{96,0},{1,33},{33,65},{65,97},{97,1},{2,34}... | collective-permute-start | bytes 24584 | tf_op jit(solution)/shard_map/ppermute | solution.py:319
  12.5 3.5 %copy-start.4 = (f32[9,8,16,128]{3,2,1,0:T(8,128)S(1)}, f32[9,8,16,128]{3,2,1,0:T(8,128)}, u32[]{:S(2)}) copy-start(f32[9,8,16,128]{3,2,1,0:T(8,128)} %diag.1) | copy-start | bytes 1769476
  12.5 3.5 %copy-start.6 = (f32[3,8,16,128]{3,2,1,0:T(8,128)S(1)}, f32[3,8,16,128]{3,2,1,0:T(8,128)}, u32[]{:S(2)}) copy-start(f32[3,8,16,128]{3,2,1,0:T(8,128)} %guess.3) | copy-start | bytes 589828
  12.5 3.5 %copy-start.7 = (f32[3,8,16,128]{3,2,1,0:T(8,128)S(1)}, f32[3,8,16,128]{3,2,1,0:T(8,128)}, u32[]{:S(2)}) copy-start(f32[3,8,16,128]{3,2,1,0:T(8,128)} %rhs.1) | copy-start | bytes 589828
  12.5 3.5 %copy-start.8 = (f32[3,8,16,128]{3,2,1,0:T(8,128)S(1)}, f32[3,8,16,128]{3,2,1,0:T(8,128)}, u32[]{:S(2)}) copy-start(f32[3,8,16,128]{3,2,1,0:T(8,128)} %couple.1) | copy-start | bytes 589828
  12.5 3.4 %collective-permute-start.2 = (f32[16,128]{1,0:T(8,128)S(1)}, f32[16,128]{1,0:T(8,128)S(1)}, u32[]{:S(2)}, u32[]{:S(2)}) collective-permute-start(f32[16,128]{1,0:T(8,128)S(1)} %get-tuple-element.22), channel_id=1, source_target_pairs={{0,96},{32,0},{64,32},{96,64},{1,97},{33,1},{65,33},{97,65},{2,98}... | collective-permute-start | bytes 24584 | tf_op jit(solution)/shard_map/ppermute | solution.py:319

commit v4 on v3

--- a/solution.py
+++ b/solution.py
@@ -8,10 +8,12 @@
 AREA = ("region", "column")
 DEPTH, ROWS, LANES = 8, 16, 128
 HALF = LANES // 2
-PACK = 26
+BLOCK = 16
+GROUPS, ACROSS = 4, 8
+PACK = 20
 BACK = 4
 
-STEP, MIXED, WELL, SOURCE = 0, 9, 18, 23
+TRIAL, WELLS = 3, 4
 
 
 def mat(a, b):
@@ -62,15 +64,61 @@
     left_out[...] = left
 
 
-def put(send, h, place, left, right):
-    is_left = iota((8, LANES), 1) < HALF
-    low_cols = jnp.where(is_left, left, pltpu.roll(right, HALF, 1))
-    high_cols = jnp.where(is_left, pltpu.roll(left, HALF, 1), right)
-    send[pl.ds(16 * h * PACK + place, 8, 2 * PACK), :] = low_cols
-    send[pl.ds((16 * h + 1) * PACK + place, 8, 2 * PACK), :] = high_cols
-
-
-def well_masks(areas, nperf, nwell, tiles, counts, inverse, same_out, block_out):
+def swapped(parts, steps):
+    parts = list(parts)
+    for step in steps:
+        block = iota(parts[0].shape, 1) // BLOCK
+        low = (block & step) == 0
+        for i in range(len(parts)):
+            if i & step == 0:
+                a, b = parts[i], parts[i + step]
+                parts[i] = jnp.where(low, a, pltpu.roll(b, BLOCK * step, 1))
+                parts[i + step] = jnp.where(low, pltpu.roll(a, LANES - BLOCK * step, 1), b)
+    return parts
+
+
+def placed(low, high, index):
+    inner = index & 7
+    return jnp.where(
+        index < 8,
+        jnp.take_along_axis(low, inner, axis=0, mode="promise_in_bounds"),
+        jnp.take_along_axis(high, inner, axis=0, mode="promise_in_bounds"),
+    )
+
+
+def put(send, h, m, parts):
+    for e, part in enumerate(swapped(parts, (1, 2, 4))):
+        for half in range(2):
+            at = (ACROSS * (2 * h + half) + e) * PACK + 4 * m
+            send[at : at + 4, :] = part[4 * half : 4 * half + 4, :]
+
+
+def lane_sum(x):
+    return jnp.sum(x, axis=1, keepdims=True)
+
+
+def row_order(flag_lane, flag_row, order_out, place_out, group_out):
+    row = iota((ROWS, LANES), 0)
+    lane = iota((ROWS, LANES), 1)
+    inner = lane % ROWS
+
+    def place_of(flag, rank, number):
+        free = number - rank
+        return jnp.where(flag > 0.0, 4 * rank, free + 1 + ((free * 11) >> 5))
+
+    rank_row = lane_sum(jnp.where((lane < ROWS) & (lane < row), flag_lane, 0.0))
+    rank_lane = jnp.sum(jnp.where(row < inner, flag_row, 0.0), axis=0, keepdims=True)
+    rank_row = jnp.broadcast_to(rank_row, (ROWS, LANES)).astype(jnp.int32)
+    rank_lane = jnp.broadcast_to(rank_lane, (ROWS, LANES)).astype(jnp.int32)
+    place_out[...] = place_of(flag_row, rank_row, row)
+    at_lane = place_of(flag_lane, rank_lane, inner)
+    number = jnp.where(lane < ROWS, lane, 0).astype(jnp.float32)
+    for out, wanted in ((order_out, row), (group_out, row & 12)):
+        found = lane_sum(jnp.where(at_lane == wanted, number, 0.0))
+        out[...] = jnp.broadcast_to(found, (ROWS, LANES)).astype(jnp.int32)
+
+
+def well_masks(areas, nperf, nwell, tiles, counts, inverse, same_out, block_out, order_out, place_out, group_out):
     me = lax.axis_index("region") * lax.axis_size("column") + lax.axis_index("column")
     tile_all = iota((areas, LANES), 0) * ROWS + iota((areas, LANES), 1) % ROWS
     tile_own = me * ROWS + iota((ROWS, LANES), 0)
@@ -79,6 +127,10 @@
     for p in range(nperf):
         place_all = jnp.where(tile_all == tiles[p], p, place_all)
         place_own = jnp.where(tile_own == tiles[p], p, place_own)
+    own_area = (iota((areas, LANES), 0) == me) & (place_all >= 0)
+    flag_lane = jnp.sum(jnp.where(own_area, 1.0, 0.0), axis=0, keepdims=True)
+    flag_lane = jnp.broadcast_to(flag_lane, (ROWS, LANES))
+    row_order(flag_lane, jnp.where(place_own >= 0, 1.0, 0.0), order_out, place_out, group_out)
     well_all = jnp.where(place_all < 0, -1, 0)
     well_own = jnp.where(place_own < 0, -2, 0)
     end = 0
@@ -98,9 +150,11 @@
 def maps_kernel(
     areas, nperf, nwell,
     tiles, counts, inverse, pivot, lower, upper, well,
-    send, cross_out, state_out, same_out, block_out, states,
+    send, cross_out, state_out, same_out, block_out, order, place_out, rest, states, maps, group,
 ):
-    well_masks(areas, nperf, nwell, tiles, counts, inverse, same_out, block_out)
+    well_masks(
+        areas, nperf, nwell, tiles, counts, inverse, same_out, block_out, order, place_out, group
+    )
     top = DEPTH - 1
     for h in range(2):
         at = slice(8 * h, 8 * h + 8)
@@ -133,15 +187,37 @@
                 state_out[c, k, at, :] = state[c]
         zero = jnp.zeros((8, LANES), jnp.float32)
         for e in range(9):
-            put(send, h, STEP + e, down[e], state[e])
-            put(send, h, MIXED + e, well_cross[e], cross[e])
-        for e in range(5):
-            put(send, h, WELL + e, well_state[e], well_state[5 + e] if e < 4 else zero)
+            maps[e, at, :] = down[e]
+            maps[9 + e, at, :] = state[e]
+            maps[18 + e, at, :] = cross[e]
+            maps[27 + e, at, :] = well_cross[e]
+            maps[36 + e, at, :] = well_state[e]
+    for h in range(2):
+        at = slice(8 * h, 8 * h + 8)
+
+        def take(e, index):
+            return placed(maps[e, 0:8, :], maps[e, 8:16, :], index[at, :])
+
+        down = [take(e, order) for e in range(9)]
+        state = [take(9 + e, order) for e in range(9)]
+        cross = [take(18 + e, order) for e in range(9)]
+        wells = [take(27 + e, group) for e in range(18)]
+        put(send, h, 0, down[:4] + state[:4])
+        put(send, h, 1, down[4:8] + state[4:8])
+        put(send, h, 2, [down[8], cross[0], cross[2], cross[4], state[8], cross[1], cross[3], cross[5]])
+        rest[0, at, :] = cross[6]
+        rest[1, at, :] = cross[7]
+        j = iota((8, LANES), 0) & 3
+        behind = []
+        for b in range(7):
+            value = jnp.where(j == 0, wells[b], wells[7 + b])
+            behind.append(value if b > 3 else jnp.where(j == 2, wells[14 + b], value))
+        put(send, h, WELLS, [cross[8]] + behind)
 
 
 def trial_kernel(
-    x_in, right_in, left_in, below_in, above_in, rhs, guess, diag, couple, pivot, lower, upper, well, sent,
-    send, trial_out, well_out, forward,
+    x_in, right_in, left_in, below_in, above_in, rhs, guess, diag, couple, pivot, lower, upper, well, order, rest, sent,
+    send, trial_out, well_out, forward, ends,
 ):
     region = lax.axis_index("region")
     column = lax.axis_index("column")
@@ -207,18 +283,26 @@
             for c in range(3):
                 trial_out[c, k, at, :] = s[c]
         for c in range(3):
-            put(send, h, SOURCE + c, f[c], s[c])
+            ends[c, at, :] = f[c]
+            ends[3 + c, at, :] = s[c]
             total = jnp.sum(well_const[c], axis=1, keepdims=True)
             well_sums = well_sums + jnp.where(lane == c * ROWS + 8 * h + row, total, 0.0)
+    for h in range(2):
+        at = slice(8 * h, 8 * h + 8)
+        source = [placed(ends[c, 0:8, :], ends[c, 8:16, :], order[at, :]) for c in range(6)]
+        put(send, h, TRIAL, source[:3] + [rest[0, at, :]] + source[3:] + [rest[1, at, :]])
     well_out[...] = jnp.broadcast_to(jnp.sum(well_sums, axis=0, keepdims=True), (8, LANES))
 
 
-def chain_kernel(peers, got, well_sums, send, step_ref, base_ref, inflow_ref):
+def chain_kernel(peers, got, well_sums, order_in, send, step_ref, base_ref, inflow_ref):
     layer = lax.axis_index("layer")
     is_left = iota((peers, LANES), 1) < HALF
 
-    def take(place, count):
-        return [got[pl.ds(place + e, peers, PACK), :] for e in range(count)]
+    def rows(m):
+        return [got[pl.ds(4 * m + j, peers, PACK), :] for j in range(4)]
+
+    def turn(x):
+        return pltpu.roll(x, HALF, 1)
 
     def chain(base, order):
         for c in range(3):
@@ -231,37 +315,58 @@
             x = add([base_ref[c, at, :] for c in range(3)], vec([step_ref[e, at, :] for e in range(9)], x))
         return [inflow_ref[c] for c in range(3)]
 
-    for e, step in enumerate(take(STEP, 9)):
-        step_ref[e] = step
-    source = take(SOURCE, 3)
-    mixed = take(MIXED, 9)
+    sets = [swapped(rows(m), (1, 2)) for m in range(4)]
+    for e in range(9):
+        step_ref[e] = sets[e // 4][e % 4]
+    source = sets[TRIAL][:3]
+    last = rows(WELLS)
+    mixed = []
+    for pair in sets[2][1:] + [sets[TRIAL][3], swapped(last, (1, 2))[0]]:
+        mixed += [turn(pair), pair]
     down = chain(source, range(peers))
-    up_base = add(source, vec(mixed, [pltpu.roll(x, HALF, 1) for x in down]))
+    up_base = add(source, vec(mixed[:9], [turn(x) for x in down]))
     up = chain(up_base, reversed(range(peers)))
     both = [jnp.where(is_left, a, b) for a, b in zip(down, up)]
-    packed = take(WELL, 5)
-    well_state = [pltpu.roll(x, HALF, 1) for x in packed] + packed[:4]
-    coef = [jnp.where(is_left, a, b) for a, b in zip(mixed, well_state)]
-    parts = vec(coef, both)
+    block = iota((peers, LANES), 1) // BLOCK
+    parts = []
+    for j in range(3):
+        factor = jnp.zeros((peers, LANES), jnp.float32)
+        for b in range(7):
+            w = 7 * j + b
+            if w < 18:
+                shift = BLOCK * (b + 1 - (0 if w < 9 else 4)) % LANES
+                value = both[w % 3]
+                factor = jnp.where(block == b + 1, pltpu.roll(value, shift, 1) if shift else value, factor)
+        parts.append(jnp.sum(last[j] * factor, axis=0, keepdims=True))
     mine = well_sums[0:1, :]
     one = iota((1, LANES), 1)
+    leader = order_in[pl.ds(4 * (layer // ACROSS), 1), :]
     for c in range(3):
-        total = jnp.sum(jnp.sum(parts[c], axis=0, keepdims=True), axis=1, keepdims=True)
-        mine = mine + jnp.where(one == c * ROWS + layer // 2, total, 0.0)
+        total = jnp.zeros((1, LANES), jnp.float32)
+        for j in range(3):
+            for b in range(7):
+                w = 7 * j + b
+                if w < 18 and (w % 9) // 3 == c:
+                    total = total + jnp.where(one // BLOCK == b + 1, parts[j], 0.0)
+        mine = mine + jnp.where(one == c * ROWS + leader, lane_sum(total), 0.0)
         send[pl.ds(c, peers, BACK), :] = both[c]
     send[pl.ds(3, peers, BACK), :] = jnp.broadcast_to(mine, (peers, LANES))
-    for place in range(4, BACK):
-        send[pl.ds(place, peers, BACK), :] = jnp.zeros((peers, LANES), jnp.float32)
-
-
-def solved_kernel(areas, peers, got, cross, state, trial, solved, sums):
-    is_left = iota((ROWS, LANES), 1) < HALF
-    u, w = [], []
+
+
+def solved_kernel(areas, peers, got, cross, state, trial, place_in, solved, sums, inflow):
     for c in range(3):
-        low_cols = got[pl.ds(c, ROWS, 2 * BACK), :]
-        high_cols = got[pl.ds(BACK + c, ROWS, 2 * BACK), :]
-        u.append(jnp.where(is_left, low_cols, pltpu.roll(high_cols, HALF, 1)))
-        w.append(jnp.where(is_left, pltpu.roll(low_cols, HALF, 1), high_cols))
+        parts = [got[pl.ds(e * BACK + c, GROUPS, ACROSS * BACK), :] for e in range(ACROSS)]
+        for i, part in enumerate(swapped(parts, (1, 2, 4))):
+            inflow[3 * (i // 4) + c, pl.ds(i % 4, GROUPS, 4), :] = part
+
+    def rows_of(c):
+        low, high = inflow[c, 0:8, :], inflow[c, 8:16, :]
+        return jnp.concatenate(
+            [placed(low, high, place_in[0:8, :]), placed(low, high, place_in[8:16, :])], axis=0
+        )
+
+    u = [rows_of(c) for c in range(3)]
+    w = [rows_of(3 + c) for c in range(3)]
     total = jnp.sum(got[pl.ds(3, peers, BACK), :], axis=0, keepdims=True)
     sums[...] = jnp.broadcast_to(total, (8 * areas, LANES))
     for k in range(DEPTH):
@@ -342,35 +447,44 @@
     left_in = moved(left_face, "column", -1)
     x_in = moved(x_face, "region", 1)
     nine, three = f32(9, *cells), f32(3, *cells)
-    send, cross, state, same, block = call(
+    index = jax.ShapeDtypeStruct((ROWS, LANES), jnp.int32)
+    send, cross, state, same, block, order, place, rest = call(
         lambda *refs: maps_kernel(areas, tiles.shape[0], counts.shape[0], *refs),
-        (f32(peers * PACK, LANES), nine, nine, f32(areas, ROWS, LANES), f32(9, ROWS, LANES)),
+        (
+            f32(peers * PACK, LANES), nine, nine, f32(areas, ROWS, LANES), f32(9, ROWS, LANES),
+            index, index, f32(2, ROWS, LANES),
+        ),
         [SMEM] * 3 + [VMEM] * 4,
-        [pltpu.VMEM((9, DEPTH, 8, LANES), jnp.float32)],
+        [
+            pltpu.VMEM((9, DEPTH, 8, LANES), jnp.float32),
+            pltpu.VMEM((45, ROWS, LANES), jnp.float32),
+            pltpu.VMEM((ROWS, LANES), jnp.int32),
+        ],
         cost=LONG,
     )(tiles, counts, inverse, pivot, lower, upper, well)
     send, trial, well_sums = call(
         trial_kernel,
         (f32(peers * PACK, LANES), three, f32(8, LANES)),
-        [VMEM] * 14,
-        [pltpu.VMEM((3, DEPTH, 8, LANES), jnp.float32)],
-        aliases={13: 0},
-    )(x_in, right_in, left_in, below_in, above_in, rhs, guess, diag, couple, pivot, lower, upper, well, send)
+        [VMEM] * 16,
+        [pltpu.VMEM((3, DEPTH, 8, LANES), jnp.float32), pltpu.VMEM((6, ROWS, LANES), jnp.float32)],
+        aliases={15: 0},
+    )(x_in, right_in, left_in, below_in, above_in, rhs, guess, diag, couple, pivot, lower, upper, well, order, rest, send)
     got = exchanged(send.reshape(peers, PACK, 1, LANES), "layer").reshape(peers * PACK, LANES)
     back = call(
         lambda *refs: chain_kernel(peers, *refs),
         f32(peers * BACK, LANES),
-        [VMEM] * 2,
+        [VMEM] * 3,
         [
             pltpu.VMEM((9, peers, LANES), jnp.float32),
             pltpu.VMEM((3, peers, LANES), jnp.float32),
             pltpu.VMEM((3, peers, LANES), jnp.float32),
         ],
-    )(got, well_sums)
+    )(got, well_sums, order)
     got = exchanged(back.reshape(peers, BACK, 1, LANES), "layer").reshape(peers * BACK, LANES)
     solved, sums = call(
-        lambda *refs: solved_kernel(areas, peers, *refs), (three, f32(8 * areas, LANES)), [VMEM] * 4
-    )(got, cross, state, trial)
+        lambda *refs: solved_kernel(areas, peers, *refs), (three, f32(8 * areas, LANES)), [VMEM] * 5,
+        [pltpu.VMEM((6, ROWS, LANES), jnp.float32)],
+    )(got, cross, state, trial, place)
     sums = exchanged(sums.reshape(areas, 8, LANES), AREA).reshape(8 * areas, LANES)
     return call(lambda *refs: wells_kernel(areas, *refs), three, [VMEM] * 5)(
         sums, same, block, solved, well

time: 62.6 us -> 61.3 us (0.979)
  blocking collectives: 44.4 us -> 42 us
  Pallas kernels: 4.02 us -> 5.08 us
    all_to_all x3, blocking collectives: 44.4 us -> 42 us  [exchanged(): return lax.all_to_all(value, axes, split_axis=0, concat_axis=0, tiled=True)]
  transfers between devices with their start and end apart: 5 -> 5, of which waited for: 0 -> 0; matrix products, arithmetic and copies ran while one was open for 0% -> 0% of each run, Pallas kernels for 3% -> 4%
where the time goes in v4:
time: 61.3 us; the launch traced here: 61.1 us
  blocking collectives  42 us (69%)
  starting transfers between devices  12.7 us (21%)
  Pallas kernels  5.08 us (8%)
  local copies, waits for them, and re-layouts  1.12 us (2%)
    all_to_all x3, blocking collectives, exchanged(): return lax.all_to_all(value, axes, split_axis=0, concat_axis=0, tiled=True)  42 us
    ppermute x5, starting transfers between devices, moved(): lax.ppermute(value, axis, [(i, (i + by) % count) for i in range(count)])  12.7 us
    pallas_call x1, Pallas kernels, local(): call(lambda *refs: maps_kernel(areas, tiles.shape[0], counts.shape[0], *r...  2.18 us
  transfers between devices with their start and end apart: 5, of which 0 were waited for; matrix products, arithmetic and copies ran while one was open for 0% of the time, Pallas kernels for 4%

profile of v4, /device:TPU:1, one launch (start us, length us, event | category | flops | bytes accessed | tf_op | source)
XLA Modules:
  0.0 61.1 jit_solution(257419177486789839)
XLA Ops:
  0.0 0.0 copy-start
  0.0 0.0 copy-start.3
  0.0 0.0 copy-start.2
  0.0 0.0 copy-start.1
  0.0 0.0 copy-start.5
  0.0 1.1 %copy-done.5 = f32[3,8,16,128]{3,2,1,0:T(8,128)S(1)} copy-done((f32[3,8,16,128]{3,2,1,0:T(8,128)S(1)}, f32[3,8,16,128]{3,2,1,0:T(8,128)}, u32[]{:S(2)}) %copy-start.5) | copy-done | bytes 196632
  1.1 0.2 shard_map.109
  1.3 0.0 copy-start.9
  1.3 2.2 %collective-permute-start.3 = (f32[3,16,128]{2,1,0:T(8,128)S(1)}, f32[3,16,128]{2,1,0:T(8,128)S(1)}, u32[]{:S(2)}, u32[]{:S(2)}) collective-permute-start(f32[3,16,128]{2,1,0:T(8,128)S(1)} %get-tuple-element.26), channel_id=1, source_target_pairs={{0,1},{1,2},{2,3},{3,4},{4,5},{5,6},{6,7},{7,8},{8,9},{9,10},{10,1... | collective-permute-start | bytes 73736 | tf_op jit(solution)/shard_map/ppermute | solution.py:424
  3.5 6.8 %collective-permute-start.4 = (f32[3,16,128]{2,1,0:T(8,128)S(1)}, f32[3,16,128]{2,1,0:T(8,128)S(1)}, u32[]{:S(2)}, u32[]{:S(2)}) collective-permute-start(f32[3,16,128]{2,1,0:T(8,128)S(1)} %get-tuple-element.27), channel_id=1, source_target_pairs={{0,31},{1,0},{2,1},{3,2},{4,3},{5,4},{6,5},{7,6},{8,7},{9,8},{10,9... | collective-permute-start | bytes 73736 | tf_op jit(solution)/shard_map/ppermute | solution.py:424
  10.3 1.0 %collective-permute-start = (f32[24,128]{1,0:T(8,128)S(1)}, f32[24,128]{1,0:T(8,128)S(1)}, u32[]{:S(2)}, u32[]{:S(2)}) collective-permute-start(f32[24,128]{1,0:T(8,128)S(1)} %get-tuple-element.23), channel_id=1, source_target_pairs={{0,128},{128,0},{1,129},{129,1},{2,130},{130,2},{3,131},{131,3},{4... | collective-permute-start | bytes 36872 | tf_op jit(solution)/shard_map/ppermute | solution.py:424
  11.3 0.0 copy-start.10
  11.3 0.0 copy-start.11
  11.3 1.2 %collective-permute-start.1 = (f32[16,128]{1,0:T(8,128)S(1)}, f32[16,128]{1,0:T(8,128)S(1)}, u32[]{:S(2)}, u32[]{:S(2)}) collective-permute-start(f32[16,128]{1,0:T(8,128)S(1)} %get-tuple-element.24), channel_id=1, source_target_pairs={{0,32},{32,64},{64,96},{96,0},{1,33},{33,65},{65,97},{97,1},{2,34}... | collective-permute-start | bytes 24584 | tf_op jit(solution)/shard_map/ppermute | solution.py:424
  12.5 0.0 copy-start.4
  12.5 0.0 copy-start.6
  12.5 0.0 copy-start.7
  12.5 0.0 copy-start.8
  12.5 1.5 %collective-permute-start.2 = (f32[16,128]{1,0:T(8,128)S(1)}, f32[16,128]{1,0:T(8,128)S(1)}, u32[]{:S(2)}, u32[]{:S(2)}) collective-permute-start(f32[16,128]{1,0:T(8,128)S(1)} %get-tuple-element.25), channel_id=1, source_target_pairs={{0,96},{32,0},{64,32},{96,64},{1,97},{33,1},{65,33},{97,65},{2,98}... | collective-permute-start | bytes 24584 | tf_op jit(solution)/shard_map/ppermute | solution.py:424
  14.0 0.0 copy-done
  14.0 0.0 copy-done.3
  14.0 0.0 copy-done.2
  14.0 0.0 copy-done.1
  14.0 0.0 copy-done.9
  14.0 0.0 copy-done.10
  14.1 0.0 copy-done.11
  14.1 2.2 %shard_map.110 = (f32[640,128]{1,0:T(8,128)S(1)}, f32[9,8,16,128]{3,2,1,0:T(8,128)S(1)}, f32[9,8,16,128]{3,2,1,0:T(8,128)S(1)}, f32[8,16,128]{2,1,0:T(8,128)S(1)...) custom-call(s32[32]{0:T(128)S(1)} %copy-done.10, ...), custom_call_target="tpu_custom_call" | custom-call | flops 20000000 | bytes 8000000 | tf_op jit(solution)/shard_map/pallas_call | solution.py:451
  16.3 0.0 collective-permute-done.1.right_in
  16.3 0.0 collective-permute-done.2.left_in
  16.3 0.0 collective-permute-done.x_in
  16.3 0.0 collective-permute-done.3.below_in
  16.3 0.0 collective-permute-done.4.above_in
  16.3 0.0 copy-done.4
  16.3 0.0 copy-done.6
  16.3 0.0 copy-done.7
  16.3 0.0 copy-done.8
  16.4 0.7 %shard_map.111 = (f32[640,128]{1,0:T(8,128)S(1)}, f32[3,8,16,128]{3,2,1,0:T(8,128)S(1)}, f32[8,128]{1,0:T(8,128)S(1)}) custom-call(f32[24,128]{1,0:T(8,128)S(1)} %collective-permute-done.x_in, f32[16,128]{1,0:T(8,128)S(1)} %collective-permute-done.1.right_in, f32[16,128]{1,0:T(8,128)S(1)} %collective-permute-done.2.left_in, ...), custom_call_target="tpu_custom_call", output_to_operand_aliasing={{0}: (15, {})} | custom-call | tf_op jit(solution)/shard_map/pallas_call | solution.py:465
  17.1 18.0 %all_to_all.15 = f32[32,20,1,128]{3,2,1,0:T(1,128)S(1)} all-to-all(f32[32,20,1,128]{3,2,1,0:T(1,128)S(1)} %bitcast.8), channel_id=1, replica_groups=mesh['region'=2,'column'=4,'layer'=32] {'layer'}, dimensions={0} | all-to-all | bytes 655360 | tf_op jit(solution)/shard_map/all_to_all | solution.py:428
  35.1 0.8 %shard_map.112 = f32[128,128]{1,0:T(8,128)S(1)} custom-call(f32[640,128]{1,0:T(8,128)S(1)} %bitcast.9, f32[8,128]{1,0:T(8,128)S(1)} %get-tuple-element.32.refs_1_, s32[16,128]{1,0:T(8,128)S(1)} %get-tuple-element.28.order.refs_2_), custom_call_target="tpu_custom_call" | custom-call | tf_op jit(solution)/shard_map/pallas_call | solution.py:473
  35.9 13.5 %all_to_all.16 = f32[32,4,1,128]{3,1,2,0:T(4,128)S(1)} all-to-all(f32[32,4,1,128]{3,1,2,0:T(4,128)S(1)} %bitcast.11), channel_id=1, replica_groups=mesh['region'=2,'column'=4,'layer'=32] {'layer'}, dimensions={0} | all-to-all | bytes 131072 | tf_op jit(solution)/shard_map/all_to_all | solution.py:428
  49.4 0.4 shard_map.113
  49.8 10.5 %all_to_all.17 = f32[8,8,128]{2,1,0:T(8,128)S(1)} all-to-all(f32[8,8,128]{2,1,0:T(8,128)S(1)} %bitcast.13), channel_id=1, replica_groups=mesh['region'=2,'column'=4,'layer'=32] {'region','column'}, dimensions={0} | all-to-all | bytes 65536 | tf_op jit(solution)/shard_map/all_to_all | solution.py:428
  60.3 0.8 %shard_map.114 = f32[3,8,16,128]{3,2,1,0:T(8,128)} custom-call(f32[64,128]{1,0:T(8,128)S(1)} %bitcast.12, f32[8,16,128]{2,1,0:T(8,128)S(1)} %get-tuple-element.38.refs_1_, f32[9,16,128]{2,1,0:T(8,128)S(1)} %get-tuple-element.39.refs_2_, f32[3,8,16,128]{3,2,1,0:T(8,128)S(1)} %get-tuple-element.40.refs_3_, f32[9,8,16,128]{3,2,1,0:T(8,128)S(1)} %copy-done), custom_call_target="tpu_custom_call" | custom-call | tf_op jit(solution)/shard_map/pallas_call | solution.py:489
Async XLA Ops:
  0.0 14.0 %copy-start = (f32[9,8,16,128]{3,2,1,0:T(8,128)S(1)}, f32[9,8,16,128]{3,2,1,0:T(8,128)}, u32[]{:S(2)}) copy-start(f32[9,8,16,128]{3,2,1,0:T(8,128)} %refs_4_.3) | copy-start | bytes 1769476
  0.0 14.0 %copy-start.3 = (f32[9,8,16,128]{3,2,1,0:T(8,128)S(1)}, f32[9,8,16,128]{3,2,1,0:T(8,128)}, u32[]{:S(2)}) copy-start(f32[9,8,16,128]{3,2,1,0:T(8,128)} %upper.1) | copy-start | bytes 1769476
  0.0 14.0 %copy-start.2 = (f32[9,8,16,128]{3,2,1,0:T(8,128)S(1)}, f32[9,8,16,128]{3,2,1,0:T(8,128)}, u32[]{:S(2)}) copy-start(f32[9,8,16,128]{3,2,1,0:T(8,128)} %lower.1) | copy-start | bytes 1769476
  0.0 14.0 %copy-start.1 = (f32[9,8,16,128]{3,2,1,0:T(8,128)S(1)}, f32[9,8,16,128]{3,2,1,0:T(8,128)}, u32[]{:S(2)}) copy-start(f32[9,8,16,128]{3,2,1,0:T(8,128)} %pivot.1) | copy-start | bytes 1769476
  0.0 1.1 %copy-start.5 = (f32[3,8,16,128]{3,2,1,0:T(8,128)S(1)}, f32[3,8,16,128]{3,2,1,0:T(8,128)}, u32[]{:S(2)}) copy-start(f32[3,8,16,128]{3,2,1,0:T(8,128)} %guess.3) | copy-start | bytes 589828
  1.3 12.8 %copy-start.9 = (f32[9,16]{1,0:T(8,128)S(1)}, f32[9,16]{1,0:T(8,128)}, u32[]{:S(2)}) copy-start(f32[9,16]{1,0:T(8,128)} %refs_2_.1) | copy-start | bytes 1732
  1.3 15.0 %collective-permute-start.3 = (f32[3,16,128]{2,1,0:T(8,128)S(1)}, f32[3,16,128]{2,1,0:T(8,128)S(1)}, u32[]{:S(2)}, u32[]{:S(2)}) collective-permute-start(f32[3,16,128]{2,1,0:T(8,128)S(1)} %get-tuple-element.26), channel_id=1, source_target_pairs={{0,1},{1,2},{2,3},{3,4},{4,5},{5,6},{6,7},{7,8},{8,9},{9,10},{10,1... | collective-permute-start | bytes 73736 | tf_op jit(solution)/shard_map/ppermute | solution.py:424
  3.5 12.8 %collective-permute-start.4 = (f32[3,16,128]{2,1,0:T(8,128)S(1)}, f32[3,16,128]{2,1,0:T(8,128)S(1)}, u32[]{:S(2)}, u32[]{:S(2)}) collective-permute-start(f32[3,16,128]{2,1,0:T(8,128)S(1)} %get-tuple-element.27), channel_id=1, source_target_pairs={{0,31},{1,0},{2,1},{3,2},{4,3},{5,4},{6,5},{7,6},{8,7},{9,8},{10,9... | collective-permute-start | bytes 73736 | tf_op jit(solution)/shard_map/ppermute | solution.py:424
  10.3 6.0 %collective-permute-start = (f32[24,128]{1,0:T(8,128)S(1)}, f32[24,128]{1,0:T(8,128)S(1)}, u32[]{:S(2)}, u32[]{:S(2)}) collective-permute-start(f32[24,128]{1,0:T(8,128)S(1)} %get-tuple-element.23), channel_id=1, source_target_pairs={{0,128},{128,0},{1,129},{129,1},{2,130},{130,2},{3,131},{131,3},{4... | collective-permute-start | bytes 36872 | tf_op jit(solution)/shard_map/ppermute | solution.py:424
  11.3 2.8 %copy-start.10 = (s32[32]{0:T(128)S(1)}, s32[32]{0:T(128)}, u32[]{:S(2)}) copy-start(s32[32]{0:T(128)} %refs_0_.1) | copy-start | bytes 388
  11.3 2.8 %copy-start.11 = (s32[16]{0:T(128)S(1)}, s32[16]{0:T(128)}, u32[]{:S(2)}) copy-start(s32[16]{0:T(128)} %refs_1_.1) | copy-start | bytes 196
  11.3 5.0 %collective-permute-start.1 = (f32[16,128]{1,0:T(8,128)S(1)}, f32[16,128]{1,0:T(8,128)S(1)}, u32[]{:S(2)}, u32[]{:S(2)}) collective-permute-start(f32[16,128]{1,0:T(8,128)S(1)} %get-tuple-element.24), channel_id=1, source_target_pairs={{0,32},{32,64},{64,96},{96,0},{1,33},{33,65},{65,97},{97,1},{2,34}... | collective-permute-start | bytes 24584 | tf_op jit(solution)/shard_map/ppermute | solution.py:424
  12.5 3.8 %copy-start.4 = (f32[9,8,16,128]{3,2,1,0:T(8,128)S(1)}, f32[9,8,16,128]{3,2,1,0:T(8,128)}, u32[]{:S(2)}) copy-start(f32[9,8,16,128]{3,2,1,0:T(8,128)} %diag.1) | copy-start | bytes 1769476
  12.5 3.9 %copy-start.6 = (f32[3,8,16,128]{3,2,1,0:T(8,128)S(1)}, f32[3,8,16,128]{3,2,1,0:T(8,128)}, u32[]{:S(2)}) copy-start(f32[3,8,16,128]{3,2,1,0:T(8,128)} %guess.3) | copy-start | bytes 589828
  12.5 3.9 %copy-start.7 = (f32[3,8,16,128]{3,2,1,0:T(8,128)S(1)}, f32[3,8,16,128]{3,2,1,0:T(8,128)}, u32[]{:S(2)}) copy-start(f32[3,8,16,128]{3,2,1,0:T(8,128)} %rhs.1) | copy-start | bytes 589828
  12.5 3.9 %copy-start.8 = (f32[3,8,16,128]{3,2,1,0:T(8,128)S(1)}, f32[3,8,16,128]{3,2,1,0:T(8,128)}, u32[]{:S(2)}) copy-start(f32[3,8,16,128]{3,2,1,0:T(8,128)} %couple.1) | copy-start | bytes 589828
  12.5 3.8 %collective-permute-start.2 = (f32[16,128]{1,0:T(8,128)S(1)}, f32[16,128]{1,0:T(8,128)S(1)}, u32[]{:S(2)}, u32[]{:S(2)}) collective-permute-start(f32[16,128]{1,0:T(8,128)S(1)} %get-tuple-element.25), channel_id=1, source_target_pairs={{0,96},{32,0},{64,32},{96,64},{1,97},{33,1},{65,33},{97,65},{2,98}... | collective-permute-start | bytes 24584 | tf_op jit(solution)/shard_map/ppermute | solution.py:424

commit v5 on v4

--- a/solution.py
+++ b/solution.py
@@ -118,19 +118,23 @@
         out[...] = jnp.broadcast_to(found, (ROWS, LANES)).astype(jnp.int32)
 
 
-def well_masks(areas, nperf, nwell, tiles, counts, inverse, same_out, block_out, order_out, place_out, group_out):
-    me = lax.axis_index("region") * lax.axis_size("column") + lax.axis_index("column")
+def own_area():
+    return lax.axis_index("region") * lax.axis_size("column") + lax.axis_index("column")
+
+
+def tile_places(areas, nperf, tiles):
     tile_all = iota((areas, LANES), 0) * ROWS + iota((areas, LANES), 1) % ROWS
-    tile_own = me * ROWS + iota((ROWS, LANES), 0)
+    tile_own = own_area() * ROWS + iota((ROWS, LANES), 0)
     place_all = jnp.full((areas, LANES), -1, jnp.int32)
     place_own = jnp.full((ROWS, LANES), -1, jnp.int32)
     for p in range(nperf):
         place_all = jnp.where(tile_all == tiles[p], p, place_all)
         place_own = jnp.where(tile_own == tiles[p], p, place_own)
-    own_area = (iota((areas, LANES), 0) == me) & (place_all >= 0)
-    flag_lane = jnp.sum(jnp.where(own_area, 1.0, 0.0), axis=0, keepdims=True)
-    flag_lane = jnp.broadcast_to(flag_lane, (ROWS, LANES))
-    row_order(flag_lane, jnp.where(place_own >= 0, 1.0, 0.0), order_out, place_out, group_out)
+    return place_all, place_own
+
+
+def well_masks(areas, nperf, nwell, tiles, counts, inverse, same_out, block_out):
+    place_all, place_own = tile_places(areas, nperf, tiles)
     well_all = jnp.where(place_all < 0, -1, 0)
     well_own = jnp.where(place_own < 0, -2, 0)
     end = 0
@@ -148,50 +152,51 @@
 
 
 def maps_kernel(
-    areas, nperf, nwell,
-    tiles, counts, inverse, pivot, lower, upper, well,
-    send, cross_out, state_out, same_out, block_out, order, place_out, rest, states, maps, group,
+    areas, nperf, tiles, pivot, lower, upper, well,
+    send, cross_out, state_out, order, place_out, rest, states, maps, group,
 ):
-    well_masks(
-        areas, nperf, nwell, tiles, counts, inverse, same_out, block_out, order, place_out, group
-    )
+    place_all, place_own = tile_places(areas, nperf, tiles)
+    mine = (iota((areas, LANES), 0) == own_area()) & (place_all >= 0)
+    flag_lane = jnp.sum(jnp.where(mine, 1.0, 0.0), axis=0, keepdims=True)
+    flag_lane = jnp.broadcast_to(flag_lane, (ROWS, LANES))
+    row_order(flag_lane, jnp.where(place_own >= 0, 1.0, 0.0), order, place_out, group)
     top = DEPTH - 1
+    halves = [slice(0, 8), slice(8, 16)]
+
+    def load(ref, k, h):
+        return [ref[c, k, halves[h], :] for c in range(9)]
+
+    state = [None, None]
+    for k in range(DEPTH):
+        for h in range(2):
+            low = load(lower, k, h)
+            state[h] = neg(mat(load(pivot, k, h), low if k == 0 else mat(low, state[h])))
+            for c in range(9):
+                states[h, c, k] = state[h][c]
+    down, cross = list(state), list(state)
+    well_state, well_cross = [None, None], [None, None]
+    for k in reversed(range(DEPTH)):
+        for h in range(2):
+            both = mat(load(pivot, k, h), load(upper, k, h))
+            if k == top:
+                state[h] = neg(both)
+            else:
+                cross[h] = sub([states[h, c, k] for c in range(9)], mat(both, cross[h]))
+                state[h] = neg(mat(both, state[h]))
+            coef = load(well, k, h)
+            more_state, more_cross = mat(coef, state[h]), mat(coef, cross[h])
+            well_state[h] = more_state if k == top else add(well_state[h], more_state)
+            well_cross[h] = more_cross if k == top else add(well_cross[h], more_cross)
+            for c in range(9):
+                cross_out[c, k, halves[h], :] = cross[h][c]
+                state_out[c, k, halves[h], :] = state[h][c]
     for h in range(2):
-        at = slice(8 * h, 8 * h + 8)
-
-        def load(ref, k):
-            return [ref[c, k, at, :] for c in range(9)]
-
-        state = None
-        for k in range(DEPTH):
-            low = load(lower, k)
-            state = neg(mat(load(pivot, k), low if k == 0 else mat(low, state)))
-            for c in range(9):
-                states[c, k] = state[c]
-        down = state
-        cross = state
-        well_state, well_cross = None, None
-        for k in reversed(range(DEPTH)):
-            both = mat(load(pivot, k), load(upper, k))
-            if k == top:
-                state = neg(both)
-            else:
-                cross = sub([states[c, k] for c in range(9)], mat(both, cross))
-                state = neg(mat(both, state))
-            coef = load(well, k)
-            more_state, more_cross = mat(coef, state), mat(coef, cross)
-            well_state = more_state if k == top else add(well_state, more_state)
-            well_cross = more_cross if k == top else add(well_cross, more_cross)
-            for c in range(9):
-                cross_out[c, k, at, :] = cross[c]
-                state_out[c, k, at, :] = state[c]
-        zero = jnp.zeros((8, LANES), jnp.float32)
         for e in range(9):
-            maps[e, at, :] = down[e]
-            maps[9 + e, at, :] = state[e]
-            maps[18 + e, at, :] = cross[e]
-            maps[27 + e, at, :] = well_cross[e]
-            maps[36 + e, at, :] = well_state[e]
+            maps[e, halves[h], :] = down[h][e]
+            maps[9 + e, halves[h], :] = state[h][e]
+            maps[18 + e, halves[h], :] = cross[h][e]
+            maps[27 + e, halves[h], :] = well_cross[h][e]
+            maps[36 + e, halves[h], :] = well_state[h][e]
     for h in range(2):
         at = slice(8 * h, 8 * h + 8)
 
@@ -228,64 +233,69 @@
     row = iota((8, LANES), 0)
     top = DEPTH - 1
     well_sums = jnp.zeros((8, LANES), jnp.float32)
+    halves = [slice(0, 8), slice(8, 16)]
+    edges_right = [jnp.where(column > 0, right_in[at, :], 0.0) for at in halves]
+    edges_left = [jnp.where(column < n_column - 1, left_in[at, :], 0.0) for at in halves]
+
+    def load(ref, k, h, count=9):
+        return [ref[c, k, halves[h], :] for c in range(count)]
+
+    def residual(k, h):
+        at, edge_right, edge_left = halves[h], edges_right[h], edges_left[h]
+        mid = load(guess, k, h, 3)
+        out = vec(load(diag, k, h), mid)
+        for c in range(3):
+            g = mid[c]
+            place = c * DEPTH + k
+            x_row = x_in[place : place + 1, :]
+            if h == 0:
+                outer = jnp.where(region > 0, x_row, 0.0)
+                below = jnp.where(row == 0, outer, pltpu.roll(g, 1, 0))
+                above = guess[c, k, 1:9, :]
+            else:
+                outer = jnp.where(region == 0, x_row, 0.0)
+                below = guess[c, k, 7:15, :]
+                above = jnp.where(row == 7, outer, pltpu.roll(g, 7, 0))
+            first = pltpu.roll(edge_right, LANES - place, 1) if place else edge_right
+            before = jnp.where(lane == 0, first, pltpu.roll(g, 1, 1))
+            last = pltpu.roll(edge_left, LANES - 1 - place, 1)
+            after = jnp.where(lane == LANES - 1, last, pltpu.roll(g, LANES - 1, 1))
+            beside = below + above + before + after
+            if k > 0:
+                beside = beside + guess[c, k - 1, at, :]
+            else:
+                beside = beside + jnp.where(layer > 0, below_in[c, at, :], 0.0)
+            if k < top:
+                beside = beside + guess[c, k + 1, at, :]
+            else:
+                beside = beside + jnp.where(layer < n_layer - 1, above_in[c, at, :], 0.0)
+            out[c] = rhs[c, k, at, :] - (out[c] - couple[c, k, at, :] * beside)
+        return out
+
+    f = [None, None]
+    for k in range(DEPTH):
+        for h in range(2):
+            res = residual(k, h)
+            if k > 0:
+                res = sub(res, vec(load(lower, k, h), f[h]))
+            f[h] = vec(load(pivot, k, h), res)
+            for c in range(3):
+                forward[h, c, k] = f[h][c]
+    s, well_const = list(f), [None, None]
+    for k in reversed(range(DEPTH)):
+        for h in range(2):
+            if k < top:
+                more = vec(load(pivot, k, h), vec(load(upper, k, h), s[h]))
+                s[h] = sub([forward[h, c, k] for c in range(3)], more)
+            more = vec(load(well, k, h), s[h])
+            well_const[h] = more if k == top else add(well_const[h], more)
+            for c in range(3):
+                trial_out[c, k, halves[h], :] = s[h][c]
     for h in range(2):
-        at = slice(8 * h, 8 * h + 8)
-
-        def load(ref, k, count=9):
-            return [ref[c, k, at, :] for c in range(count)]
-
-        edge_right = jnp.where(column > 0, right_in[at, :], 0.0)
-        edge_left = jnp.where(column < n_column - 1, left_in[at, :], 0.0)
-
-        def residual(k):
-            mid = load(guess, k, 3)
-            out = vec(load(diag, k), mid)
-            for c in range(3):
-                g = mid[c]
-                place = c * DEPTH + k
-                x_row = x_in[place : place + 1, :]
-                if h == 0:
-                    outer = jnp.where(region > 0, x_row, 0.0)
-                    below = jnp.where(row == 0, outer, pltpu.roll(g, 1, 0))
-                    above = guess[c, k, 1:9, :]
-                else:
-                    outer = jnp.where(region == 0, x_row, 0.0)
-                    below = guess[c, k, 7:15, :]
-                    above = jnp.where(row == 7, outer, pltpu.roll(g, 7, 0))
-                first = pltpu.roll(edge_right, LANES - place, 1) if place else edge_right
-                before = jnp.where(lane == 0, first, pltpu.roll(g, 1, 1))
-                last = pltpu.roll(edge_left, LANES - 1 - place, 1)
-                after = jnp.where(lane == LANES - 1, last, pltpu.roll(g, LANES - 1, 1))
-                beside = below + above + before + after
-                if k > 0:
-                    beside = beside + guess[c, k - 1, at, :]
-                else:
-                    beside = beside + jnp.where(layer > 0, below_in[c, at, :], 0.0)
-                if k < top:
-                    beside = beside + guess[c, k + 1, at, :]
-                else:
-                    beside = beside + jnp.where(layer < n_layer - 1, above_in[c, at, :], 0.0)
-                out[c] = rhs[c, k, at, :] - (out[c] - couple[c, k, at, :] * beside)
-            return out
-
-        f = None
-        for k in range(DEPTH):
-            res = residual(k)
-            f = vec(load(pivot, k), res if k == 0 else sub(res, vec(load(lower, k), f)))
-            for c in range(3):
-                forward[c, k] = f[c]
-        s, well_const = f, None
-        for k in reversed(range(DEPTH)):
-            if k < top:
-                s = sub([forward[c, k] for c in range(3)], vec(load(pivot, k), vec(load(upper, k), s)))
-            more = vec(load(well, k), s)
-            well_const = more if k == top else add(well_const, more)
-            for c in range(3):
-                trial_out[c, k, at, :] = s[c]
         for c in range(3):
-            ends[c, at, :] = f[c]
-            ends[3 + c, at, :] = s[c]
-            total = jnp.sum(well_const[c], axis=1, keepdims=True)
+            ends[c, halves[h], :] = f[h][c]
+            ends[3 + c, halves[h], :] = s[h][c]
+            total = lane_sum(well_const[h][c])
             well_sums = well_sums + jnp.where(lane == c * ROWS + 8 * h + row, total, 0.0)
     for h in range(2):
         at = slice(8 * h, 8 * h + 8)
@@ -312,7 +322,11 @@
             at = slice(d, d + 1)
             for c in range(3):
                 inflow_ref[c, at, :] = x[c]
-            x = add([base_ref[c, at, :] for c in range(3)], vec([step_ref[e, at, :] for e in range(9)], x))
+            step = [step_ref[e, at, :] for e in range(9)]
+            x = [
+                (base_ref[i, at, :] + step[3 * i] * x[0]) + (step[3 * i + 1] * x[1] + step[3 * i + 2] * x[2])
+                for i in range(3)
+            ]
         return [inflow_ref[c] for c in range(3)]
 
     sets = [swapped(rows(m), (1, 2)) for m in range(4)]
@@ -353,7 +367,16 @@
     send[pl.ds(3, peers, BACK), :] = jnp.broadcast_to(mine, (peers, LANES))
 
 
-def solved_kernel(areas, peers, got, cross, state, trial, place_in, solved, sums, inflow):
+def sums_kernel(peers, got, sums):
+    total = jnp.sum(got[pl.ds(3, peers, BACK), :], axis=0, keepdims=True)
+    sums[...] = jnp.broadcast_to(total, (8, LANES))
+
+
+def solved_kernel(
+    areas, nperf, nwell, tiles, counts, inverse, got, cross, state, trial, place_in,
+    solved, same_out, block_out, inflow,
+):
+    well_masks(areas, nperf, nwell, tiles, counts, inverse, same_out, block_out)
     for c in range(3):
         parts = [got[pl.ds(e * BACK + c, GROUPS, ACROSS * BACK), :] for e in range(ACROSS)]
         for i, part in enumerate(swapped(parts, (1, 2, 4))):
@@ -367,18 +390,26 @@
 
     u = [rows_of(c) for c in range(3)]
     w = [rows_of(3 + c) for c in range(3)]
-    total = jnp.sum(got[pl.ds(3, peers, BACK), :], axis=0, keepdims=True)
-    sums[...] = jnp.broadcast_to(total, (8 * areas, LANES))
     for k in range(DEPTH):
         part = add(vec([cross[e, k] for e in range(9)], u), vec([state[e, k] for e in range(9)], w))
         for c in range(3):
             solved[c, k] = trial[c, k] + part[c]
 
 
-def wells_kernel(areas, sums, same, block, solved, well, out):
+def pair_kernel(mine, other, out):
+    region = lax.axis_index("region")
+    out[0:1, :] = jnp.where(region == 0, mine[0:1, :], other[0:1, :])
+    out[1:8, :] = jnp.where(region == 0, other[1:8, :], mine[1:8, :])
+
+
+def wells_kernel(near, after, before, across, same, block, solved, well, out, held, sems):
     gathered = jnp.zeros((ROWS, LANES), jnp.float32)
-    for a in range(areas):
-        gathered = gathered + jnp.where(same[a] > 0.0, sums[8 * a : 8 * a + 1, :], 0.0)
+    column = lax.axis_index("column")
+    n_column = lax.axis_size("column")
+    for by, sums in enumerate((near, after, across, before)):
+        at = lax.rem(column + by, n_column)
+        for r in range(2):
+            gathered = gathered + jnp.where(same[r * n_column + at] > 0.0, sums[r : r + 1, :], 0.0)
     wide = iota((ROWS, LANES), 1)
     totals = [
         jnp.sum(
@@ -389,11 +420,15 @@
         for c in range(3)
     ]
     rate = vec([block[e] for e in range(9)], totals)
-    for k in range(DEPTH):
-        for c in range(3):
-            out[c, k] = solved[c, k] - (
+    copies = [pltpu.make_async_copy(held.at[c], out.at[c], sems.at[c]) for c in range(3)]
+    for c in range(3):
+        for k in range(DEPTH):
+            held[c, k] = solved[c, k] - (
                 well[c, k] * rate[0] + well[3 + c, k] * rate[1] + well[6 + c, k] * rate[2]
             )
+        copies[c].start()
+    for copy in copies:
+        copy.wait()
 
 
 def f32(*shape):
@@ -406,12 +441,12 @@
 FIRST = pl.CostEstimate(flops=20_000_000_000, bytes_accessed=80_000_000, transcendentals=0)
 
 
-def call(kernel, out_shape, in_specs, scratch=(), cost=None, aliases=None):
+def call(kernel, out_shape, in_specs, scratch=(), cost=None, aliases=None, out_space=None):
     return pl.pallas_call(
         kernel,
         out_shape=out_shape,
         in_specs=in_specs,
-        out_specs=jax.tree.map(lambda _: VMEM, out_shape),
+        out_specs=jax.tree.map(lambda _: out_space or VMEM, out_shape),
         scratch_shapes=scratch,
         cost_estimate=cost,
         input_output_aliases=aliases or {},
@@ -448,25 +483,24 @@
     x_in = moved(x_face, "region", 1)
     nine, three = f32(9, *cells), f32(3, *cells)
     index = jax.ShapeDtypeStruct((ROWS, LANES), jnp.int32)
-    send, cross, state, same, block, order, place, rest = call(
-        lambda *refs: maps_kernel(areas, tiles.shape[0], counts.shape[0], *refs),
+    send, cross, state, order, place, rest = call(
+        lambda *refs: maps_kernel(areas, tiles.shape[0], *refs),
         (
-            f32(peers * PACK, LANES), nine, nine, f32(areas, ROWS, LANES), f32(9, ROWS, LANES),
-            index, index, f32(2, ROWS, LANES),
+            f32(peers * PACK, LANES), nine, nine, index, index, f32(2, ROWS, LANES),
         ),
-        [SMEM] * 3 + [VMEM] * 4,
+        [SMEM] + [VMEM] * 4,
         [
-            pltpu.VMEM((9, DEPTH, 8, LANES), jnp.float32),
+            pltpu.VMEM((2, 9, DEPTH, 8, LANES), jnp.float32),
             pltpu.VMEM((45, ROWS, LANES), jnp.float32),
             pltpu.VMEM((ROWS, LANES), jnp.int32),
         ],
         cost=LONG,
-    )(tiles, counts, inverse, pivot, lower, upper, well)
+    )(tiles, pivot, lower, upper, well)
     send, trial, well_sums = call(
         trial_kernel,
         (f32(peers * PACK, LANES), three, f32(8, LANES)),
         [VMEM] * 16,
-        [pltpu.VMEM((3, DEPTH, 8, LANES), jnp.float32), pltpu.VMEM((6, ROWS, LANES), jnp.float32)],
+        [pltpu.VMEM((2, 3, DEPTH, 8, LANES), jnp.float32), pltpu.VMEM((6, ROWS, LANES), jnp.float32)],
         aliases={15: 0},
     )(x_in, right_in, left_in, below_in, above_in, rhs, guess, diag, couple, pivot, lower, upper, well, order, rest, send)
     got = exchanged(send.reshape(peers, PACK, 1, LANES), "layer").reshape(peers * PACK, LANES)
@@ -481,14 +515,23 @@
         ],
     )(got, well_sums, order)
     got = exchanged(back.reshape(peers, BACK, 1, LANES), "layer").reshape(peers * BACK, LANES)
-    solved, sums = call(
-        lambda *refs: solved_kernel(areas, peers, *refs), (three, f32(8 * areas, LANES)), [VMEM] * 5,
+    sums = call(lambda *refs: sums_kernel(peers, *refs), f32(8, LANES), [VMEM])(got)
+    near = call(pair_kernel, f32(8, LANES), [VMEM] * 2)(sums, moved(sums, "region", 1))
+    after, before, across = [moved(near, "column", by) for by in (-1, 1, 2)]
+    solved, same, block = call(
+        lambda *refs: solved_kernel(areas, tiles.shape[0], counts.shape[0], *refs),
+        (three, f32(areas, ROWS, LANES), f32(9, ROWS, LANES)),
+        [SMEM] * 3 + [VMEM] * 5,
         [pltpu.VMEM((6, ROWS, LANES), jnp.float32)],
-    )(got, cross, state, trial, place)
-    sums = exchanged(sums.reshape(areas, 8, LANES), AREA).reshape(8 * areas, LANES)
-    return call(lambda *refs: wells_kernel(areas, *refs), three, [VMEM] * 5)(
-        sums, same, block, solved, well
-    )
+        cost=LONG,
+    )(tiles, counts, inverse, got, cross, state, trial, place)
+    return call(
+        wells_kernel,
+        three,
+        [VMEM] * 8,
+        [pltpu.VMEM((3, *cells), jnp.float32), pltpu.SemaphoreType.DMA((3,))],
+        out_space=pl.BlockSpec(memory_space=pl.ANY),
+    )(near, after, before, across, same, block, solved, well)
 
 
 def solution(mesh):

time: 61.3 us -> 59.6 us (0.972)
  blocking collectives: 42 us -> 31.5 us
  starting transfers between devices: 12.7 us -> 19.9 us
  waiting for transfers between devices: 0.01 us -> 0.84 us
  local copies, waits for them, and re-layouts: 1.12 us -> 1.76 us
    all_to_all x3 -> x2, blocking collectives: 42 us -> 31.5 us  [exchanged(): return lax.all_to_all(value, axes, split_axis=0, concat_axis=0, tiled=True)]
    ppermute x5 -> x9, starting transfers between devices: 12.7 us -> 19.9 us  [moved(): lax.ppermute(value, axis, [(i, (i + by) % count) for i in range(count)])]
    ppermute x5 -> x9, waiting for transfers between devices: 0.01 us -> 0.84 us  [moved(): lax.ppermute(value, axis, [(i, (i + by) % count) for i in range(count)])]
    unnamed x24, local copies, waits for them, and re-layouts: 1.12 us -> 1.76 us
    pallas_call x3 -> x5, Pallas kernels: 3.36 us -> 3.74 us  [the longest x1 1.78 us: local(): call(lambda *refs: maps_kernel(areas, tiles.shape[0], *refs), (f32(peers...]
  transfers between devices with their start and end apart: 5 -> 9, of which waited for: 0 -> 1; matrix products, arithmetic and copies ran while one was open for 0% -> 0% of each run, Pallas kernels for 4% -> 5%
where the time goes in v5:
time: 59.6 us; the launch traced here: 59.5 us
  blocking collectives  31.5 us (53%)
  starting transfers between devices  19.9 us (33%)
  Pallas kernels  5.34 us (9%)
  local copies, waits for them, and re-layouts  1.76 us (3%)
  waiting for transfers between devices  0.84 us (1%)
    all_to_all x2, blocking collectives, exchanged(): return lax.all_to_all(value, axes, split_axis=0, concat_axis=0, tiled=True)  31.5 us
    ppermute x9, starting transfers between devices, moved(): lax.ppermute(value, axis, [(i, (i + by) % count) for i in range(count)])  19.9 us
    pallas_call x1, Pallas kernels, local(): call(lambda *refs: maps_kernel(areas, tiles.shape[0], *refs), (f32(peers...  1.78 us
    unnamed x24, local copies, waits for them, and re-layouts  1.76 us
  transfers between devices with their start and end apart: 9, of which 1 were waited for; matrix products, arithmetic and copies ran while one was open for 0% of the time, Pallas kernels for 5%

profile of v5, /device:TPU:1, one launch (start us, length us, event | category | flops | bytes accessed | tf_op | source)
XLA Modules:
  0.0 59.5 jit_solution(16746766999999920379)
XLA Ops:
  0.0 0.0 copy-start
  0.0 0.0 copy-start.3
  0.0 0.0 copy-start.2
  0.0 0.0 copy-start.1
  0.0 0.0 copy-start.5
  0.0 1.1 %copy-done.5 = f32[3,8,16,128]{3,2,1,0:T(8,128)S(1)} copy-done((f32[3,8,16,128]{3,2,1,0:T(8,128)S(1)}, f32[3,8,16,128]{3,2,1,0:T(8,128)}, u32[]{:S(2)}) %copy-start.5) | copy-done | bytes 196632
  1.1 0.2 shard_map.109
  1.3 2.2 %collective-permute-start.3 = (f32[3,16,128]{2,1,0:T(8,128)S(1)}, f32[3,16,128]{2,1,0:T(8,128)S(1)}, u32[]{:S(2)}, u32[]{:S(2)}) collective-permute-start(f32[3,16,128]{2,1,0:T(8,128)S(1)} %get-tuple-element.25), channel_id=1, source_target_pairs={{0,1},{1,2},{2,3},{3,4},{4,5},{5,6},{6,7},{7,8},{8,9},{9,10},{10,1... | collective-permute-start | bytes 73736 | tf_op jit(solution)/shard_map/ppermute | solution.py:459
  3.5 6.8 %collective-permute-start.4 = (f32[3,16,128]{2,1,0:T(8,128)S(1)}, f32[3,16,128]{2,1,0:T(8,128)S(1)}, u32[]{:S(2)}, u32[]{:S(2)}) collective-permute-start(f32[3,16,128]{2,1,0:T(8,128)S(1)} %get-tuple-element.26), channel_id=1, source_target_pairs={{0,31},{1,0},{2,1},{3,2},{4,3},{5,4},{6,5},{7,6},{8,7},{9,8},{10,9... | collective-permute-start | bytes 73736 | tf_op jit(solution)/shard_map/ppermute | solution.py:459
  10.3 1.0 %collective-permute-start = (f32[24,128]{1,0:T(8,128)S(1)}, f32[24,128]{1,0:T(8,128)S(1)}, u32[]{:S(2)}, u32[]{:S(2)}) collective-permute-start(f32[24,128]{1,0:T(8,128)S(1)} %get-tuple-element.22), channel_id=1, source_target_pairs={{0,128},{128,0},{1,129},{129,1},{2,130},{130,2},{3,131},{131,3},{4... | collective-permute-start | bytes 36872 | tf_op jit(solution)/shard_map/ppermute | solution.py:459
  11.2 0.0 copy-start.10
  11.2 1.2 %collective-permute-start.1 = (f32[16,128]{1,0:T(8,128)S(1)}, f32[16,128]{1,0:T(8,128)S(1)}, u32[]{:S(2)}, u32[]{:S(2)}) collective-permute-start(f32[16,128]{1,0:T(8,128)S(1)} %get-tuple-element.23), channel_id=1, source_target_pairs={{0,32},{32,64},{64,96},{96,0},{1,33},{33,65},{65,97},{97,1},{2,34}... | collective-permute-start | bytes 24584 | tf_op jit(solution)/shard_map/ppermute | solution.py:459
  12.5 0.0 copy-start.4
  12.5 0.0 copy-start.6
  12.5 0.0 copy-start.7
  12.5 1.5 %collective-permute-start.2 = (f32[16,128]{1,0:T(8,128)S(1)}, f32[16,128]{1,0:T(8,128)S(1)}, u32[]{:S(2)}, u32[]{:S(2)}) collective-permute-start(f32[16,128]{1,0:T(8,128)S(1)} %get-tuple-element.24), channel_id=1, source_target_pairs={{0,96},{32,0},{64,32},{96,64},{1,97},{33,1},{65,33},{97,65},{2,98}... | collective-permute-start | bytes 24584 | tf_op jit(solution)/shard_map/ppermute | solution.py:459
  14.0 0.0 copy-done
  14.0 0.0 copy-done.3
  14.0 0.0 copy-done.2
  14.0 0.0 copy-done.1
  14.0 0.0 copy-done.10
  14.0 1.8 %shard_map.110 = (f32[640,128]{1,0:T(8,128)S(1)}, f32[9,8,16,128]{3,2,1,0:T(8,128)S(1)}, f32[9,8,16,128]{3,2,1,0:T(8,128)S(1)}, s32[16,128]{1,0:T(8,128)S(1)}, s...) custom-call(s32[32]{0:T(128)S(1)} %copy-done.10, f32[9,8,16,128]{3,2,1,0:T(8,128)S(1)} %copy-done.1, ...), custom_call_target="tpu_custom_call" | custom-call | flops 20000000 | bytes 8000000 | tf_op jit(solution)/shard_map/pallas_call | solution.py:486
  15.8 0.0 collective-permute-done.1.right_in
  15.8 0.0 collective-permute-done.2.left_in
  15.8 0.0 collective-permute-done.x_in
  15.9 0.0 collective-permute-done.3.below_in
  15.9 0.0 collective-permute-done.4.above_in
  15.9 0.0 copy-done.4
  15.9 0.0 copy-done.6
  15.9 0.0 copy-done.7
  15.9 0.0 copy-done.8
  15.9 0.7 %shard_map.111 = (f32[640,128]{1,0:T(8,128)S(1)}, f32[3,8,16,128]{3,2,1,0:T(8,128)S(1)}, f32[8,128]{1,0:T(8,128)S(1)}) custom-call(f32[24,128]{1,0:T(8,128)S(1)} %collective-permute-done.x_in, f32[16,128]{1,0:T(8,128)S(1)} %collective-permute-done.1.right_in, f32[16,128]{1,0:T(8,128)S(1)} %collective-permute-done.2.left_in, ...), custom_call_target="tpu_custom_call", output_to_operand_aliasing={{0}: (15, {})} | custom-call | tf_op jit(solution)/shard_map/pallas_call | solution.py:499
  16.6 17.9 %all_to_all.10 = f32[32,20,1,128]{3,2,1,0:T(1,128)S(1)} all-to-all(f32[32,20,1,128]{3,2,1,0:T(1,128)S(1)} %bitcast.6), channel_id=1, replica_groups=mesh['region'=2,'column'=4,'layer'=32] {'layer'}, dimensions={0} | all-to-all | bytes 655360 | tf_op jit(solution)/shard_map/all_to_all | solution.py:463
  34.5 0.8 %shard_map.112 = f32[128,128]{1,0:T(8,128)S(1)} custom-call(f32[640,128]{1,0:T(8,128)S(1)} %bitcast.7, f32[8,128]{1,0:T(8,128)S(1)} %get-tuple-element.31.refs_1_, s32[16,128]{1,0:T(8,128)S(1)} %get-tuple-element.27.order.refs_2_), custom_call_target="tpu_custom_call" | custom-call | tf_op jit(solution)/shard_map/pallas_call | solution.py:507
  35.2 13.6 %all_to_all.11 = f32[32,4,1,128]{3,1,2,0:T(4,128)S(1)} all-to-all(f32[32,4,1,128]{3,1,2,0:T(4,128)S(1)} %bitcast.10), channel_id=1, replica_groups=mesh['region'=2,'column'=4,'layer'=32] {'layer'}, dimensions={0} | all-to-all | bytes 131072 | tf_op jit(solution)/shard_map/all_to_all | solution.py:463
  48.8 0.0 copy-start.9
  48.9 2.9 %collective-permute-start.5 = (f32[8,128]{1,0:T(8,128)S(1)}, f32[8,128]{1,0:T(8,128)S(1)}, u32[]{:S(2)}, u32[]{:S(2)}) collective-permute-start(f32[8,128]{1,0:T(8,128)S(1)} %shard_map.113.mine), channel_id=1, source_target_pairs={{0,128},{128,0},{1,129},{129,1},{2,130},{130,2},{3,131},{131,3},{4... | collective-permute-start | bytes 12296 | tf_op jit(solution)/shard_map/ppermute | solution.py:459
  51.7 0.8 %collective-permute-done.5.other = f32[8,128]{1,0:T(8,128)S(1)} collective-permute-done((f32[8,128]{1,0:T(8,128)S(1)}, f32[8,128]{1,0:T(8,128)S(1)}, u32[]{:S(2)}, u32[]{:S(2)}) %collective-permute-start.5) | collective-permute-done | bytes 4128 | tf_op jit(solution)/shard_map/ppermute | solution.py:459
  52.5 1.6 %collective-permute-start.8 = (f32[8,128]{1,0:T(8,128)S(1)}, f32[8,128]{1,0:T(8,128)S(1)}, u32[]{:S(2)}, u32[]{:S(2)}) collective-permute-start(f32[8,128]{1,0:T(8,128)S(1)} %shard_map.114.near), channel_id=1, source_target_pairs={{0,64},{32,96},{64,0},{96,32},{1,65},{33,97},{65,1},{97,33},{2,66}... | collective-permute-start | bytes 12296 | tf_op jit(solution)/shard_map/ppermute | solution.py:459
  54.2 0.8 %collective-permute-start.7 = (f32[8,128]{1,0:T(8,128)S(1)}, f32[8,128]{1,0:T(8,128)S(1)}, u32[]{:S(2)}, u32[]{:S(2)}) collective-permute-start(f32[8,128]{1,0:T(8,128)S(1)} %shard_map.114.near), channel_id=1, source_target_pairs={{0,32},{32,64},{64,96},{96,0},{1,33},{33,65},{65,97},{97,1},{2,34}... | collective-permute-start | bytes 12296 | tf_op jit(solution)/shard_map/ppermute | solution.py:459
  55.0 1.9 %collective-permute-start.6 = (f32[8,128]{1,0:T(8,128)S(1)}, f32[8,128]{1,0:T(8,128)S(1)}, u32[]{:S(2)}, u32[]{:S(2)}) collective-permute-start(f32[8,128]{1,0:T(8,128)S(1)} %shard_map.114.near), channel_id=1, source_target_pairs={{0,96},{32,0},{64,32},{96,64},{1,97},{33,1},{65,33},{97,65},{2,98}... | collective-permute-start | bytes 12296 | tf_op jit(solution)/shard_map/ppermute | solution.py:459
  56.8 0.0 copy-done.9
  56.8 0.7 %copy-done.11 = s32[16]{0:T(128)S(1)} copy-done((s32[16]{0:T(128)S(1)}, s32[16]{0:T(128)}, u32[]{:S(2)}) %copy-start.11) | copy-done | bytes 88
  57.5 1.1 %shard_map.115 = (f32[3,8,16,128]{3,2,1,0:T(8,128)S(1)}, f32[8,16,128]{2,1,0:T(8,128)S(1)}, f32[9,16,128]{2,1,0:T(8,128)S(1)}) custom-call(s32[32]{0:T(128)S(1)} %copy-done.10, s32[16]{0:T(128)S(1)} %copy-done.11, f32[9,16]{1,0:T(8,128)S(1)} %copy-done.9, f32[128,128]{1,0:T(8,128)S(1)} %bitcast.9, f32[9,8,16,128]{3,2,1,0:T(8,128)S(1)} %get-tuple-element.32.refs_4_, ...), custom_call_target="tpu_custom_call" | custom-call | flops 20000000 | bytes 8000000 | tf_op jit(solution)/shard_map/pallas_call | solution.py:521
  58.6 0.0 collective-permute-done.8.across
  58.6 0.0 collective-permute-done.7.before
  58.6 0.0 collective-permute-done.6.after
  58.6 0.8 %shard_map.116 = f32[3,8,16,128]{3,2,1,0:T(8,128)} custom-call(f32[8,128]{1,0:T(8,128)S(1)} %shard_map.114.near, f32[8,128]{1,0:T(8,128)S(1)} %collective-permute-done.6.after, f32[8,128]{1,0:T(8,128)S(1)} %collective-permute-done.7.before, f32[8,128]{1,0:T(8,128)S(1)} %collective-permute-done.8.across, f32[8,16,128]{2,1,0:T(8,128)S(1)} %get-tuple-element.36.same, ...), custom_call_target="tpu_custom_call" | custom-call | tf_op jit(solution)/shard_map/pallas_call | solution.py:528
  (4 shorter events, 0.0 us)
Async XLA Ops:
  0.0 14.0 %copy-start = (f32[9,8,16,128]{3,2,1,0:T(8,128)S(1)}, f32[9,8,16,128]{3,2,1,0:T(8,128)}, u32[]{:S(2)}) copy-start(f32[9,8,16,128]{3,2,1,0:T(8,128)} %well.3) | copy-start | bytes 1769476
  0.0 14.0 %copy-start.3 = (f32[9,8,16,128]{3,2,1,0:T(8,128)S(1)}, f32[9,8,16,128]{3,2,1,0:T(8,128)}, u32[]{:S(2)}) copy-start(f32[9,8,16,128]{3,2,1,0:T(8,128)} %upper.1) | copy-start | bytes 1769476
  0.0 14.0 %copy-start.2 = (f32[9,8,16,128]{3,2,1,0:T(8,128)S(1)}, f32[9,8,16,128]{3,2,1,0:T(8,128)}, u32[]{:S(2)}) copy-start(f32[9,8,16,128]{3,2,1,0:T(8,128)} %lower.1) | copy-start | bytes 1769476
  0.0 14.0 %copy-start.1 = (f32[9,8,16,128]{3,2,1,0:T(8,128)S(1)}, f32[9,8,16,128]{3,2,1,0:T(8,128)}, u32[]{:S(2)}) copy-start(f32[9,8,16,128]{3,2,1,0:T(8,128)} %pivot.1) | copy-start | bytes 1769476
  0.0 1.1 %copy-start.5 = (f32[3,8,16,128]{3,2,1,0:T(8,128)S(1)}, f32[3,8,16,128]{3,2,1,0:T(8,128)}, u32[]{:S(2)}) copy-start(f32[3,8,16,128]{3,2,1,0:T(8,128)} %guess.3) | copy-start | bytes 589828
  1.3 14.6 %collective-permute-start.3 = (f32[3,16,128]{2,1,0:T(8,128)S(1)}, f32[3,16,128]{2,1,0:T(8,128)S(1)}, u32[]{:S(2)}, u32[]{:S(2)}) collective-permute-start(f32[3,16,128]{2,1,0:T(8,128)S(1)} %get-tuple-element.25), channel_id=1, source_target_pairs={{0,1},{1,2},{2,3},{3,4},{4,5},{5,6},{6,7},{7,8},{8,9},{9,10},{10,1... | collective-permute-start | bytes 73736 | tf_op jit(solution)/shard_map/ppermute | solution.py:459
  3.5 12.4 %collective-permute-start.4 = (f32[3,16,128]{2,1,0:T(8,128)S(1)}, f32[3,16,128]{2,1,0:T(8,128)S(1)}, u32[]{:S(2)}, u32[]{:S(2)}) collective-permute-start(f32[3,16,128]{2,1,0:T(8,128)S(1)} %get-tuple-element.26), channel_id=1, source_target_pairs={{0,31},{1,0},{2,1},{3,2},{4,3},{5,4},{6,5},{7,6},{8,7},{9,8},{10,9... | collective-permute-start | bytes 73736 | tf_op jit(solution)/shard_map/ppermute | solution.py:459
  10.3 5.6 %collective-permute-start = (f32[24,128]{1,0:T(8,128)S(1)}, f32[24,128]{1,0:T(8,128)S(1)}, u32[]{:S(2)}, u32[]{:S(2)}) collective-permute-start(f32[24,128]{1,0:T(8,128)S(1)} %get-tuple-element.22), channel_id=1, source_target_pairs={{0,128},{128,0},{1,129},{129,1},{2,130},{130,2},{3,131},{131,3},{4... | collective-permute-start | bytes 36872 | tf_op jit(solution)/shard_map/ppermute | solution.py:459
  11.2 2.8 %copy-start.10 = (s32[32]{0:T(128)S(1)}, s32[32]{0:T(128)}, u32[]{:S(2)}) copy-start(s32[32]{0:T(128)} %refs_0_.3) | copy-start | bytes 388
  11.2 4.6 %collective-permute-start.1 = (f32[16,128]{1,0:T(8,128)S(1)}, f32[16,128]{1,0:T(8,128)S(1)}, u32[]{:S(2)}, u32[]{:S(2)}) collective-permute-start(f32[16,128]{1,0:T(8,128)S(1)} %get-tuple-element.23), channel_id=1, source_target_pairs={{0,32},{32,64},{64,96},{96,0},{1,33},{33,65},{65,97},{97,1},{2,34}... | collective-permute-start | bytes 24584 | tf_op jit(solution)/shard_map/ppermute | solution.py:459
  12.5 3.4 %copy-start.4 = (f32[9,8,16,128]{3,2,1,0:T(8,128)S(1)}, f32[9,8,16,128]{3,2,1,0:T(8,128)}, u32[]{:S(2)}) copy-start(f32[9,8,16,128]{3,2,1,0:T(8,128)} %diag.1) | copy-start | bytes 1769476
  12.5 3.4 %copy-start.6 = (f32[3,8,16,128]{3,2,1,0:T(8,128)S(1)}, f32[3,8,16,128]{3,2,1,0:T(8,128)}, u32[]{:S(2)}) copy-start(f32[3,8,16,128]{3,2,1,0:T(8,128)} %guess.3) | copy-start | bytes 589828
  12.5 3.4 %copy-start.7 = (f32[3,8,16,128]{3,2,1,0:T(8,128)S(1)}, f32[3,8,16,128]{3,2,1,0:T(8,128)}, u32[]{:S(2)}) copy-start(f32[3,8,16,128]{3,2,1,0:T(8,128)} %rhs.1) | copy-start | bytes 589828
  12.5 3.4 %copy-start.8 = (f32[3,8,16,128]{3,2,1,0:T(8,128)S(1)}, f32[3,8,16,128]{3,2,1,0:T(8,128)}, u32[]{:S(2)}) copy-start(f32[3,8,16,128]{3,2,1,0:T(8,128)} %couple.1) | copy-start | bytes 589828
  12.5 3.4 %collective-permute-start.2 = (f32[16,128]{1,0:T(8,128)S(1)}, f32[16,128]{1,0:T(8,128)S(1)}, u32[]{:S(2)}, u32[]{:S(2)}) collective-permute-start(f32[16,128]{1,0:T(8,128)S(1)} %get-tuple-element.24), channel_id=1, source_target_pairs={{0,96},{32,0},{64,32},{96,64},{1,97},{33,1},{65,33},{97,65},{2,98}... | collective-permute-start | bytes 24584 | tf_op jit(solution)/shard_map/ppermute | solution.py:459
  48.8 8.0 %copy-start.9 = (f32[9,16]{1,0:T(8,128)S(1)}, f32[9,16]{1,0:T(8,128)}, u32[]{:S(2)}) copy-start(f32[9,16]{1,0:T(8,128)} %refs_2_.3) | copy-start | bytes 1732
  48.9 3.7 %collective-permute-start.5 = (f32[8,128]{1,0:T(8,128)S(1)}, f32[8,128]{1,0:T(8,128)S(1)}, u32[]{:S(2)}, u32[]{:S(2)}) collective-permute-start(f32[8,128]{1,0:T(8,128)S(1)} %shard_map.113.mine), channel_id=1, source_target_pairs={{0,128},{128,0},{1,129},{129,1},{2,130},{130,2},{3,131},{131,3},{4... | collective-permute-start | bytes 12296 | tf_op jit(solution)/shard_map/ppermute | solution.py:459
  52.5 6.1 %collective-permute-start.8 = (f32[8,128]{1,0:T(8,128)S(1)}, f32[8,128]{1,0:T(8,128)S(1)}, u32[]{:S(2)}, u32[]{:S(2)}) collective-permute-start(f32[8,128]{1,0:T(8,128)S(1)} %shard_map.114.near), channel_id=1, source_target_pairs={{0,64},{32,96},{64,0},{96,32},{1,65},{33,97},{65,1},{97,33},{2,66}... | collective-permute-start | bytes 12296 | tf_op jit(solution)/shard_map/ppermute | solution.py:459
  54.2 4.5 %collective-permute-start.7 = (f32[8,128]{1,0:T(8,128)S(1)}, f32[8,128]{1,0:T(8,128)S(1)}, u32[]{:S(2)}, u32[]{:S(2)}) collective-permute-start(f32[8,128]{1,0:T(8,128)S(1)} %shard_map.114.near), channel_id=1, source_target_pairs={{0,32},{32,64},{64,96},{96,0},{1,33},{33,65},{65,97},{97,1},{2,34}... | collective-permute-start | bytes 12296 | tf_op jit(solution)/shard_map/ppermute | solution.py:459
  55.0 3.7 %collective-permute-start.6 = (f32[8,128]{1,0:T(8,128)S(1)}, f32[8,128]{1,0:T(8,128)S(1)}, u32[]{:S(2)}, u32[]{:S(2)}) collective-permute-start(f32[8,128]{1,0:T(8,128)S(1)} %shard_map.114.near), channel_id=1, source_target_pairs={{0,96},{32,0},{64,32},{96,64},{1,97},{33,1},{65,33},{97,65},{2,98}... | collective-permute-start | bytes 12296 | tf_op jit(solution)/shard_map/ppermute | solution.py:459
  56.8 0.7 %copy-start.11 = (s32[16]{0:T(128)S(1)}, s32[16]{0:T(128)}, u32[]{:S(2)}) copy-start(s32[16]{0:T(128)} %refs_1_.3) | copy-start | bytes 196

commit v6 on v5

--- a/solution.py
+++ b/solution.py
@@ -10,7 +10,7 @@
 HALF = LANES // 2
 BLOCK = 16
 GROUPS, ACROSS = 4, 8
-PACK = 20
+PACK = 19
 BACK = 4
 
 TRIAL, WELLS = 3, 4
@@ -86,11 +86,11 @@
     )
 
 
-def put(send, h, m, parts):
+def put(send, h, m, parts, count=4):
     for e, part in enumerate(swapped(parts, (1, 2, 4))):
         for half in range(2):
             at = (ACROSS * (2 * h + half) + e) * PACK + 4 * m
-            send[at : at + 4, :] = part[4 * half : 4 * half + 4, :]
+            send[at : at + count, :] = part[4 * half : 4 * half + count, :]
 
 
 def lane_sum(x):
@@ -216,8 +216,9 @@
         behind = []
         for b in range(7):
             value = jnp.where(j == 0, wells[b], wells[7 + b])
-            behind.append(value if b > 3 else jnp.where(j == 2, wells[14 + b], value))
-        put(send, h, WELLS, [cross[8]] + behind)
+            third = wells[14 + b] if b < 4 else pltpu.roll(cross[8], 7, 0)
+            behind.append(jnp.where(j == 2, third, value) if b < 5 else value)
+        put(send, h, WELLS, [cross[8]] + behind, 3)
 
 
 def trial_kernel(
@@ -308,8 +309,8 @@
     layer = lax.axis_index("layer")
     is_left = iota((peers, LANES), 1) < HALF
 
-    def rows(m):
-        return [got[pl.ds(4 * m + j, peers, PACK), :] for j in range(4)]
+    def rows(m, count=4):
+        return [got[pl.ds(4 * m + j, peers, PACK), :] for j in range(count)]
 
     def turn(x):
         return pltpu.roll(x, HALF, 1)
@@ -333,9 +334,10 @@
     for e in range(9):
         step_ref[e] = sets[e // 4][e % 4]
     source = sets[TRIAL][:3]
-    last = rows(WELLS)
+    last = rows(WELLS, 3)
+    fourth = pltpu.roll(last[2], LANES - 5 * BLOCK, 1)
     mixed = []
-    for pair in sets[2][1:] + [sets[TRIAL][3], swapped(last, (1, 2))[0]]:
+    for pair in sets[2][1:] + [sets[TRIAL][3], swapped(last + [fourth], (1, 2))[0]]:
         mixed += [turn(pair), pair]
     down = chain(source, range(peers))
     up_base = add(source, vec(mixed[:9], [turn(x) for x in down]))

time: 59.6 us -> 59.3 us (level)
  no operation moved by 1% of the time
where the time goes in v6:
time: 59.3 us; the launch traced here: 59.1 us
  blocking collectives  31.1 us (52%)
  starting transfers between devices  19.9 us (34%)
  Pallas kernels  5.36 us (9%)
  local copies, waits for them, and re-layouts  1.76 us (3%)
  waiting for transfers between devices  0.84 us (1%)
    all_to_all x2, blocking collectives, exchanged(): return lax.all_to_all(value, axes, split_axis=0, concat_axis=0, tiled=True)  31.1 us
    ppermute x9, starting transfers between devices, moved(): lax.ppermute(value, axis, [(i, (i + by) % count) for i in range(count)])  19.9 us
    pallas_call x1, Pallas kernels, local(): call(lambda *refs: maps_kernel(areas, tiles.shape[0], *refs), (f32(peers...  1.8 us
    unnamed x24, local copies, waits for them, and re-layouts  1.76 us
  transfers between devices with their start and end apart: 9, of which 1 were waited for; matrix products, arithmetic and copies ran while one was open for 0% of the time, Pallas kernels for 5%

profile of v6, /device:TPU:1, one launch (start us, length us, event | category | flops | bytes accessed | tf_op | source)
XLA Modules:
  0.0 59.1 jit_solution(999077435597013825)
XLA Ops:
  0.0 0.0 copy-start
  0.0 0.0 copy-start.3
  0.0 0.0 copy-start.2
  0.0 0.0 copy-start.1
  0.0 0.0 copy-start.5
  0.0 1.1 %copy-done.5 = f32[3,8,16,128]{3,2,1,0:T(8,128)S(1)} copy-done((f32[3,8,16,128]{3,2,1,0:T(8,128)S(1)}, f32[3,8,16,128]{3,2,1,0:T(8,128)}, u32[]{:S(2)}) %copy-start.5) | copy-done | bytes 196632
  1.1 0.2 shard_map.109
  1.3 2.2 %collective-permute-start.3 = (f32[3,16,128]{2,1,0:T(8,128)S(1)}, f32[3,16,128]{2,1,0:T(8,128)S(1)}, u32[]{:S(2)}, u32[]{:S(2)}) collective-permute-start(f32[3,16,128]{2,1,0:T(8,128)S(1)} %get-tuple-element.25), channel_id=1, source_target_pairs={{0,1},{1,2},{2,3},{3,4},{4,5},{5,6},{6,7},{7,8},{8,9},{9,10},{10,1... | collective-permute-start | bytes 73736 | tf_op jit(solution)/shard_map/ppermute | solution.py:461
  3.5 6.8 %collective-permute-start.4 = (f32[3,16,128]{2,1,0:T(8,128)S(1)}, f32[3,16,128]{2,1,0:T(8,128)S(1)}, u32[]{:S(2)}, u32[]{:S(2)}) collective-permute-start(f32[3,16,128]{2,1,0:T(8,128)S(1)} %get-tuple-element.26), channel_id=1, source_target_pairs={{0,31},{1,0},{2,1},{3,2},{4,3},{5,4},{6,5},{7,6},{8,7},{9,8},{10,9... | collective-permute-start | bytes 73736 | tf_op jit(solution)/shard_map/ppermute | solution.py:461
  10.3 1.0 %collective-permute-start = (f32[24,128]{1,0:T(8,128)S(1)}, f32[24,128]{1,0:T(8,128)S(1)}, u32[]{:S(2)}, u32[]{:S(2)}) collective-permute-start(f32[24,128]{1,0:T(8,128)S(1)} %get-tuple-element.22), channel_id=1, source_target_pairs={{0,128},{128,0},{1,129},{129,1},{2,130},{130,2},{3,131},{131,3},{4... | collective-permute-start | bytes 36872 | tf_op jit(solution)/shard_map/ppermute | solution.py:461
  11.2 0.0 copy-start.10
  11.2 1.2 %collective-permute-start.1 = (f32[16,128]{1,0:T(8,128)S(1)}, f32[16,128]{1,0:T(8,128)S(1)}, u32[]{:S(2)}, u32[]{:S(2)}) collective-permute-start(f32[16,128]{1,0:T(8,128)S(1)} %get-tuple-element.23), channel_id=1, source_target_pairs={{0,32},{32,64},{64,96},{96,0},{1,33},{33,65},{65,97},{97,1},{2,34}... | collective-permute-start | bytes 24584 | tf_op jit(solution)/shard_map/ppermute | solution.py:461
  12.5 0.0 copy-start.4
  12.5 0.0 copy-start.6
  12.5 0.0 copy-start.7
  12.5 1.5 %collective-permute-start.2 = (f32[16,128]{1,0:T(8,128)S(1)}, f32[16,128]{1,0:T(8,128)S(1)}, u32[]{:S(2)}, u32[]{:S(2)}) collective-permute-start(f32[16,128]{1,0:T(8,128)S(1)} %get-tuple-element.24), channel_id=1, source_target_pairs={{0,96},{32,0},{64,32},{96,64},{1,97},{33,1},{65,33},{97,65},{2,98}... | collective-permute-start | bytes 24584 | tf_op jit(solution)/shard_map/ppermute | solution.py:461
  14.0 0.0 copy-done
  14.0 0.0 copy-done.3
  14.0 0.0 copy-done.2
  14.0 0.0 copy-done.1
  14.0 0.0 copy-done.10
  14.0 1.8 %shard_map.110 = (f32[608,128]{1,0:T(8,128)S(1)}, f32[9,8,16,128]{3,2,1,0:T(8,128)S(1)}, f32[9,8,16,128]{3,2,1,0:T(8,128)S(1)}, s32[16,128]{1,0:T(8,128)S(1)}, s...) custom-call(s32[32]{0:T(128)S(1)} %copy-done.10, f32[9,8,16,128]{3,2,1,0:T(8,128)S(1)} %copy-done.1, ...), custom_call_target="tpu_custom_call" | custom-call | flops 20000000 | bytes 8000000 | tf_op jit(solution)/shard_map/pallas_call | solution.py:488
  15.8 0.0 collective-permute-done.1.right_in
  15.8 0.0 collective-permute-done.2.left_in
  15.9 0.0 collective-permute-done.x_in
  15.9 0.0 collective-permute-done.3.below_in
  15.9 0.0 collective-permute-done.4.above_in
  15.9 0.0 copy-done.4
  15.9 0.0 copy-done.6
  15.9 0.0 copy-done.7
  15.9 0.0 copy-done.8
  15.9 0.7 %shard_map.111 = (f32[608,128]{1,0:T(8,128)S(1)}, f32[3,8,16,128]{3,2,1,0:T(8,128)S(1)}, f32[8,128]{1,0:T(8,128)S(1)}) custom-call(f32[24,128]{1,0:T(8,128)S(1)} %collective-permute-done.x_in, f32[16,128]{1,0:T(8,128)S(1)} %collective-permute-done.1.right_in, f32[16,128]{1,0:T(8,128)S(1)} %collective-permute-done.2.left_in, ...), custom_call_target="tpu_custom_call", output_to_operand_aliasing={{0}: (15, {})} | custom-call | tf_op jit(solution)/shard_map/pallas_call | solution.py:501
  16.6 17.6 %all_to_all.10 = f32[32,19,1,128]{3,2,1,0:T(1,128)S(1)} all-to-all(f32[32,19,1,128]{3,2,1,0:T(1,128)S(1)} %bitcast.6), channel_id=1, replica_groups=mesh['region'=2,'column'=4,'layer'=32] {'layer'}, dimensions={0} | all-to-all | bytes 622592 | tf_op jit(solution)/shard_map/all_to_all | solution.py:465
  34.2 0.8 %shard_map.112 = f32[128,128]{1,0:T(8,128)S(1)} custom-call(f32[608,128]{1,0:T(8,128)S(1)} %bitcast.7, f32[8,128]{1,0:T(8,128)S(1)} %get-tuple-element.31.refs_1_, s32[16,128]{1,0:T(8,128)S(1)} %get-tuple-element.27.order.refs_2_), custom_call_target="tpu_custom_call" | custom-call | tf_op jit(solution)/shard_map/pallas_call | solution.py:509
  34.9 13.6 %all_to_all.11 = f32[32,4,1,128]{3,1,2,0:T(4,128)S(1)} all-to-all(f32[32,4,1,128]{3,1,2,0:T(4,128)S(1)} %bitcast.10), channel_id=1, replica_groups=mesh['region'=2,'column'=4,'layer'=32] {'layer'}, dimensions={0} | all-to-all | bytes 131072 | tf_op jit(solution)/shard_map/all_to_all | solution.py:465
  48.5 0.0 copy-start.9
  48.5 2.9 %collective-permute-start.5 = (f32[8,128]{1,0:T(8,128)S(1)}, f32[8,128]{1,0:T(8,128)S(1)}, u32[]{:S(2)}, u32[]{:S(2)}) collective-permute-start(f32[8,128]{1,0:T(8,128)S(1)} %shard_map.113.mine), channel_id=1, source_target_pairs={{0,128},{128,0},{1,129},{129,1},{2,130},{130,2},{3,131},{131,3},{4... | collective-permute-start | bytes 12296 | tf_op jit(solution)/shard_map/ppermute | solution.py:461
  51.4 0.8 %collective-permute-done.5.other = f32[8,128]{1,0:T(8,128)S(1)} collective-permute-done((f32[8,128]{1,0:T(8,128)S(1)}, f32[8,128]{1,0:T(8,128)S(1)}, u32[]{:S(2)}, u32[]{:S(2)}) %collective-permute-start.5) | collective-permute-done | bytes 4128 | tf_op jit(solution)/shard_map/ppermute | solution.py:461
  52.2 1.6 %collective-permute-start.8 = (f32[8,128]{1,0:T(8,128)S(1)}, f32[8,128]{1,0:T(8,128)S(1)}, u32[]{:S(2)}, u32[]{:S(2)}) collective-permute-start(f32[8,128]{1,0:T(8,128)S(1)} %shard_map.114.near), channel_id=1, source_target_pairs={{0,64},{32,96},{64,0},{96,32},{1,65},{33,97},{65,1},{97,33},{2,66}... | collective-permute-start | bytes 12296 | tf_op jit(solution)/shard_map/ppermute | solution.py:461
  53.8 0.8 %collective-permute-start.7 = (f32[8,128]{1,0:T(8,128)S(1)}, f32[8,128]{1,0:T(8,128)S(1)}, u32[]{:S(2)}, u32[]{:S(2)}) collective-permute-start(f32[8,128]{1,0:T(8,128)S(1)} %shard_map.114.near), channel_id=1, source_target_pairs={{0,32},{32,64},{64,96},{96,0},{1,33},{33,65},{65,97},{97,1},{2,34}... | collective-permute-start | bytes 12296 | tf_op jit(solution)/shard_map/ppermute | solution.py:461
  54.6 1.9 %collective-permute-start.6 = (f32[8,128]{1,0:T(8,128)S(1)}, f32[8,128]{1,0:T(8,128)S(1)}, u32[]{:S(2)}, u32[]{:S(2)}) collective-permute-start(f32[8,128]{1,0:T(8,128)S(1)} %shard_map.114.near), channel_id=1, source_target_pairs={{0,96},{32,0},{64,32},{96,64},{1,97},{33,1},{65,33},{97,65},{2,98}... | collective-permute-start | bytes 12296 | tf_op jit(solution)/shard_map/ppermute | solution.py:461
  56.5 0.0 copy-done.9
  56.5 0.7 %copy-done.11 = s32[16]{0:T(128)S(1)} copy-done((s32[16]{0:T(128)S(1)}, s32[16]{0:T(128)}, u32[]{:S(2)}) %copy-start.11) | copy-done | bytes 88
  57.1 1.1 %shard_map.115 = (f32[3,8,16,128]{3,2,1,0:T(8,128)S(1)}, f32[8,16,128]{2,1,0:T(8,128)S(1)}, f32[9,16,128]{2,1,0:T(8,128)S(1)}) custom-call(s32[32]{0:T(128)S(1)} %copy-done.10, s32[16]{0:T(128)S(1)} %copy-done.11, f32[9,16]{1,0:T(8,128)S(1)} %copy-done.9, f32[128,128]{1,0:T(8,128)S(1)} %bitcast.9, f32[9,8,16,128]{3,2,1,0:T(8,128)S(1)} %get-tuple-element.32.refs_4_, ...), custom_call_target="tpu_custom_call" | custom-call | flops 20000000 | bytes 8000000 | tf_op jit(solution)/shard_map/pallas_call | solution.py:523
  58.3 0.0 collective-permute-done.8.across
  58.3 0.0 collective-permute-done.7.before
  58.3 0.0 collective-permute-done.6.after
  58.3 0.8 %shard_map.116 = f32[3,8,16,128]{3,2,1,0:T(8,128)} custom-call(f32[8,128]{1,0:T(8,128)S(1)} %shard_map.114.near, f32[8,128]{1,0:T(8,128)S(1)} %collective-permute-done.6.after, f32[8,128]{1,0:T(8,128)S(1)} %collective-permute-done.7.before, f32[8,128]{1,0:T(8,128)S(1)} %collective-permute-done.8.across, f32[8,16,128]{2,1,0:T(8,128)S(1)} %get-tuple-element.36.same, ...), custom_call_target="tpu_custom_call" | custom-call | tf_op jit(solution)/shard_map/pallas_call | solution.py:530
  (4 shorter events, 0.0 us)
Async XLA Ops:
  0.0 14.0 %copy-start = (f32[9,8,16,128]{3,2,1,0:T(8,128)S(1)}, f32[9,8,16,128]{3,2,1,0:T(8,128)}, u32[]{:S(2)}) copy-start(f32[9,8,16,128]{3,2,1,0:T(8,128)} %well.3) | copy-start | bytes 1769476
  0.0 14.0 %copy-start.3 = (f32[9,8,16,128]{3,2,1,0:T(8,128)S(1)}, f32[9,8,16,128]{3,2,1,0:T(8,128)}, u32[]{:S(2)}) copy-start(f32[9,8,16,128]{3,2,1,0:T(8,128)} %upper.1) | copy-start | bytes 1769476
  0.0 14.0 %copy-start.2 = (f32[9,8,16,128]{3,2,1,0:T(8,128)S(1)}, f32[9,8,16,128]{3,2,1,0:T(8,128)}, u32[]{:S(2)}) copy-start(f32[9,8,16,128]{3,2,1,0:T(8,128)} %lower.1) | copy-start | bytes 1769476
  0.0 14.0 %copy-start.1 = (f32[9,8,16,128]{3,2,1,0:T(8,128)S(1)}, f32[9,8,16,128]{3,2,1,0:T(8,128)}, u32[]{:S(2)}) copy-start(f32[9,8,16,128]{3,2,1,0:T(8,128)} %pivot.1) | copy-start | bytes 1769476
  0.0 1.1 %copy-start.5 = (f32[3,8,16,128]{3,2,1,0:T(8,128)S(1)}, f32[3,8,16,128]{3,2,1,0:T(8,128)}, u32[]{:S(2)}) copy-start(f32[3,8,16,128]{3,2,1,0:T(8,128)} %guess.3) | copy-start | bytes 589828
  1.3 14.6 %collective-permute-start.3 = (f32[3,16,128]{2,1,0:T(8,128)S(1)}, f32[3,16,128]{2,1,0:T(8,128)S(1)}, u32[]{:S(2)}, u32[]{:S(2)}) collective-permute-start(f32[3,16,128]{2,1,0:T(8,128)S(1)} %get-tuple-element.25), channel_id=1, source_target_pairs={{0,1},{1,2},{2,3},{3,4},{4,5},{5,6},{6,7},{7,8},{8,9},{9,10},{10,1... | collective-permute-start | bytes 73736 | tf_op jit(solution)/shard_map/ppermute | solution.py:461
  3.5 12.4 %collective-permute-start.4 = (f32[3,16,128]{2,1,0:T(8,128)S(1)}, f32[3,16,128]{2,1,0:T(8,128)S(1)}, u32[]{:S(2)}, u32[]{:S(2)}) collective-permute-start(f32[3,16,128]{2,1,0:T(8,128)S(1)} %get-tuple-element.26), channel_id=1, source_target_pairs={{0,31},{1,0},{2,1},{3,2},{4,3},{5,4},{6,5},{7,6},{8,7},{9,8},{10,9... | collective-permute-start | bytes 73736 | tf_op jit(solution)/shard_map/ppermute | solution.py:461
  10.3 5.6 %collective-permute-start = (f32[24,128]{1,0:T(8,128)S(1)}, f32[24,128]{1,0:T(8,128)S(1)}, u32[]{:S(2)}, u32[]{:S(2)}) collective-permute-start(f32[24,128]{1,0:T(8,128)S(1)} %get-tuple-element.22), channel_id=1, source_target_pairs={{0,128},{128,0},{1,129},{129,1},{2,130},{130,2},{3,131},{131,3},{4... | collective-permute-start | bytes 36872 | tf_op jit(solution)/shard_map/ppermute | solution.py:461
  11.2 2.8 %copy-start.10 = (s32[32]{0:T(128)S(1)}, s32[32]{0:T(128)}, u32[]{:S(2)}) copy-start(s32[32]{0:T(128)} %refs_0_.3) | copy-start | bytes 388
  11.2 4.6 %collective-permute-start.1 = (f32[16,128]{1,0:T(8,128)S(1)}, f32[16,128]{1,0:T(8,128)S(1)}, u32[]{:S(2)}, u32[]{:S(2)}) collective-permute-start(f32[16,128]{1,0:T(8,128)S(1)} %get-tuple-element.23), channel_id=1, source_target_pairs={{0,32},{32,64},{64,96},{96,0},{1,33},{33,65},{65,97},{97,1},{2,34}... | collective-permute-start | bytes 24584 | tf_op jit(solution)/shard_map/ppermute | solution.py:461
  12.5 3.4 %copy-start.4 = (f32[9,8,16,128]{3,2,1,0:T(8,128)S(1)}, f32[9,8,16,128]{3,2,1,0:T(8,128)}, u32[]{:S(2)}) copy-start(f32[9,8,16,128]{3,2,1,0:T(8,128)} %diag.1) | copy-start | bytes 1769476
  12.5 3.4 %copy-start.6 = (f32[3,8,16,128]{3,2,1,0:T(8,128)S(1)}, f32[3,8,16,128]{3,2,1,0:T(8,128)}, u32[]{:S(2)}) copy-start(f32[3,8,16,128]{3,2,1,0:T(8,128)} %guess.3) | copy-start | bytes 589828
  12.5 3.5 %copy-start.7 = (f32[3,8,16,128]{3,2,1,0:T(8,128)S(1)}, f32[3,8,16,128]{3,2,1,0:T(8,128)}, u32[]{:S(2)}) copy-start(f32[3,8,16,128]{3,2,1,0:T(8,128)} %rhs.1) | copy-start | bytes 589828
  12.5 3.5 %copy-start.8 = (f32[3,8,16,128]{3,2,1,0:T(8,128)S(1)}, f32[3,8,16,128]{3,2,1,0:T(8,128)}, u32[]{:S(2)}) copy-start(f32[3,8,16,128]{3,2,1,0:T(8,128)} %couple.1) | copy-start | bytes 589828
  12.5 3.4 %collective-permute-start.2 = (f32[16,128]{1,0:T(8,128)S(1)}, f32[16,128]{1,0:T(8,128)S(1)}, u32[]{:S(2)}, u32[]{:S(2)}) collective-permute-start(f32[16,128]{1,0:T(8,128)S(1)} %get-tuple-element.24), channel_id=1, source_target_pairs={{0,96},{32,0},{64,32},{96,64},{1,97},{33,1},{65,33},{97,65},{2,98}... | collective-permute-start | bytes 24584 | tf_op jit(solution)/shard_map/ppermute | solution.py:461
  48.5 8.0 %copy-start.9 = (f32[9,16]{1,0:T(8,128)S(1)}, f32[9,16]{1,0:T(8,128)}, u32[]{:S(2)}) copy-start(f32[9,16]{1,0:T(8,128)} %refs_2_.3) | copy-start | bytes 1732
  48.5 3.7 %collective-permute-start.5 = (f32[8,128]{1,0:T(8,128)S(1)}, f32[8,128]{1,0:T(8,128)S(1)}, u32[]{:S(2)}, u32[]{:S(2)}) collective-permute-start(f32[8,128]{1,0:T(8,128)S(1)} %shard_map.113.mine), channel_id=1, source_target_pairs={{0,128},{128,0},{1,129},{129,1},{2,130},{130,2},{3,131},{131,3},{4... | collective-permute-start | bytes 12296 | tf_op jit(solution)/shard_map/ppermute | solution.py:461
  52.2 6.0 %collective-permute-start.8 = (f32[8,128]{1,0:T(8,128)S(1)}, f32[8,128]{1,0:T(8,128)S(1)}, u32[]{:S(2)}, u32[]{:S(2)}) collective-permute-start(f32[8,128]{1,0:T(8,128)S(1)} %shard_map.114.near), channel_id=1, source_target_pairs={{0,64},{32,96},{64,0},{96,32},{1,65},{33,97},{65,1},{97,33},{2,66}... | collective-permute-start | bytes 12296 | tf_op jit(solution)/shard_map/ppermute | solution.py:461
  53.8 4.5 %collective-permute-start.7 = (f32[8,128]{1,0:T(8,128)S(1)}, f32[8,128]{1,0:T(8,128)S(1)}, u32[]{:S(2)}, u32[]{:S(2)}) collective-permute-start(f32[8,128]{1,0:T(8,128)S(1)} %shard_map.114.near), channel_id=1, source_target_pairs={{0,32},{32,64},{64,96},{96,0},{1,33},{33,65},{65,97},{97,1},{2,34}... | collective-permute-start | bytes 12296 | tf_op jit(solution)/shard_map/ppermute | solution.py:461
  54.6 3.7 %collective-permute-start.6 = (f32[8,128]{1,0:T(8,128)S(1)}, f32[8,128]{1,0:T(8,128)S(1)}, u32[]{:S(2)}, u32[]{:S(2)}) collective-permute-start(f32[8,128]{1,0:T(8,128)S(1)} %shard_map.114.near), channel_id=1, source_target_pairs={{0,96},{32,0},{64,32},{96,64},{1,97},{33,1},{65,33},{97,65},{2,98}... | collective-permute-start | bytes 12296 | tf_op jit(solution)/shard_map/ppermute | solution.py:461
  56.5 0.7 %copy-start.11 = (s32[16]{0:T(128)S(1)}, s32[16]{0:T(128)}, u32[]{:S(2)}) copy-start(s32[16]{0:T(128)} %refs_1_.3) | copy-start | bytes 196

commit v7 on v6

--- a/solution.py
+++ b/solution.py
@@ -152,8 +152,8 @@
 
 
 def maps_kernel(
-    areas, nperf, tiles, pivot, lower, upper, well,
-    send, cross_out, state_out, order, place_out, rest, states, maps, group,
+    areas, nperf, tiles, pivot, lower, upper, well, rhs, guess, diag, couple,
+    send, cross_out, state_out, order, place_out, rest, inner, states, maps, group,
 ):
     place_all, place_own = tile_places(areas, nperf, tiles)
     mine = (iota((areas, LANES), 0) == own_area()) & (place_all >= 0)
@@ -165,6 +165,30 @@
 
     def load(ref, k, h):
         return [ref[c, k, halves[h], :] for c in range(9)]
+
+    row = iota((8, LANES), 0)
+    lane = iota((8, LANES), 1)
+    for k in range(DEPTH):
+        for h in range(2):
+            at = halves[h]
+            mid = [guess[c, k, at, :] for c in range(3)]
+            out = vec(load(diag, k, h), mid)
+            for c in range(3):
+                g = mid[c]
+                if h == 0:
+                    below = jnp.where(row == 0, 0.0, pltpu.roll(g, 1, 0))
+                    above = guess[c, k, 1:9, :]
+                else:
+                    below = guess[c, k, 7:15, :]
+                    above = jnp.where(row == 7, 0.0, pltpu.roll(g, 7, 0))
+                before = jnp.where(lane == 0, 0.0, pltpu.roll(g, 1, 1))
+                after = jnp.where(lane == LANES - 1, 0.0, pltpu.roll(g, LANES - 1, 1))
+                beside = below + above + before + after
+                if k > 0:
+                    beside = beside + guess[c, k - 1, at, :]
+                if k < top:
+                    beside = beside + guess[c, k + 1, at, :]
+                inner[c, k, at, :] = rhs[c, k, at, :] - (out[c] - couple[c, k, at, :] * beside)
 
     state = [None, None]
     for k in range(DEPTH):
@@ -222,7 +246,7 @@
 
 
 def trial_kernel(
-    x_in, right_in, left_in, below_in, above_in, rhs, guess, diag, couple, pivot, lower, upper, well, order, rest, sent,
+    x_in, right_in, left_in, below_in, above_in, inner, couple, pivot, lower, upper, well, order, rest, sent,
     send, trial_out, well_out, forward, ends,
 ):
     region = lax.axis_index("region")
@@ -243,34 +267,21 @@
 
     def residual(k, h):
         at, edge_right, edge_left = halves[h], edges_right[h], edges_left[h]
-        mid = load(guess, k, h, 3)
-        out = vec(load(diag, k, h), mid)
+        out = []
         for c in range(3):
-            g = mid[c]
             place = c * DEPTH + k
             x_row = x_in[place : place + 1, :]
-            if h == 0:
-                outer = jnp.where(region > 0, x_row, 0.0)
-                below = jnp.where(row == 0, outer, pltpu.roll(g, 1, 0))
-                above = guess[c, k, 1:9, :]
-            else:
-                outer = jnp.where(region == 0, x_row, 0.0)
-                below = guess[c, k, 7:15, :]
-                above = jnp.where(row == 7, outer, pltpu.roll(g, 7, 0))
+            outer = jnp.where(region > 0 if h == 0 else region == 0, x_row, 0.0)
+            beside = jnp.where(row == (0 if h == 0 else 7), outer, 0.0)
             first = pltpu.roll(edge_right, LANES - place, 1) if place else edge_right
-            before = jnp.where(lane == 0, first, pltpu.roll(g, 1, 1))
             last = pltpu.roll(edge_left, LANES - 1 - place, 1)
-            after = jnp.where(lane == LANES - 1, last, pltpu.roll(g, LANES - 1, 1))
-            beside = below + above + before + after
-            if k > 0:
-                beside = beside + guess[c, k - 1, at, :]
-            else:
+            ends_y = jnp.where(lane == 0, first, jnp.where(lane == LANES - 1, last, 0.0))
+            beside = beside + ends_y
+            if k == 0:
                 beside = beside + jnp.where(layer > 0, below_in[c, at, :], 0.0)
-            if k < top:
-                beside = beside + guess[c, k + 1, at, :]
-            else:
+            if k == top:
                 beside = beside + jnp.where(layer < n_layer - 1, above_in[c, at, :], 0.0)
-            out[c] = rhs[c, k, at, :] - (out[c] - couple[c, k, at, :] * beside)
+            out.append(inner[c, k, at, :] + couple[c, k, at, :] * beside)
         return out
 
     f = [None, None]
@@ -485,26 +496,27 @@
     x_in = moved(x_face, "region", 1)
     nine, three = f32(9, *cells), f32(3, *cells)
     index = jax.ShapeDtypeStruct((ROWS, LANES), jnp.int32)
-    send, cross, state, order, place, rest = call(
+    send, cross, state, order, place, rest, inner = call(
         lambda *refs: maps_kernel(areas, tiles.shape[0], *refs),
         (
             f32(peers * PACK, LANES), nine, nine, index, index, f32(2, ROWS, LANES),
+            three,
         ),
-        [SMEM] + [VMEM] * 4,
+        [SMEM] + [VMEM] * 8,
         [
             pltpu.VMEM((2, 9, DEPTH, 8, LANES), jnp.float32),
             pltpu.VMEM((45, ROWS, LANES), jnp.float32),
             pltpu.VMEM((ROWS, LANES), jnp.int32),
         ],
         cost=LONG,
-    )(tiles, pivot, lower, upper, well)
+    )(tiles, pivot, lower, upper, well, rhs, guess, diag, couple)
     send, trial, well_sums = call(
         trial_kernel,
         (f32(peers * PACK, LANES), three, f32(8, LANES)),
-        [VMEM] * 16,
+        [VMEM] * 14,
         [pltpu.VMEM((2, 3, DEPTH, 8, LANES), jnp.float32), pltpu.VMEM((6, ROWS, LANES), jnp.float32)],
-        aliases={15: 0},
-    )(x_in, right_in, left_in, below_in, above_in, rhs, guess, diag, couple, pivot, lower, upper, well, order, rest, send)
+        aliases={13: 0},
+    )(x_in, right_in, left_in, below_in, above_in, inner, couple, pivot, lower, upper, well, order, rest, send)
     got = exchanged(send.reshape(peers, PACK, 1, LANES), "layer").reshape(peers * PACK, LANES)
     back = call(
         lambda *refs: chain_kernel(peers, *refs),

time: 59.3 us -> 59.3 us (level)
    unnamed x24 -> x22, local copies, waits for them, and re-layouts: 1.76 us -> 1.76 us
where the time goes in v7:
time: 59.3 us; the launch traced here: 59.1 us
  blocking collectives  31.1 us (52%)
  starting transfers between devices  19.8 us (33%)
  Pallas kernels  5.47 us (9%)
  local copies, waits for them, and re-layouts  1.76 us (3%)
  waiting for transfers between devices  0.84 us (1%)
    all_to_all x2, blocking collectives, exchanged(): return lax.all_to_all(value, axes, split_axis=0, concat_axis=0, tiled=True)  31.1 us
    ppermute x9, starting transfers between devices, moved(): lax.ppermute(value, axis, [(i, (i + by) % count) for i in range(count)])  19.8 us
    pallas_call x1, Pallas kernels, local(): call(lambda *refs: maps_kernel(areas, tiles.shape[0], *refs), (f32(peers...  2.07 us
    unnamed x22, local copies, waits for them, and re-layouts  1.76 us
  transfers between devices with their start and end apart: 9, of which 1 were waited for; matrix products, arithmetic and copies ran while one was open for 0% of the time, Pallas kernels for 5%

profile of v7, /device:TPU:1, one launch (start us, length us, event | category | flops | bytes accessed | tf_op | source)
XLA Modules:
  0.0 59.1 jit_solution(4972007123809506474)
XLA Ops:
  0.0 0.0 copy-start
  0.0 0.0 copy-start.3
  0.0 0.0 copy-start.2
  0.0 0.0 copy-start.1
  0.0 0.0 copy-start.4
  0.0 0.0 copy-start.5
  0.0 0.0 copy-start.6
  0.0 1.1 %copy-done.6 = f32[3,8,16,128]{3,2,1,0:T(8,128)S(1)} copy-done((f32[3,8,16,128]{3,2,1,0:T(8,128)S(1)}, f32[3,8,16,128]{3,2,1,0:T(8,128)}, u32[]{:S(2)}) %copy-start.6) | copy-done | bytes 196632
  1.1 0.0 copy-start.7
  1.1 0.2 shard_map.109
  1.3 2.2 %collective-permute-start.3 = (f32[3,16,128]{2,1,0:T(8,128)S(1)}, f32[3,16,128]{2,1,0:T(8,128)S(1)}, u32[]{:S(2)}, u32[]{:S(2)}) collective-permute-start(f32[3,16,128]{2,1,0:T(8,128)S(1)} %get-tuple-element.26), channel_id=1, source_target_pairs={{0,1},{1,2},{2,3},{3,4},{4,5},{5,6},{6,7},{7,8},{8,9},{9,10},{10,1... | collective-permute-start | bytes 73736 | tf_op jit(solution)/shard_map/ppermute | solution.py:472
  3.5 6.8 %collective-permute-start.4 = (f32[3,16,128]{2,1,0:T(8,128)S(1)}, f32[3,16,128]{2,1,0:T(8,128)S(1)}, u32[]{:S(2)}, u32[]{:S(2)}) collective-permute-start(f32[3,16,128]{2,1,0:T(8,128)S(1)} %get-tuple-element.27), channel_id=1, source_target_pairs={{0,31},{1,0},{2,1},{3,2},{4,3},{5,4},{6,5},{7,6},{8,7},{9,8},{10,9... | collective-permute-start | bytes 73736 | tf_op jit(solution)/shard_map/ppermute | solution.py:472
  10.3 1.0 %collective-permute-start = (f32[24,128]{1,0:T(8,128)S(1)}, f32[24,128]{1,0:T(8,128)S(1)}, u32[]{:S(2)}, u32[]{:S(2)}) collective-permute-start(f32[24,128]{1,0:T(8,128)S(1)} %get-tuple-element.23), channel_id=1, source_target_pairs={{0,128},{128,0},{1,129},{129,1},{2,130},{130,2},{3,131},{131,3},{4... | collective-permute-start | bytes 36872 | tf_op jit(solution)/shard_map/ppermute | solution.py:472
  11.3 0.0 copy-start.9
  11.3 1.2 %collective-permute-start.1 = (f32[16,128]{1,0:T(8,128)S(1)}, f32[16,128]{1,0:T(8,128)S(1)}, u32[]{:S(2)}, u32[]{:S(2)}) collective-permute-start(f32[16,128]{1,0:T(8,128)S(1)} %get-tuple-element.24), channel_id=1, source_target_pairs={{0,32},{32,64},{64,96},{96,0},{1,33},{33,65},{65,97},{97,1},{2,34}... | collective-permute-start | bytes 24584 | tf_op jit(solution)/shard_map/ppermute | solution.py:472
  12.5 1.5 %collective-permute-start.2 = (f32[16,128]{1,0:T(8,128)S(1)}, f32[16,128]{1,0:T(8,128)S(1)}, u32[]{:S(2)}, u32[]{:S(2)}) collective-permute-start(f32[16,128]{1,0:T(8,128)S(1)} %get-tuple-element.25), channel_id=1, source_target_pairs={{0,96},{32,0},{64,32},{96,64},{1,97},{33,1},{65,33},{97,65},{2,98}... | collective-permute-start | bytes 24584 | tf_op jit(solution)/shard_map/ppermute | solution.py:472
  13.9 0.0 copy-done
  13.9 0.0 copy-done.3
  13.9 0.0 copy-done.2
  13.9 0.0 copy-done.1
  14.0 0.0 copy-done.4
  14.0 0.0 copy-done.5
  14.0 0.0 copy-done.7
  14.0 0.0 copy-done.9
  14.0 2.1 %shard_map.110 = (f32[608,128]{1,0:T(8,128)S(1)}, f32[9,8,16,128]{3,2,1,0:T(8,128)S(1)}, f32[9,8,16,128]{3,2,1,0:T(8,128)S(1)}, s32[16,128]{1,0:T(8,128)S(1)}, s...) custom-call(s32[32]{0:T(128)S(1)} %copy-done.9, f32[9,8,16,128]{3,2,1,0:T(8,128)S(1)} %copy-done.1, ...), custom_call_target="tpu_custom_call" | custom-call | flops 20000000 | bytes 8000000 | tf_op jit(solution)/shard_map/pallas_call | solution.py:499
  16.1 0.0 collective-permute-done.1.right_in
  16.1 0.0 collective-permute-done.2.left_in
  16.1 0.0 collective-permute-done.x_in
  16.1 0.0 collective-permute-done.3.below_in
  16.1 0.0 collective-permute-done.4.above_in
  16.1 0.5 shard_map.111
  16.6 17.6 %all_to_all.10 = f32[32,19,1,128]{3,2,1,0:T(1,128)S(1)} all-to-all(f32[32,19,1,128]{3,2,1,0:T(1,128)S(1)} %bitcast.6), channel_id=1, replica_groups=mesh['region'=2,'column'=4,'layer'=32] {'layer'}, dimensions={0} | all-to-all | bytes 622592 | tf_op jit(solution)/shard_map/all_to_all | solution.py:476
  34.3 0.8 %shard_map.112 = f32[128,128]{1,0:T(8,128)S(1)} custom-call(f32[608,128]{1,0:T(8,128)S(1)} %bitcast.7, f32[8,128]{1,0:T(8,128)S(1)} %get-tuple-element.33.refs_1_, s32[16,128]{1,0:T(8,128)S(1)} %get-tuple-element.29.order.refs_2_), custom_call_target="tpu_custom_call" | custom-call | tf_op jit(solution)/shard_map/pallas_call | solution.py:521
  35.1 13.5 %all_to_all.11 = f32[32,4,1,128]{3,1,2,0:T(4,128)S(1)} all-to-all(f32[32,4,1,128]{3,1,2,0:T(4,128)S(1)} %bitcast.10), channel_id=1, replica_groups=mesh['region'=2,'column'=4,'layer'=32] {'layer'}, dimensions={0} | all-to-all | bytes 131072 | tf_op jit(solution)/shard_map/all_to_all | solution.py:476
  48.6 0.0 copy-start.8
  48.6 2.9 %collective-permute-start.5 = (f32[8,128]{1,0:T(8,128)S(1)}, f32[8,128]{1,0:T(8,128)S(1)}, u32[]{:S(2)}, u32[]{:S(2)}) collective-permute-start(f32[8,128]{1,0:T(8,128)S(1)} %shard_map.113.mine), channel_id=1, source_target_pairs={{0,128},{128,0},{1,129},{129,1},{2,130},{130,2},{3,131},{131,3},{4... | collective-permute-start | bytes 12296 | tf_op jit(solution)/shard_map/ppermute | solution.py:472
  51.4 0.8 %collective-permute-done.5.other = f32[8,128]{1,0:T(8,128)S(1)} collective-permute-done((f32[8,128]{1,0:T(8,128)S(1)}, f32[8,128]{1,0:T(8,128)S(1)}, u32[]{:S(2)}, u32[]{:S(2)}) %collective-permute-start.5) | collective-permute-done | bytes 4128 | tf_op jit(solution)/shard_map/ppermute | solution.py:472
  52.2 1.6 %collective-permute-start.8 = (f32[8,128]{1,0:T(8,128)S(1)}, f32[8,128]{1,0:T(8,128)S(1)}, u32[]{:S(2)}, u32[]{:S(2)}) collective-permute-start(f32[8,128]{1,0:T(8,128)S(1)} %shard_map.114.near), channel_id=1, source_target_pairs={{0,64},{32,96},{64,0},{96,32},{1,65},{33,97},{65,1},{97,33},{2,66}... | collective-permute-start | bytes 12296 | tf_op jit(solution)/shard_map/ppermute | solution.py:472
  53.8 0.5 collective-permute-start.7
  54.3 2.2 %collective-permute-start.6 = (f32[8,128]{1,0:T(8,128)S(1)}, f32[8,128]{1,0:T(8,128)S(1)}, u32[]{:S(2)}, u32[]{:S(2)}) collective-permute-start(f32[8,128]{1,0:T(8,128)S(1)} %shard_map.114.near), channel_id=1, source_target_pairs={{0,96},{32,0},{64,32},{96,64},{1,97},{33,1},{65,33},{97,65},{2,98}... | collective-permute-start | bytes 12296 | tf_op jit(solution)/shard_map/ppermute | solution.py:472
  56.5 0.0 copy-start.10
  56.5 0.0 copy-done.8
  56.5 0.7 %copy-done.10 = s32[16]{0:T(128)S(1)} copy-done((s32[16]{0:T(128)S(1)}, s32[16]{0:T(128)}, u32[]{:S(2)}) %copy-start.10) | copy-done | bytes 88
  57.2 1.1 %shard_map.115 = (f32[3,8,16,128]{3,2,1,0:T(8,128)S(1)}, f32[8,16,128]{2,1,0:T(8,128)S(1)}, f32[9,16,128]{2,1,0:T(8,128)S(1)}) custom-call(s32[32]{0:T(128)S(1)} %copy-done.9, s32[16]{0:T(128)S(1)} %copy-done.10, f32[9,16]{1,0:T(8,128)S(1)} %copy-done.8, f32[128,128]{1,0:T(8,128)S(1)} %bitcast.9, f32[9,8,16,128]{3,2,1,0:T(8,128)S(1)} %get-tuple-element.34.refs_4_, ...), custom_call_target="tpu_custom_call" | custom-call | flops 20000000 | bytes 8000000 | tf_op jit(solution)/shard_map/pallas_call | solution.py:535
  58.3 0.0 collective-permute-done.8.across
  58.3 0.0 collective-permute-done.7.before
  58.3 0.0 collective-permute-done.6.after
  58.3 0.8 %shard_map.116 = f32[3,8,16,128]{3,2,1,0:T(8,128)} custom-call(f32[8,128]{1,0:T(8,128)S(1)} %shard_map.114.near, f32[8,128]{1,0:T(8,128)S(1)} %collective-permute-done.6.after, f32[8,128]{1,0:T(8,128)S(1)} %collective-permute-done.7.before, f32[8,128]{1,0:T(8,128)S(1)} %collective-permute-done.8.across, f32[8,16,128]{2,1,0:T(8,128)S(1)} %get-tuple-element.38.same, ...), custom_call_target="tpu_custom_call" | custom-call | tf_op jit(solution)/shard_map/pallas_call | solution.py:542
  (2 shorter events, 0.0 us)
Async XLA Ops:
  0.0 13.9 %copy-start = (f32[9,8,16,128]{3,2,1,0:T(8,128)S(1)}, f32[9,8,16,128]{3,2,1,0:T(8,128)}, u32[]{:S(2)}) copy-start(f32[9,8,16,128]{3,2,1,0:T(8,128)} %well.3) | copy-start | bytes 1769476
  0.0 13.9 %copy-start.3 = (f32[9,8,16,128]{3,2,1,0:T(8,128)S(1)}, f32[9,8,16,128]{3,2,1,0:T(8,128)}, u32[]{:S(2)}) copy-start(f32[9,8,16,128]{3,2,1,0:T(8,128)} %upper.1) | copy-start | bytes 1769476
  0.0 13.9 %copy-start.2 = (f32[9,8,16,128]{3,2,1,0:T(8,128)S(1)}, f32[9,8,16,128]{3,2,1,0:T(8,128)}, u32[]{:S(2)}) copy-start(f32[9,8,16,128]{3,2,1,0:T(8,128)} %lower.1) | copy-start | bytes 1769476
  0.0 13.9 %copy-start.1 = (f32[9,8,16,128]{3,2,1,0:T(8,128)S(1)}, f32[9,8,16,128]{3,2,1,0:T(8,128)}, u32[]{:S(2)}) copy-start(f32[9,8,16,128]{3,2,1,0:T(8,128)} %pivot.1) | copy-start | bytes 1769476
  0.0 13.9 %copy-start.4 = (f32[3,8,16,128]{3,2,1,0:T(8,128)S(1)}, f32[3,8,16,128]{3,2,1,0:T(8,128)}, u32[]{:S(2)}) copy-start(f32[3,8,16,128]{3,2,1,0:T(8,128)} %couple.1) | copy-start | bytes 589828
  0.0 13.9 %copy-start.5 = (f32[9,8,16,128]{3,2,1,0:T(8,128)S(1)}, f32[9,8,16,128]{3,2,1,0:T(8,128)}, u32[]{:S(2)}) copy-start(f32[9,8,16,128]{3,2,1,0:T(8,128)} %refs_7_.1) | copy-start | bytes 1769476
  0.0 1.1 %copy-start.6 = (f32[3,8,16,128]{3,2,1,0:T(8,128)S(1)}, f32[3,8,16,128]{3,2,1,0:T(8,128)}, u32[]{:S(2)}) copy-start(f32[3,8,16,128]{3,2,1,0:T(8,128)} %refs_6_.1) | copy-start | bytes 589828
  1.1 12.9 %copy-start.7 = (f32[3,8,16,128]{3,2,1,0:T(8,128)S(1)}, f32[3,8,16,128]{3,2,1,0:T(8,128)}, u32[]{:S(2)}) copy-start(f32[3,8,16,128]{3,2,1,0:T(8,128)} %refs_5_.1) | copy-start | bytes 589828
  1.3 14.8 %collective-permute-start.3 = (f32[3,16,128]{2,1,0:T(8,128)S(1)}, f32[3,16,128]{2,1,0:T(8,128)S(1)}, u32[]{:S(2)}, u32[]{:S(2)}) collective-permute-start(f32[3,16,128]{2,1,0:T(8,128)S(1)} %get-tuple-element.26), channel_id=1, source_target_pairs={{0,1},{1,2},{2,3},{3,4},{4,5},{5,6},{6,7},{7,8},{8,9},{9,10},{10,1... | collective-permute-start | bytes 73736 | tf_op jit(solution)/shard_map/ppermute | solution.py:472
  3.5 12.6 %collective-permute-start.4 = (f32[3,16,128]{2,1,0:T(8,128)S(1)}, f32[3,16,128]{2,1,0:T(8,128)S(1)}, u32[]{:S(2)}, u32[]{:S(2)}) collective-permute-start(f32[3,16,128]{2,1,0:T(8,128)S(1)} %get-tuple-element.27), channel_id=1, source_target_pairs={{0,31},{1,0},{2,1},{3,2},{4,3},{5,4},{6,5},{7,6},{8,7},{9,8},{10,9... | collective-permute-start | bytes 73736 | tf_op jit(solution)/shard_map/ppermute | solution.py:472
  10.3 5.8 %collective-permute-start = (f32[24,128]{1,0:T(8,128)S(1)}, f32[24,128]{1,0:T(8,128)S(1)}, u32[]{:S(2)}, u32[]{:S(2)}) collective-permute-start(f32[24,128]{1,0:T(8,128)S(1)} %get-tuple-element.23), channel_id=1, source_target_pairs={{0,128},{128,0},{1,129},{129,1},{2,130},{130,2},{3,131},{131,3},{4... | collective-permute-start | bytes 36872 | tf_op jit(solution)/shard_map/ppermute | solution.py:472
  11.3 2.7 %copy-start.9 = (s32[32]{0:T(128)S(1)}, s32[32]{0:T(128)}, u32[]{:S(2)}) copy-start(s32[32]{0:T(128)} %refs_0_.3) | copy-start | bytes 388
  11.3 4.8 %collective-permute-start.1 = (f32[16,128]{1,0:T(8,128)S(1)}, f32[16,128]{1,0:T(8,128)S(1)}, u32[]{:S(2)}, u32[]{:S(2)}) collective-permute-start(f32[16,128]{1,0:T(8,128)S(1)} %get-tuple-element.24), channel_id=1, source_target_pairs={{0,32},{32,64},{64,96},{96,0},{1,33},{33,65},{65,97},{97,1},{2,34}... | collective-permute-start | bytes 24584 | tf_op jit(solution)/shard_map/ppermute | solution.py:472
  12.5 3.6 %collective-permute-start.2 = (f32[16,128]{1,0:T(8,128)S(1)}, f32[16,128]{1,0:T(8,128)S(1)}, u32[]{:S(2)}, u32[]{:S(2)}) collective-permute-start(f32[16,128]{1,0:T(8,128)S(1)} %get-tuple-element.25), channel_id=1, source_target_pairs={{0,96},{32,0},{64,32},{96,64},{1,97},{33,1},{65,33},{97,65},{2,98}... | collective-permute-start | bytes 24584 | tf_op jit(solution)/shard_map/ppermute | solution.py:472
  48.6 8.0 %copy-start.8 = (f32[9,16]{1,0:T(8,128)S(1)}, f32[9,16]{1,0:T(8,128)}, u32[]{:S(2)}) copy-start(f32[9,16]{1,0:T(8,128)} %refs_2_.3) | copy-start | bytes 1732
  48.6 3.7 %collective-permute-start.5 = (f32[8,128]{1,0:T(8,128)S(1)}, f32[8,128]{1,0:T(8,128)S(1)}, u32[]{:S(2)}, u32[]{:S(2)}) collective-permute-start(f32[8,128]{1,0:T(8,128)S(1)} %shard_map.113.mine), channel_id=1, source_target_pairs={{0,128},{128,0},{1,129},{129,1},{2,130},{130,2},{3,131},{131,3},{4... | collective-permute-start | bytes 12296 | tf_op jit(solution)/shard_map/ppermute | solution.py:472
  52.2 6.0 %collective-permute-start.8 = (f32[8,128]{1,0:T(8,128)S(1)}, f32[8,128]{1,0:T(8,128)S(1)}, u32[]{:S(2)}, u32[]{:S(2)}) collective-permute-start(f32[8,128]{1,0:T(8,128)S(1)} %shard_map.114.near), channel_id=1, source_target_pairs={{0,64},{32,96},{64,0},{96,32},{1,65},{33,97},{65,1},{97,33},{2,66}... | collective-permute-start | bytes 12296 | tf_op jit(solution)/shard_map/ppermute | solution.py:472
  53.8 4.5 %collective-permute-start.7 = (f32[8,128]{1,0:T(8,128)S(1)}, f32[8,128]{1,0:T(8,128)S(1)}, u32[]{:S(2)}, u32[]{:S(2)}) collective-permute-start(f32[8,128]{1,0:T(8,128)S(1)} %shard_map.114.near), channel_id=1, source_target_pairs={{0,32},{32,64},{64,96},{96,0},{1,33},{33,65},{65,97},{97,1},{2,34}... | collective-permute-start | bytes 12296 | tf_op jit(solution)/shard_map/ppermute | solution.py:472
  54.3 4.0 %collective-permute-start.6 = (f32[8,128]{1,0:T(8,128)S(1)}, f32[8,128]{1,0:T(8,128)S(1)}, u32[]{:S(2)}, u32[]{:S(2)}) collective-permute-start(f32[8,128]{1,0:T(8,128)S(1)} %shard_map.114.near), channel_id=1, source_target_pairs={{0,96},{32,0},{64,32},{96,64},{1,97},{33,1},{65,33},{97,65},{2,98}... | collective-permute-start | bytes 12296 | tf_op jit(solution)/shard_map/ppermute | solution.py:472
  56.5 0.7 %copy-start.10 = (s32[16]{0:T(128)S(1)}, s32[16]{0:T(128)}, u32[]{:S(2)}) copy-start(s32[16]{0:T(128)} %refs_1_.3) | copy-start | bytes 196

commit v8 on v7

--- a/solution.py
+++ b/solution.py
@@ -382,7 +382,7 @@
 
 def sums_kernel(peers, got, sums):
     total = jnp.sum(got[pl.ds(3, peers, BACK), :], axis=0, keepdims=True)
-    sums[...] = jnp.broadcast_to(total, (8, LANES))
+    sums[...] = total
 
 
 def solved_kernel(
@@ -411,8 +411,8 @@
 
 def pair_kernel(mine, other, out):
     region = lax.axis_index("region")
-    out[0:1, :] = jnp.where(region == 0, mine[0:1, :], other[0:1, :])
-    out[1:8, :] = jnp.where(region == 0, other[1:8, :], mine[1:8, :])
+    out[0:1, :] = jnp.where(region == 0, mine[...], other[...])
+    out[1:2, :] = jnp.where(region == 0, other[...], mine[...])
 
 
 def wells_kernel(near, after, before, across, same, block, solved, well, out, held, sems):
@@ -529,8 +529,8 @@
         ],
     )(got, well_sums, order)
     got = exchanged(back.reshape(peers, BACK, 1, LANES), "layer").reshape(peers * BACK, LANES)
-    sums = call(lambda *refs: sums_kernel(peers, *refs), f32(8, LANES), [VMEM])(got)
-    near = call(pair_kernel, f32(8, LANES), [VMEM] * 2)(sums, moved(sums, "region", 1))
+    sums = call(lambda *refs: sums_kernel(peers, *refs), f32(1, LANES), [VMEM])(got)
+    near = call(pair_kernel, f32(2, LANES), [VMEM] * 2)(sums, moved(sums, "region", 1))
     after, before, across = [moved(near, "column", by) for by in (-1, 1, 2)]
     solved, same, block = call(
         lambda *refs: solved_kernel(areas, tiles.shape[0], counts.shape[0], *refs),

time: 59.3 us -> 59.3 us (level)
  no operation moved by 1% of the time
where the time goes in v8:
time: 59.3 us; the launch traced here: 59.1 us
  blocking collectives  31.1 us (52%)
  starting transfers between devices  19.8 us (33%)
  Pallas kernels  5.47 us (9%)
  local copies, waits for them, and re-layouts  1.76 us (3%)
  waiting for transfers between devices  0.84 us (1%)
    all_to_all x2, blocking collectives, exchanged(): return lax.all_to_all(value, axes, split_axis=0, concat_axis=0, tiled=True)  31.1 us
    ppermute x9, starting transfers between devices, moved(): lax.ppermute(value, axis, [(i, (i + by) % count) for i in range(count)])  19.8 us
    pallas_call x1, Pallas kernels, local(): call(lambda *refs: maps_kernel(areas, tiles.shape[0], *refs), (f32(peers...  2.07 us
    unnamed x22, local copies, waits for them, and re-layouts  1.76 us
  transfers between devices with their start and end apart: 9, of which 1 were waited for; matrix products, arithmetic and copies ran while one was open for 0% of the time, Pallas kernels for 5%

profile of v8, /device:TPU:1, one launch (start us, length us, event | category | flops | bytes accessed | tf_op | source)
XLA Modules:
  0.0 59.1 jit_solution(4930387013744589965)
XLA Ops:
  0.0 0.0 copy-start
  0.0 0.0 copy-start.3
  0.0 0.0 copy-start.2
  0.0 0.0 copy-start.1
  0.0 0.0 copy-start.4
  0.0 0.0 copy-start.5
  0.0 0.0 copy-start.6
  0.0 1.1 %copy-done.6 = f32[3,8,16,128]{3,2,1,0:T(8,128)S(1)} copy-done((f32[3,8,16,128]{3,2,1,0:T(8,128)S(1)}, f32[3,8,16,128]{3,2,1,0:T(8,128)}, u32[]{:S(2)}) %copy-start.6) | copy-done | bytes 196632
  1.1 0.0 copy-start.7
  1.1 0.2 shard_map.109
  1.3 2.2 %collective-permute-start.3 = (f32[3,16,128]{2,1,0:T(8,128)S(1)}, f32[3,16,128]{2,1,0:T(8,128)S(1)}, u32[]{:S(2)}, u32[]{:S(2)}) collective-permute-start(f32[3,16,128]{2,1,0:T(8,128)S(1)} %get-tuple-element.26), channel_id=1, source_target_pairs={{0,1},{1,2},{2,3},{3,4},{4,5},{5,6},{6,7},{7,8},{8,9},{9,10},{10,1... | collective-permute-start | bytes 73736 | tf_op jit(solution)/shard_map/ppermute | solution.py:472
  3.5 6.8 %collective-permute-start.4 = (f32[3,16,128]{2,1,0:T(8,128)S(1)}, f32[3,16,128]{2,1,0:T(8,128)S(1)}, u32[]{:S(2)}, u32[]{:S(2)}) collective-permute-start(f32[3,16,128]{2,1,0:T(8,128)S(1)} %get-tuple-element.27), channel_id=1, source_target_pairs={{0,31},{1,0},{2,1},{3,2},{4,3},{5,4},{6,5},{7,6},{8,7},{9,8},{10,9... | collective-permute-start | bytes 73736 | tf_op jit(solution)/shard_map/ppermute | solution.py:472
  10.3 1.0 %collective-permute-start = (f32[24,128]{1,0:T(8,128)S(1)}, f32[24,128]{1,0:T(8,128)S(1)}, u32[]{:S(2)}, u32[]{:S(2)}) collective-permute-start(f32[24,128]{1,0:T(8,128)S(1)} %get-tuple-element.23), channel_id=1, source_target_pairs={{0,128},{128,0},{1,129},{129,1},{2,130},{130,2},{3,131},{131,3},{4... | collective-permute-start | bytes 36872 | tf_op jit(solution)/shard_map/ppermute | solution.py:472
  11.3 0.0 copy-start.9
  11.3 1.2 %collective-permute-start.1 = (f32[16,128]{1,0:T(8,128)S(1)}, f32[16,128]{1,0:T(8,128)S(1)}, u32[]{:S(2)}, u32[]{:S(2)}) collective-permute-start(f32[16,128]{1,0:T(8,128)S(1)} %get-tuple-element.24), channel_id=1, source_target_pairs={{0,32},{32,64},{64,96},{96,0},{1,33},{33,65},{65,97},{97,1},{2,34}... | collective-permute-start | bytes 24584 | tf_op jit(solution)/shard_map/ppermute | solution.py:472
  12.5 1.5 %collective-permute-start.2 = (f32[16,128]{1,0:T(8,128)S(1)}, f32[16,128]{1,0:T(8,128)S(1)}, u32[]{:S(2)}, u32[]{:S(2)}) collective-permute-start(f32[16,128]{1,0:T(8,128)S(1)} %get-tuple-element.25), channel_id=1, source_target_pairs={{0,96},{32,0},{64,32},{96,64},{1,97},{33,1},{65,33},{97,65},{2,98}... | collective-permute-start | bytes 24584 | tf_op jit(solution)/shard_map/ppermute | solution.py:472
  13.9 0.0 copy-done
  13.9 0.0 copy-done.3
  13.9 0.0 copy-done.2
  13.9 0.0 copy-done.1
  14.0 0.0 copy-done.4
  14.0 0.0 copy-done.5
  14.0 0.0 copy-done.7
  14.0 0.0 copy-done.9
  14.0 2.1 %shard_map.110 = (f32[608,128]{1,0:T(8,128)S(1)}, f32[9,8,16,128]{3,2,1,0:T(8,128)S(1)}, f32[9,8,16,128]{3,2,1,0:T(8,128)S(1)}, s32[16,128]{1,0:T(8,128)S(1)}, s...) custom-call(s32[32]{0:T(128)S(1)} %copy-done.9, f32[9,8,16,128]{3,2,1,0:T(8,128)S(1)} %copy-done.1, ...), custom_call_target="tpu_custom_call" | custom-call | flops 20000000 | bytes 8000000 | tf_op jit(solution)/shard_map/pallas_call | solution.py:499
  16.1 0.0 collective-permute-done.1.right_in
  16.1 0.0 collective-permute-done.2.left_in
  16.1 0.0 collective-permute-done.x_in
  16.1 0.0 collective-permute-done.3.below_in
  16.1 0.0 collective-permute-done.4.above_in
  16.1 0.5 shard_map.111
  16.6 17.6 %all_to_all.10 = f32[32,19,1,128]{3,2,1,0:T(1,128)S(1)} all-to-all(f32[32,19,1,128]{3,2,1,0:T(1,128)S(1)} %bitcast.6), channel_id=1, replica_groups=mesh['region'=2,'column'=4,'layer'=32] {'layer'}, dimensions={0} | all-to-all | bytes 622592 | tf_op jit(solution)/shard_map/all_to_all | solution.py:476
  34.3 0.8 %shard_map.112 = f32[128,128]{1,0:T(8,128)S(1)} custom-call(f32[608,128]{1,0:T(8,128)S(1)} %bitcast.7, f32[8,128]{1,0:T(8,128)S(1)} %get-tuple-element.33.refs_1_, s32[16,128]{1,0:T(8,128)S(1)} %get-tuple-element.29.order.refs_2_), custom_call_target="tpu_custom_call" | custom-call | tf_op jit(solution)/shard_map/pallas_call | solution.py:521
  35.1 13.5 %all_to_all.11 = f32[32,4,1,128]{3,1,2,0:T(4,128)S(1)} all-to-all(f32[32,4,1,128]{3,1,2,0:T(4,128)S(1)} %bitcast.10), channel_id=1, replica_groups=mesh['region'=2,'column'=4,'layer'=32] {'layer'}, dimensions={0} | all-to-all | bytes 131072 | tf_op jit(solution)/shard_map/all_to_all | solution.py:476
  48.6 0.0 copy-start.8
  48.6 2.9 %collective-permute-start.5 = (f32[1,128]{1,0:T(1,128)S(1)}, f32[1,128]{1,0:T(1,128)S(1)}, u32[]{:S(2)}, u32[]{:S(2)}) collective-permute-start(f32[1,128]{1,0:T(1,128)S(1)} %shard_map.113.mine), channel_id=1, source_target_pairs={{0,128},{128,0},{1,129},{129,1},{2,130},{130,2},{3,131},{131,3},{4... | collective-permute-start | bytes 1544 | tf_op jit(solution)/shard_map/ppermute | solution.py:472
  51.4 0.8 %collective-permute-done.5.other = f32[1,128]{1,0:T(1,128)S(1)} collective-permute-done((f32[1,128]{1,0:T(1,128)S(1)}, f32[1,128]{1,0:T(1,128)S(1)}, u32[]{:S(2)}, u32[]{:S(2)}) %collective-permute-start.5) | collective-permute-done | bytes 544 | tf_op jit(solution)/shard_map/ppermute | solution.py:472
  52.2 1.6 %collective-permute-start.8 = (f32[2,128]{1,0:T(2,128)S(1)}, f32[2,128]{1,0:T(2,128)S(1)}, u32[]{:S(2)}, u32[]{:S(2)}) collective-permute-start(f32[2,128]{1,0:T(2,128)S(1)} %shard_map.114.near), channel_id=1, source_target_pairs={{0,64},{32,96},{64,0},{96,32},{1,65},{33,97},{65,1},{97,33},{2,66}... | collective-permute-start | bytes 3080 | tf_op jit(solution)/shard_map/ppermute | solution.py:472
  53.8 0.5 collective-permute-start.7
  54.3 2.2 %collective-permute-start.6 = (f32[2,128]{1,0:T(2,128)S(1)}, f32[2,128]{1,0:T(2,128)S(1)}, u32[]{:S(2)}, u32[]{:S(2)}) collective-permute-start(f32[2,128]{1,0:T(2,128)S(1)} %shard_map.114.near), channel_id=1, source_target_pairs={{0,96},{32,0},{64,32},{96,64},{1,97},{33,1},{65,33},{97,65},{2,98}... | collective-permute-start | bytes 3080 | tf_op jit(solution)/shard_map/ppermute | solution.py:472
  56.5 0.0 copy-start.10
  56.5 0.0 copy-done.8
  56.5 0.7 %copy-done.10 = s32[16]{0:T(128)S(1)} copy-done((s32[16]{0:T(128)S(1)}, s32[16]{0:T(128)}, u32[]{:S(2)}) %copy-start.10) | copy-done | bytes 88
  57.2 1.1 %shard_map.115 = (f32[3,8,16,128]{3,2,1,0:T(8,128)S(1)}, f32[8,16,128]{2,1,0:T(8,128)S(1)}, f32[9,16,128]{2,1,0:T(8,128)S(1)}) custom-call(s32[32]{0:T(128)S(1)} %copy-done.9, s32[16]{0:T(128)S(1)} %copy-done.10, f32[9,16]{1,0:T(8,128)S(1)} %copy-done.8, f32[128,128]{1,0:T(8,128)S(1)} %bitcast.9, f32[9,8,16,128]{3,2,1,0:T(8,128)S(1)} %get-tuple-element.34.refs_4_, ...), custom_call_target="tpu_custom_call" | custom-call | flops 20000000 | bytes 8000000 | tf_op jit(solution)/shard_map/pallas_call | solution.py:535
  58.3 0.0 collective-permute-done.8.across
  58.3 0.0 collective-permute-done.7.before
  58.3 0.0 collective-permute-done.6.after
  58.3 0.8 %shard_map.116 = f32[3,8,16,128]{3,2,1,0:T(8,128)} custom-call(f32[2,128]{1,0:T(2,128)S(1)} %shard_map.114.near, f32[2,128]{1,0:T(2,128)S(1)} %collective-permute-done.6.after, f32[2,128]{1,0:T(2,128)S(1)} %collective-permute-done.7.before, f32[2,128]{1,0:T(2,128)S(1)} %collective-permute-done.8.across, f32[8,16,128]{2,1,0:T(8,128)S(1)} %get-tuple-element.38.same, ...), custom_call_target="tpu_custom_call" | custom-call | tf_op jit(solution)/shard_map/pallas_call | solution.py:542
  (2 shorter events, 0.0 us)
Async XLA Ops:
  0.0 13.9 %copy-start = (f32[9,8,16,128]{3,2,1,0:T(8,128)S(1)}, f32[9,8,16,128]{3,2,1,0:T(8,128)}, u32[]{:S(2)}) copy-start(f32[9,8,16,128]{3,2,1,0:T(8,128)} %well.3) | copy-start | bytes 1769476
  0.0 13.9 %copy-start.3 = (f32[9,8,16,128]{3,2,1,0:T(8,128)S(1)}, f32[9,8,16,128]{3,2,1,0:T(8,128)}, u32[]{:S(2)}) copy-start(f32[9,8,16,128]{3,2,1,0:T(8,128)} %upper.1) | copy-start | bytes 1769476
  0.0 13.9 %copy-start.2 = (f32[9,8,16,128]{3,2,1,0:T(8,128)S(1)}, f32[9,8,16,128]{3,2,1,0:T(8,128)}, u32[]{:S(2)}) copy-start(f32[9,8,16,128]{3,2,1,0:T(8,128)} %lower.1) | copy-start | bytes 1769476
  0.0 13.9 %copy-start.1 = (f32[9,8,16,128]{3,2,1,0:T(8,128)S(1)}, f32[9,8,16,128]{3,2,1,0:T(8,128)}, u32[]{:S(2)}) copy-start(f32[9,8,16,128]{3,2,1,0:T(8,128)} %pivot.1) | copy-start | bytes 1769476
  0.0 13.9 %copy-start.4 = (f32[3,8,16,128]{3,2,1,0:T(8,128)S(1)}, f32[3,8,16,128]{3,2,1,0:T(8,128)}, u32[]{:S(2)}) copy-start(f32[3,8,16,128]{3,2,1,0:T(8,128)} %couple.1) | copy-start | bytes 589828
  0.0 13.9 %copy-start.5 = (f32[9,8,16,128]{3,2,1,0:T(8,128)S(1)}, f32[9,8,16,128]{3,2,1,0:T(8,128)}, u32[]{:S(2)}) copy-start(f32[9,8,16,128]{3,2,1,0:T(8,128)} %refs_7_.1) | copy-start | bytes 1769476
  0.0 1.1 %copy-start.6 = (f32[3,8,16,128]{3,2,1,0:T(8,128)S(1)}, f32[3,8,16,128]{3,2,1,0:T(8,128)}, u32[]{:S(2)}) copy-start(f32[3,8,16,128]{3,2,1,0:T(8,128)} %refs_6_.1) | copy-start | bytes 589828
  1.1 12.9 %copy-start.7 = (f32[3,8,16,128]{3,2,1,0:T(8,128)S(1)}, f32[3,8,16,128]{3,2,1,0:T(8,128)}, u32[]{:S(2)}) copy-start(f32[3,8,16,128]{3,2,1,0:T(8,128)} %refs_5_.1) | copy-start | bytes 589828
  1.3 14.8 %collective-permute-start.3 = (f32[3,16,128]{2,1,0:T(8,128)S(1)}, f32[3,16,128]{2,1,0:T(8,128)S(1)}, u32[]{:S(2)}, u32[]{:S(2)}) collective-permute-start(f32[3,16,128]{2,1,0:T(8,128)S(1)} %get-tuple-element.26), channel_id=1, source_target_pairs={{0,1},{1,2},{2,3},{3,4},{4,5},{5,6},{6,7},{7,8},{8,9},{9,10},{10,1... | collective-permute-start | bytes 73736 | tf_op jit(solution)/shard_map/ppermute | solution.py:472
  3.5 12.6 %collective-permute-start.4 = (f32[3,16,128]{2,1,0:T(8,128)S(1)}, f32[3,16,128]{2,1,0:T(8,128)S(1)}, u32[]{:S(2)}, u32[]{:S(2)}) collective-permute-start(f32[3,16,128]{2,1,0:T(8,128)S(1)} %get-tuple-element.27), channel_id=1, source_target_pairs={{0,31},{1,0},{2,1},{3,2},{4,3},{5,4},{6,5},{7,6},{8,7},{9,8},{10,9... | collective-permute-start | bytes 73736 | tf_op jit(solution)/shard_map/ppermute | solution.py:472
  10.3 5.8 %collective-permute-start = (f32[24,128]{1,0:T(8,128)S(1)}, f32[24,128]{1,0:T(8,128)S(1)}, u32[]{:S(2)}, u32[]{:S(2)}) collective-permute-start(f32[24,128]{1,0:T(8,128)S(1)} %get-tuple-element.23), channel_id=1, source_target_pairs={{0,128},{128,0},{1,129},{129,1},{2,130},{130,2},{3,131},{131,3},{4... | collective-permute-start | bytes 36872 | tf_op jit(solution)/shard_map/ppermute | solution.py:472
  11.3 2.7 %copy-start.9 = (s32[32]{0:T(128)S(1)}, s32[32]{0:T(128)}, u32[]{:S(2)}) copy-start(s32[32]{0:T(128)} %refs_0_.3) | copy-start | bytes 388
  11.3 4.8 %collective-permute-start.1 = (f32[16,128]{1,0:T(8,128)S(1)}, f32[16,128]{1,0:T(8,128)S(1)}, u32[]{:S(2)}, u32[]{:S(2)}) collective-permute-start(f32[16,128]{1,0:T(8,128)S(1)} %get-tuple-element.24), channel_id=1, source_target_pairs={{0,32},{32,64},{64,96},{96,0},{1,33},{33,65},{65,97},{97,1},{2,34}... | collective-permute-start | bytes 24584 | tf_op jit(solution)/shard_map/ppermute | solution.py:472
  12.5 3.6 %collective-permute-start.2 = (f32[16,128]{1,0:T(8,128)S(1)}, f32[16,128]{1,0:T(8,128)S(1)}, u32[]{:S(2)}, u32[]{:S(2)}) collective-permute-start(f32[16,128]{1,0:T(8,128)S(1)} %get-tuple-element.25), channel_id=1, source_target_pairs={{0,96},{32,0},{64,32},{96,64},{1,97},{33,1},{65,33},{97,65},{2,98}... | collective-permute-start | bytes 24584 | tf_op jit(solution)/shard_map/ppermute | solution.py:472
  48.6 8.0 %copy-start.8 = (f32[9,16]{1,0:T(8,128)S(1)}, f32[9,16]{1,0:T(8,128)}, u32[]{:S(2)}) copy-start(f32[9,16]{1,0:T(8,128)} %refs_2_.3) | copy-start | bytes 1732
  48.6 3.7 %collective-permute-start.5 = (f32[1,128]{1,0:T(1,128)S(1)}, f32[1,128]{1,0:T(1,128)S(1)}, u32[]{:S(2)}, u32[]{:S(2)}) collective-permute-start(f32[1,128]{1,0:T(1,128)S(1)} %shard_map.113.mine), channel_id=1, source_target_pairs={{0,128},{128,0},{1,129},{129,1},{2,130},{130,2},{3,131},{131,3},{4... | collective-permute-start | bytes 1544 | tf_op jit(solution)/shard_map/ppermute | solution.py:472
  52.2 6.0 %collective-permute-start.8 = (f32[2,128]{1,0:T(2,128)S(1)}, f32[2,128]{1,0:T(2,128)S(1)}, u32[]{:S(2)}, u32[]{:S(2)}) collective-permute-start(f32[2,128]{1,0:T(2,128)S(1)} %shard_map.114.near), channel_id=1, source_target_pairs={{0,64},{32,96},{64,0},{96,32},{1,65},{33,97},{65,1},{97,33},{2,66}... | collective-permute-start | bytes 3080 | tf_op jit(solution)/shard_map/ppermute | solution.py:472
  53.8 4.5 %collective-permute-start.7 = (f32[2,128]{1,0:T(2,128)S(1)}, f32[2,128]{1,0:T(2,128)S(1)}, u32[]{:S(2)}, u32[]{:S(2)}) collective-permute-start(f32[2,128]{1,0:T(2,128)S(1)} %shard_map.114.near), channel_id=1, source_target_pairs={{0,32},{32,64},{64,96},{96,0},{1,33},{33,65},{65,97},{97,1},{2,34}... | collective-permute-start | bytes 3080 | tf_op jit(solution)/shard_map/ppermute | solution.py:472
  54.3 4.0 %collective-permute-start.6 = (f32[2,128]{1,0:T(2,128)S(1)}, f32[2,128]{1,0:T(2,128)S(1)}, u32[]{:S(2)}, u32[]{:S(2)}) collective-permute-start(f32[2,128]{1,0:T(2,128)S(1)} %shard_map.114.near), channel_id=1, source_target_pairs={{0,96},{32,0},{64,32},{96,64},{1,97},{33,1},{65,33},{97,65},{2,98}... | collective-permute-start | bytes 3080 | tf_op jit(solution)/shard_map/ppermute | solution.py:472
  56.5 0.7 %copy-start.10 = (s32[16]{0:T(128)S(1)}, s32[16]{0:T(128)}, u32[]{:S(2)}) copy-start(s32[16]{0:T(128)} %refs_1_.3) | copy-start | bytes 196
